TPU v7x, 32 devices: a whole 2x2x4 slice. The times are simulated.
32 devices in a mesh: dp: 4 (over y, core), seq: 8 (over z, x).
Axes of the slice: x: 2, y: 2, z: 4, core: 2. Of those that a mesh axis runs over, the one named last changes fastest.
Arguments:
- inputs: float32 [12, 2048, 768], P('dp', 'seq'), may hold values from -6 to 6
- lengths: int32 [12], P('dp'), may hold values from 512 to 2048, as said below
- norm_attn: float32 [768], replicated, may hold values from 0.25 to 1.75
- w_query: bfloat16 [768, 768], replicated, may hold values from -0.0546875 to 0.0546875
- w_key: bfloat16 [768, 768], replicated, may hold values from -0.21875 to 0.21875
- w_value: bfloat16 [768, 768], replicated, may hold values from -0.21875 to 0.21875
- w_out: bfloat16 [768, 768], replicated, may hold values from -1.75 to 1.75
- norm_ffn: float32 [768], replicated, may hold values from 0.25 to 1.75
- w_gate: bfloat16 [768, 2048], replicated, may hold values from -0.21875 to 0.21875
- w_up: bfloat16 [768, 2048], replicated, may hold values from -0.21875 to 0.21875
- w_down: bfloat16 [2048, 768], replicated, may hold values from -0.125 to 0.125
- bucket_bias: float32 [32, 12], replicated, may hold values from -4 to 4
- cotangent: float32 [12, 2048, 768], P('dp', 'seq'), may hold values from -6 to 6
Outputs:
- output: float32 [12, 2048, 768], P('dp', 'seq')
- grad_input: float32 [12, 2048, 768], P('dp', 'seq')
- grad_norm_attn: float32 [768], P('dp')
- grad_norm_ffn: float32 [768], P('dp')
- grad_query: float32 [768, 768], P('dp')
- grad_key: float32 [768, 768], P('dp')
- grad_value: float32 [768, 768], P('dp')
- grad_out: float32 [768, 768], P('dp')
- grad_gate: float32 [768, 2048], P('dp')
- grad_up: float32 [768, 2048], P('dp')
- grad_down: float32 [2048, 768], P('dp')
- grad_table: float32 [32, 12], P('dp')
Inputs may be any that keep to these rules, and one draw needn't show every extreme that they name: `lengths`: of the 3 sequences of each index of dp, one has all 2048 positions valid.
All inputs are finite; a program needn't handle non-finite values.
Results may differ from a plain program's by a relative error of at most 0.024.
Values may be sent and summed in bfloat16 or wider, within the bound.
A program may use at most 384 MiB of HBM per device.

v0:
```python
import math

import jax
import jax.numpy as jnp
from jax import lax
from jax.sharding import PartitionSpec as P

H = 12
DH = 64
NB = 32


epsilon = 1e-06
limits = (1, 2, 3, 4, 5, 6, 7, 8, 12, 16, 23, 32, 46, 64, 91)
highest = lax.Precision.HIGHEST


def bucket_of(relative):
    distance = jnp.abs(relative)
    count = sum(((distance >= limit).astype(jnp.int32) for limit in limits))
    return count + (relative > 0).astype(jnp.int32) * (NB // 2)


def block_onehot(offset, height, width):
    relative = (
        offset
        + jnp.arange(width, dtype=jnp.int32)[None, :]
        - jnp.arange(height, dtype=jnp.int32)[:, None]
    )
    buckets = bucket_of(relative)
    return (buckets[:, :, None] == jnp.arange(NB, dtype=jnp.int32)[None, None, :]).astype(
        jnp.float32
    )


def bias_block(table, offset, height, width):
    return jnp.einsum("rkn,nh->hrk", block_onehot(offset, height, width), table, precision=highest)


def bias_grad(grad_bias, offset, height, width):
    return jnp.einsum(
        "hrk,rkn->nh", grad_bias, block_onehot(offset, height, width), precision=highest
    )


def scale_norm(values, gain):
    return values * lax.rsqrt(jnp.mean(values * values, axis=-1, keepdims=True) + epsilon) * gain


def gating(gate, upward):
    return jax.nn.gelu(gate, approximate=True) * upward


def project(left, weight):
    return jnp.einsum("bsd,de->bse", left, weight, preferred_element_type=jnp.float32)


def project_back(grad, weight):
    return jnp.einsum("bse,de->bsd", grad, weight, preferred_element_type=jnp.float32)


def weight_grad(left, grad):
    return jnp.einsum("bsd,bse->de", left, grad, preferred_element_type=jnp.float32)


def split_heads(values):
    return values.reshape(values.shape[0], values.shape[1], H, DH)


def scores_of(queries, keys, table, lengths, query_start, key_start):
    height = queries.shape[1]
    width = keys.shape[1]
    logits = jnp.einsum("brhd,bkhd->bhrk", queries, keys, preferred_element_type=jnp.float32)
    logits = logits + bias_block(table, key_start - query_start, height, width)[None]
    valid = (key_start + jnp.arange(width, dtype=jnp.int32))[None, :] < lengths[:, None]
    return (logits, valid[:, None, None, :])


def grad_block(
    queries, grad_part, log_total, delta, keys, values, table, lengths, query_start, key_start
):
    logits, valid = scores_of(queries, keys, table, lengths, query_start, key_start)
    chances = jnp.where(valid, jnp.exp(logits - log_total[..., None]), 0.0)
    grad_weights = jnp.einsum(
        "brhd,bkhd->bhrk", grad_part, values, preferred_element_type=jnp.float32
    )
    grad_logits = (chances * (grad_weights - delta[..., None])).astype(jnp.bfloat16)
    return (chances.astype(jnp.bfloat16), grad_logits)


def forward_fold(queries, table, lengths, query_start):

    def fold(carry, piece, start):
        keys, values = piece
        width = keys.shape[1]
        block = math.gcd(width, 512)

        def turn(index, state):
            best, total, weighted = state
            offset = index * block
            key_part = split_heads(lax.dynamic_slice_in_dim(keys, offset, block, 1))
            value_part = split_heads(lax.dynamic_slice_in_dim(values, offset, block, 1))
            logits, valid = scores_of(queries, key_part, table, lengths, query_start, offset)
            masked = jnp.where(valid, logits, -1e30)
            newest = jnp.maximum(best, jnp.max(masked, axis=-1))
            factor = jnp.exp(best - newest)
            expo = jnp.where(valid, jnp.exp(masked - newest[..., None]), 0.0)
            total = total * factor + jnp.sum(expo, axis=-1)
            weighted = weighted * factor[..., None] + jnp.einsum(
                "bhrk,bkhd->bhrd",
                expo.astype(jnp.bfloat16),
                value_part,
                preferred_element_type=jnp.float32,
            )
            return (newest, total, weighted)

        return lax.fori_loop(0, width // block, turn, carry)

    return fold


def shards(
    inputs,
    lengths,
    norm_attn,
    w_query,
    w_key,
    w_value,
    w_out,
    norm_ffn,
    w_gate,
    w_up,
    w_down,
    bucket_bias,
    cotangent,
):
    batch, height, _ = inputs.shape
    query_start = lax.axis_index("seq") * height
    normed = scale_norm(inputs, norm_attn).astype(jnp.bfloat16)
    queries = project(normed, w_query).astype(jnp.bfloat16)
    keys = project(normed, w_key).astype(jnp.bfloat16)
    values = project(normed, w_value).astype(jnp.bfloat16)
    query_heads = split_heads(queries)
    initial = (
        jnp.full((batch, H, height), -1e30, jnp.float32),
        jnp.zeros((batch, H, height), jnp.float32),
        jnp.zeros((batch, H, height, DH), jnp.float32),
    )
    fold = forward_fold(query_heads, bucket_bias, lengths, query_start)
    best, total, weighted = fold(
        initial,
        (
            lax.all_gather(keys, "seq", axis=1, tiled=True),
            lax.all_gather(values, "seq", axis=1, tiled=True),
        ),
        jnp.int32(0),
    )
    attended = (weighted / total[..., None]).transpose(0, 2, 1, 3)
    log_total = best + jnp.log(total)
    attended_low = attended.reshape(batch, height, -1).astype(jnp.bfloat16)
    mixed = inputs + project(attended_low, w_out)
    normed_ffn = scale_norm(mixed, norm_ffn).astype(jnp.bfloat16)
    gate = project(normed_ffn, w_gate)
    upward = project(normed_ffn, w_up)
    hidden = gating(gate, upward).astype(jnp.bfloat16)
    result = mixed + project(hidden, w_down)
    grad_out_low = cotangent.astype(jnp.bfloat16)
    grad_down = weight_grad(hidden, grad_out_low)
    grad_hidden = project_back(grad_out_low, w_down)
    _, gating_back = jax.vjp(gating, gate, upward)
    grad_gate_raw, grad_up_raw = gating_back(grad_hidden)
    grad_gate_low = grad_gate_raw.astype(jnp.bfloat16)
    grad_up_low = grad_up_raw.astype(jnp.bfloat16)
    grad_w_gate = weight_grad(normed_ffn, grad_gate_low)
    grad_w_up = weight_grad(normed_ffn, grad_up_low)
    grad_normed_ffn = project_back(grad_gate_low, w_gate) + project_back(grad_up_low, w_up)
    _, second_back = jax.vjp(scale_norm, mixed, norm_ffn)
    grad_mixed_norm, grad_norm_ffn = second_back(grad_normed_ffn)
    grad_mixed = cotangent + grad_mixed_norm
    grad_mixed_low = grad_mixed.astype(jnp.bfloat16)
    grad_w_out = weight_grad(attended_low, grad_mixed_low)
    grad_attended_rows = project_back(grad_mixed_low, w_out).astype(jnp.bfloat16)
    grad_attended = split_heads(grad_attended_rows)
    delta = jnp.sum(grad_attended.astype(jnp.float32) * attended, axis=-1).transpose(0, 2, 1)
    key_all, value_all = (
        lax.all_gather(keys, "seq", axis=1, tiled=True),
        lax.all_gather(values, "seq", axis=1, tiled=True),
    )
    length_all = key_all.shape[1]
    block = math.gcd(length_all, 512)

    def key_block(index):
        offset = index * block
        key_part = split_heads(lax.dynamic_slice_in_dim(key_all, offset, block, 1))
        value_part = split_heads(lax.dynamic_slice_in_dim(value_all, offset, block, 1))
        chances_low, grad_logits = grad_block(
            query_heads,
            grad_attended,
            log_total,
            delta,
            key_part,
            value_part,
            bucket_bias,
            lengths,
            query_start,
            offset,
        )
        grad_query_add = jnp.einsum(
            "bhrk,bkhd->brhd", grad_logits, key_part, preferred_element_type=jnp.float32
        )
        grad_table_add = bias_grad(
            jnp.sum(grad_logits.astype(jnp.float32), axis=0), offset - query_start, height, block
        )
        return (offset, chances_low, grad_logits, grad_query_add, grad_table_add)

    zero_heads = jnp.zeros((batch, height, H, DH), jnp.float32)
    zero_table = jnp.zeros((NB, H), jnp.float32)

    def back_turn(index, state):
        grad_queries, grad_table, key_terms, value_terms = state
        offset, chances_low, grad_logits, grad_query_add, grad_table_add = key_block(index)
        key_add = jnp.einsum(
            "bhrk,brhd->kbhd", grad_logits, query_heads, preferred_element_type=jnp.float32
        )
        value_add = jnp.einsum(
            "bhrk,brhd->kbhd", chances_low, grad_attended, preferred_element_type=jnp.float32
        )
        key_terms = lax.dynamic_update_slice_in_dim(
            key_terms, key_add.reshape(block, batch, -1), offset, 0
        )
        value_terms = lax.dynamic_update_slice_in_dim(
            value_terms, value_add.reshape(block, batch, -1), offset, 0
        )
        return (grad_queries + grad_query_add, grad_table + grad_table_add, key_terms, value_terms)

    empty_terms = jnp.zeros((length_all, batch, H * DH), jnp.float32)
    grad_queries, grad_table, key_terms, value_terms = lax.fori_loop(
        0, length_all // block, back_turn, (zero_heads, zero_table, empty_terms, empty_terms)
    )
    key_sum, value_sum = (
        lax.psum_scatter(
            key_terms.astype(jnp.bfloat16), "seq", scatter_dimension=0, tiled=True
        ).astype(jnp.float32),
        lax.psum_scatter(
            value_terms.astype(jnp.bfloat16), "seq", scatter_dimension=0, tiled=True
        ).astype(jnp.float32),
    )
    grad_keys = key_sum.transpose(1, 0, 2)
    grad_values = value_sum.transpose(1, 0, 2)
    grad_queries_low = grad_queries.reshape(batch, height, -1).astype(jnp.bfloat16)
    grad_keys_low = grad_keys.astype(jnp.bfloat16)
    grad_values_low = grad_values.astype(jnp.bfloat16)
    grad_w_query = weight_grad(normed, grad_queries_low)
    grad_w_key = weight_grad(normed, grad_keys_low)
    grad_w_value = weight_grad(normed, grad_values_low)
    grad_normed = (
        project_back(grad_queries_low, w_query)
        + project_back(grad_keys_low, w_key)
        + project_back(grad_values_low, w_value)
    )
    _, first_back = jax.vjp(scale_norm, inputs, norm_attn)
    grad_inputs_norm, grad_norm_attn = first_back(grad_normed)
    grad_inputs = grad_mixed + grad_inputs_norm
    (
        part_norm_attn,
        part_query,
        part_key,
        part_value,
        part_out,
        part_norm_ffn,
        part_gate,
        part_up,
        part_down,
        part_table,
    ) = (
        lax.psum_scatter(
            grad_norm_attn.astype(jnp.bfloat16), "dp", scatter_dimension=0, tiled=True
        ).astype(jnp.float32),
        lax.psum_scatter(
            grad_w_query.astype(jnp.bfloat16), "dp", scatter_dimension=0, tiled=True
        ).astype(jnp.float32),
        lax.psum_scatter(
            grad_w_key.astype(jnp.bfloat16), "dp", scatter_dimension=0, tiled=True
        ).astype(jnp.float32),
        lax.psum_scatter(
            grad_w_value.astype(jnp.bfloat16), "dp", scatter_dimension=0, tiled=True
        ).astype(jnp.float32),
        lax.psum_scatter(
            grad_w_out.astype(jnp.bfloat16), "dp", scatter_dimension=0, tiled=True
        ).astype(jnp.float32),
        lax.psum_scatter(
            grad_norm_ffn.astype(jnp.bfloat16), "dp", scatter_dimension=0, tiled=True
        ).astype(jnp.float32),
        lax.psum_scatter(
            grad_w_gate.astype(jnp.bfloat16), "dp", scatter_dimension=0, tiled=True
        ).astype(jnp.float32),
        lax.psum_scatter(
            grad_w_up.astype(jnp.bfloat16), "dp", scatter_dimension=0, tiled=True
        ).astype(jnp.float32),
        lax.psum_scatter(
            grad_down.astype(jnp.bfloat16), "dp", scatter_dimension=0, tiled=True
        ).astype(jnp.float32),
        lax.psum_scatter(
            grad_table.astype(jnp.bfloat16), "dp", scatter_dimension=0, tiled=True
        ).astype(jnp.float32),
    )
    totals = (
        lax.psum(part_norm_attn.astype(jnp.bfloat16), "seq").astype(jnp.float32),
        lax.psum(part_norm_ffn.astype(jnp.bfloat16), "seq").astype(jnp.float32),
        lax.psum(part_query.astype(jnp.bfloat16), "seq").astype(jnp.float32),
        lax.psum(part_key.astype(jnp.bfloat16), "seq").astype(jnp.float32),
        lax.psum(part_value.astype(jnp.bfloat16), "seq").astype(jnp.float32),
        lax.psum(part_out.astype(jnp.bfloat16), "seq").astype(jnp.float32),
        lax.psum(part_gate.astype(jnp.bfloat16), "seq").astype(jnp.float32),
        lax.psum(part_up.astype(jnp.bfloat16), "seq").astype(jnp.float32),
        lax.psum(part_down.astype(jnp.bfloat16), "seq").astype(jnp.float32),
        lax.psum(part_table.astype(jnp.bfloat16), "seq").astype(jnp.float32),
    )
    return (
        result,
        grad_inputs,
        totals[0],
        totals[1],
        totals[2],
        totals[3],
        totals[4],
        totals[5],
        totals[6],
        totals[7],
        totals[8],
        totals[9],
    )


def solution(mesh):
    return jax.shard_map(
        shards,
        mesh=mesh,
        in_specs=(
            P("dp", "seq", None),
            P("dp"),
            P(),
            P(),
            P(),
            P(),
            P(),
            P(),
            P(),
            P(),
            P(),
            P(),
            P("dp", "seq", None),
        ),
        out_specs=(
            P("dp", "seq", None),
            P("dp", "seq", None),
            P("dp"),
            P("dp"),
            P("dp", None),
            P("dp", None),
            P("dp", None),
            P("dp", None),
            P("dp", None),
            P("dp", None),
            P("dp", None),
            P("dp", None),
        ),
        check_vma=False,
    )
```

profile of v0, /device:TPU:0, one launch (start us, length us, event | category | flops | bytes accessed | tf_op | source)
XLA Modules:
  0.0 2397.2 jit_solution(5413679073761367697)
XLA Ops:
  32.1 122.5 %all-gather.5.cloned.1.call-done = bf16[3,2048,768]{2,1,0:T(8,128)(2,1)} async-done(((bf16[3,256,768]{2,1,0:T(8,128)(2,1)}), bf16[3,2048,768]{2,1,0:T(8,128)(2,1)}) %all-gather.5.cloned.1.call-update) | async-done | bytes 9437200 | tf_op jit(solution)/shard_map/all_gather | solution.py:154
  167.5 126.1 %all-gather.3.cloned.1.call-done = bf16[3,2048,768]{2,1,0:T(8,128)(2,1)} async-done(((bf16[3,256,768]{2,1,0:T(8,128)(2,1)}), bf16[3,2048,768]{2,1,0:T(8,128)(2,1)}) %all-gather.3.cloned.1.call-update) | async-done | bytes 9437200 | tf_op jit(solution)/shard_map/all_gather | solution.py:153
  306.1 218.7 %while.38 = (s32[]{:T(128)}, f32[3,12,256]{2,1,0:T(8,128)S(1)}, f32[3,12,256]{2,1,0:T(8,128)S(1)}, f32[3,12,256,64]{2,3,1,0:T(8,128)}, s32[3]{0:T(128)S(1)}, /*i...) while((s32[]{:T(128)}, f32[3,12,256]{2,1,0:T(8,128)S(1)}, ...), condition=%wide.region_4.5_spmd.clone, body=%wide.region_1.4_spmd.clone.sunk | while | flops 1885715968 | bytes 169557856 | solution.py:117
  569.9 1098.3 %while.39 = (s32[]{:T(128)}, f32[3,256,12,64]{1,3,2,0:T(8,128)}, f32[32,12]{0,1:T(8,128)S(1)}, bf16[2048,3,768]{0,2,1:T(8,128)(2,1)}, bf16[2048,3,768]{0,2,1:T(8...) while((s32[]{:T(128)}, f32[3,256,12,64]{1,3,2,0:T(8,128)}, ...), condition=%wide.region_10.11_spmd.clone, body=%wide.region_8.0_spmd.clone.sunk | while | flops 4298902528 | bytes 283506112 | solution.py:237
  594.4 185.3 %copy.166 = pred[256,512,32]{1,2,0:T(32,128)(4,1)S(1)} copy(pred[256,512,32]{0,2,1:T(32,128)(4,1)S(1)} %iota_compare_fusion.11) | data formatting | bytes 8388608 | tf_op jit(solution)/shard_map/while/body/eval_jaxpr/eq | solution.py:31
  829.0 15.4 fusion.206
  864.8 185.3 %copy.166 = pred[256,512,32]{1,2,0:T(32,128)(4,1)S(1)} copy(pred[256,512,32]{0,2,1:T(32,128)(4,1)S(1)} %iota_compare_fusion.11) | data formatting | bytes 8388608 | tf_op jit(solution)/shard_map/while/body/eval_jaxpr/eq | solution.py:31
  1084.9 14.5 convert_reduce_fusion.2
  1099.4 15.4 fusion.206
  1135.3 185.3 %copy.166 = pred[256,512,32]{1,2,0:T(32,128)(4,1)S(1)} copy(pred[256,512,32]{0,2,1:T(32,128)(4,1)S(1)} %iota_compare_fusion.11) | data formatting | bytes 8388608 | tf_op jit(solution)/shard_map/while/body/eval_jaxpr/eq | solution.py:31
  1369.9 15.4 fusion.206
  1405.7 185.3 %copy.166 = pred[256,512,32]{1,2,0:T(32,128)(4,1)S(1)} copy(pred[256,512,32]{0,2,1:T(32,128)(4,1)S(1)} %iota_compare_fusion.11) | data formatting | bytes 8388608 | tf_op jit(solution)/shard_map/while/body/eval_jaxpr/eq | solution.py:31
  1640.3 15.4 fusion.206
  1699.3 131.2 %reduce-scatter.10.cloned.1.call-done = bf16[256,3,768]{0,2,1:T(8,128)(2,1)} async-done(((bf16[2048,3,768]{0,2,1:T(8,128)(2,1)}), bf16[256,3,768]{0,2,1:T(8,128)(2,1)}) %reduce-scatter.10.cloned.1.call-update) | async-done | bytes 1179664 | tf_op jit(solution)/shard_map/reduce_scatter | solution.py:241
  1834.0 162.8 %reduce-scatter.12.cloned.1.call-done = bf16[256,3,768]{0,2,1:T(8,128)(2,1)} async-done(((bf16[2048,3,768]{0,2,1:T(8,128)(2,1)}), bf16[256,3,768]{0,2,1:T(8,128)(2,1)}) %reduce-scatter.12.cloned.1.call-update) | async-done | bytes 1179664 | tf_op jit(solution)/shard_map/reduce_scatter | solution.py:244
  2000.4 23.6 reduce-scatter.20.cloned.1.call-done
  2024.0 28.9 %reduce-scatter.14.cloned.1.call-done = bf16[192,768]{1,0:T(8,128)(2,1)} async-done(((bf16[768,768]{1,0:T(8,128)(2,1)}), bf16[192,768]{1,0:T(8,128)(2,1)}) %reduce-scatter.14.cloned.1.call-update) | async-done | bytes 294928 | tf_op jit(solution)/shard_map/reduce_scatter | solution.py:279
  2053.0 40.5 %reduce-scatter.24.cloned.1.call-done = bf16[192,2048]{1,0:T(8,128)(2,1)} async-done(((bf16[768,2048]{1,0:T(8,128)(2,1)}), bf16[192,2048]{1,0:T(8,128)(2,1)}) %reduce-scatter.24.cloned.1.call-update) | async-done | bytes 786448 | tf_op jit(solution)/shard_map/reduce_scatter | solution.py:297
  2093.5 40.7 %reduce-scatter.26.cloned.1.call-done = bf16[512,768]{1,0:T(8,128)(2,1)} async-done(((bf16[2048,768]{1,0:T(8,128)(2,1)}), bf16[512,768]{1,0:T(8,128)(2,1)}) %reduce-scatter.26.cloned.1.call-update) | async-done | bytes 786448 | tf_op jit(solution)/shard_map/reduce_scatter | solution.py:300
  2134.2 40.5 %reduce-scatter.22.cloned.1.call-done = bf16[192,2048]{1,0:T(8,128)(2,1)} async-done(((bf16[768,2048]{1,0:T(8,128)(2,1)}), bf16[192,2048]{1,0:T(8,128)(2,1)}) %reduce-scatter.22.cloned.1.call-update) | async-done | bytes 786448 | tf_op jit(solution)/shard_map/reduce_scatter | solution.py:294
  2174.7 28.9 %reduce-scatter.16.cloned.1.call-done = bf16[192,768]{1,0:T(8,128)(2,1)} async-done(((bf16[768,768]{1,0:T(8,128)(2,1)}), bf16[192,768]{1,0:T(8,128)(2,1)}) %reduce-scatter.16.cloned.1.call-update) | async-done | bytes 294928 | tf_op jit(solution)/shard_map/reduce_scatter | solution.py:282
  2203.6 28.9 %reduce-scatter.18.cloned.1.call-done = bf16[192,768]{1,0:T(8,128)(2,1)} async-done(((bf16[768,768]{1,0:T(8,128)(2,1)}), bf16[192,768]{1,0:T(8,128)(2,1)}) %reduce-scatter.18.cloned.1.call-update) | async-done | bytes 294928 | tf_op jit(solution)/shard_map/reduce_scatter | solution.py:285
  2261.0 22.7 all-reduce.3
  2289.8 89.9 %all-reduce.8.cloned.1.call-done = (bf16[192,768]{1,0:T(8,128)(2,1)}, bf16[192,768]{1,0:T(8,128)(2,1)}, bf16[192,768]{1,0:T(8,128)(2,1)}, bf16[192,768]{1,0:T(8,...) async-done(((bf16[192,768]{1,0:T(8,128)(2,1)}, bf16[192,768]{1,0:T(8,128)(2,1)}, bf16[192,768]{1,0:T(8,128)(2,1)}, ...) | async-done | bytes 3538960 | tf_op jit(solution)/shard_map/psum | solution.py:310
  (370 shorter events, 658.4 us)
Async XLA Ops:
  7.2 527.0 %copy-start = (bf16[768,2048]{1,0:T(8,128)(2,1)S(1)}, bf16[768,2048]{1,0:T(8,128)(2,1)}, u32[]{:S(2)}) copy-start(bf16[768,2048]{1,0:T(8,128)(2,1)} %param.25) | copy-start | bytes 9437188
  7.2 147.4 %all-gather.5.cloned.1.call-start = ((), (), s32[]{:S(2)}) async-start(), calls=%async_computation.10 | async-start | bytes 10616832 | tf_op jit(solution)/shard_map/all_gather | solution.py:154
  13.7 280.0 %all-gather.3.cloned.1.call-start = ((), (), s32[]{:S(2)}) async-start(), calls=%async_computation.9 | async-start | bytes 10616832 | tf_op jit(solution)/shard_map/all_gather | solution.py:153
  17.5 1813.0 %reduce-scatter.10.cloned.1.call-start = ((), (), s32[]{:S(2)}) async-start(), calls=%async_computation.11 | async-start | bytes 10616832 | tf_op jit(solution)/shard_map/reduce_scatter | solution.py:241
  167.5 138.7 %copy-start.33 = (f32[32,12]{0,1:T(8,128)S(1)}, f32[32,12]{0,1:T(8,128)}, u32[]{:S(2)}) copy-start(f32[32,12]{0,1:T(8,128)} %param.28) | copy-start | bytes 4612
  167.5 138.7 %copy-start.41 = (s32[3]{0:T(128)S(1)}, s32[3]{0:T(128)}, u32[]{:S(2)}) copy-start(s32[3]{0:T(128)} %param.18) | copy-start | bytes 40
  528.8 23.0 copy-start.17
  829.0 15.4 copy-start.11
  1099.4 15.4 copy-start.4
  1099.4 15.4 copy-start.11
  1369.9 15.4 copy-start.11
  1640.3 15.4 copy-start.11
  1668.2 328.5 %reduce-scatter.12.cloned.1.call-start = ((), (), s32[]{:S(2)}) async-start(), calls=%async_computation.12 | async-start | bytes 10616832 | tf_op jit(solution)/shard_map/reduce_scatter | solution.py:244
  1668.8 355.2 %reduce-scatter.20.cloned.1.call-start = ((), (), s32[]{:S(2)}) async-start(), calls=%async_computation.16 | async-start | bytes 1474560 | tf_op jit(solution)/shard_map/reduce_scatter | solution.py:288
  1673.2 379.8 %reduce-scatter.14.cloned.1.call-start = ((), (), s32[]{:S(2)}) async-start(), calls=%async_computation.13 | async-start | bytes 1474560 | tf_op jit(solution)/shard_map/reduce_scatter | solution.py:279
  1678.0 415.5 %reduce-scatter.24.cloned.1.call-start = ((), (), s32[]{:S(2)}) async-start(), calls=%async_computation.18 | async-start | bytes 3932160 | tf_op jit(solution)/shard_map/reduce_scatter | solution.py:297
  1684.0 450.2 %reduce-scatter.26.cloned.1.call-start = ((), (), s32[]{:S(2)}) async-start(), calls=%async_computation.19 | async-start | bytes 3932160 | tf_op jit(solution)/shard_map/reduce_scatter | solution.py:300
  1692.0 482.8 %reduce-scatter.22.cloned.1.call-start = ((), (), s32[]{:S(2)}) async-start(), calls=%async_computation.17 | async-start | bytes 3932160 | tf_op jit(solution)/shard_map/reduce_scatter | solution.py:294
  1699.2 131.3 %copy-start.24 = (bf16[3,256,768]{2,1,0:T(8,128)(2,1)S(1)}, bf16[3,256,768]{2,1,0:T(8,128)(2,1)}, u32[]{:S(2)}) copy-start(bf16[3,256,768]{2,1,0:T(8,128)(2,1)} %copy-done.23) | copy-start | bytes 3538948
  1699.2 504.4 %reduce-scatter.16.cloned.1.call-start = ((), (), s32[]{:S(2)}) async-start(), calls=%async_computation.14 | async-start | bytes 1474560 | tf_op jit(solution)/shard_map/reduce_scatter | solution.py:282
  1833.9 398.6 %reduce-scatter.18.cloned.1.call-start = ((), (), s32[]{:S(2)}) async-start(), calls=%async_computation.15 | async-start | bytes 1474560 | tf_op jit(solution)/shard_map/reduce_scatter | solution.py:285
  2000.2 232.4 %copy-start.52 = (u32[32]{0:T(128)S(1)}, u32[32]{0:T(128)}, u32[]{:S(2)}) copy-start(u32[32]{0:T(128)} %constant.302) | copy-start | bytes 388
  2000.2 379.5 %all-reduce.8.cloned.1.call-start = ((), (), s32[]{:S(2)}) async-start(), calls=%async_computation.20 | async-start | bytes 7077888 | tf_op jit(solution)/shard_map/psum | solution.py:310
  2246.3 39.1 %copy-start.45 = (f32[3,256]{1,0:T(4,128)S(1)}, f32[3,256]{1,0:T(4,128)}, u32[]{:S(2)}) copy-start(f32[3,256]{1,0:T(4,128)} %copy-done.44) | copy-start | bytes 9220
  (74 other events, 397.4 us)
Sparse Core Ops, SparseCore 0:
  13.8 140.7 all-gather.4
  157.3 136.2 all-gather.2
  1668.4 162.0 reduce-scatter.9
  1833.9 162.7 reduce-scatter.11
  1999.2 24.8 reduce-scatter.19
  2027.2 25.7 reduce-scatter.13
  2055.5 37.9 reduce-scatter.23
  2096.2 37.9 reduce-scatter.25
  2136.7 37.9 reduce-scatter.21
  2177.9 25.7 reduce-scatter.15
  2206.8 25.7 reduce-scatter.17
  2237.5 142.1 all-reduce.7
where the time goes:
time: 2410 us; the launch traced here: 2400 us
  local copies, waits for them, and re-layouts  924 us (38%)
  waiting for transfers between devices  865 us (36%)
  matrix products  458 us (19%)
  other arithmetic  81.5 us (3%)
  blocking collectives  34.1 us (1%)
    eq x4, local copies, waits for them, and re-layouts, block_onehot(): buckets[:, :, None] == jnp.arange(NB, dtype=jnp.int32)[None, None, :]  741 us
    reduce_scatter x1, waiting for transfers between devices, shards(): lax.psum_scatter(value_terms.astype(jnp.bfloat16), 'seq', scatter_dimensi...  163 us
    reduce_scatter x1, waiting for transfers between devices, shards(): lax.psum_scatter(key_terms.astype(jnp.bfloat16), 'seq', scatter_dimension...  131 us
    all_gather x1, waiting for transfers between devices, shards(): lax.all_gather(keys, 'seq', axis=1, tiled=True)  126 us
    all_gather x1, waiting for transfers between devices, shards(): lax.all_gather(values, 'seq', axis=1, tiled=True)  122 us
    psum x1, waiting for transfers between devices, shards(): lax.psum(part_query.astype(jnp.bfloat16), 'seq').astype(jnp.float32)  89.9 us
    dot_general x8, matrix products, scores_of(): jnp.einsum('brhd,bkhd->bhrk', queries, keys, preferred_element_type=jnp.f...  81.5 us
    dot_general x8, local copies, waits for them, and re-layouts, bias_block(): jnp.einsum('rkn,nh->hrk', block_onehot(offset, height, width), table, pre...  73.3 us
  transfers between devices with their start and end apart: 12, of which 12 were waited for; matrix products, arithmetic and copies ran while one was open for 4% of the time, Pallas kernels for 0%

commit v1 on v0

v1 whole, which is shorter than its diff:
```python
import functools

import jax
import jax.numpy as jnp
from jax import lax
from jax.experimental import pallas as pl
from jax.experimental.pallas import tpu as pltpu
from jax.sharding import PartitionSpec as P

H = 12
DH = 64
NB = 32
OUTER = 4
HEADS = H // OUTER
HW = HEADS * DH
BLK = 256
AUG = DH + 16
SPAN = 4 * BLK
LOG2E = 1.4426950408889634
LN2 = 0.6931471805599453
F32 = jnp.float32
BF16 = jnp.bfloat16
NT = (((1,), (1,)), ((), ()))
VMEM_BYTES = 48 << 20

epsilon = 1e-06
limits = (1, 2, 3, 4, 5, 6, 7, 8, 12, 16, 23, 32, 46, 64, 91)
highest = lax.Precision.HIGHEST


def bucket_of(relative):
    distance = jnp.abs(relative)
    count = sum(((distance >= limit).astype(jnp.int32) for limit in limits))
    return count + (relative > 0).astype(jnp.int32) * (NB // 2)


def scale_norm(values, gain):
    return values * lax.rsqrt(jnp.mean(values * values, axis=-1, keepdims=True) + epsilon) * gain


def gating(gate, upward):
    return jax.nn.gelu(gate, approximate=True) * upward


def params():
    return pltpu.CompilerParams(vmem_limit_bytes=VMEM_BYTES)


def smem():
    return pl.BlockSpec(memory_space=pltpu.SMEM)


def whole():
    return pl.BlockSpec(memory_space=pltpu.VMEM)


def split3(v):
    a = v.astype(BF16)
    r = v - a.astype(F32)
    b = r.astype(BF16)
    c = (r - b.astype(F32)).astype(BF16)
    return a.astype(F32), b.astype(F32), c.astype(F32)


def tail(width, values):
    row = lax.broadcasted_iota(jnp.int32, (16, width), 0)
    out = jnp.zeros((16, width), F32)
    for i, v in enumerate(values):
        out = jnp.where(row == i, v, out)
    return out


def tiles_kernel(line_ref, out_ref):
    out_ref[0, 0] = jnp.zeros((BLK, BLK), F32)
    out_ref[0, 4] = jnp.zeros((BLK, BLK), F32)
    line = jnp.broadcast_to(line_ref[0], (BLK, SPAN))
    for off in (-1, 0, 1):
        shift = (off * BLK - (2 * BLK - 1)) % SPAN
        rolled = pltpu.roll(line, shift, 1, stride=1, stride_axis=0)
        out_ref[0, off + 2] = rolled[:, :BLK]


def bias_tiles(lines):
    heads = lines.shape[0]
    return pl.pallas_call(
        tiles_kernel,
        grid=(heads,),
        in_specs=[pl.BlockSpec((1, 1, SPAN), lambda h: (h, 0, 0))],
        out_specs=pl.BlockSpec((1, 5, BLK, BLK), lambda h: (h, 0, 0, 0)),
        out_shape=jax.ShapeDtypeStruct((heads, 5, BLK, BLK), F32),
        compiler_params=params(),
        name="bias_tiles",
    )(lines)


def diagonals_kernel(*refs):
    near, out_ref = refs[:-1], refs[-1]
    row = lax.broadcasted_iota(jnp.int32, (BLK, BLK), 0)
    col = lax.broadcasted_iota(jnp.int32, (BLK, BLK), 1)
    flip = (row + col == BLK - 1).astype(F32)
    total = jnp.zeros((1, SPAN), F32)
    for off in (-1, 0, 1):
        tile = sum(r[0, off + 1] for r in near)
        flipped = jnp.dot(flip, tile, preferred_element_type=F32, precision=highest)
        padded = jnp.concatenate([flipped, jnp.zeros((BLK, SPAN - BLK), F32)], axis=1)
        rolled = pltpu.roll(padded, (BLK - off * BLK) % SPAN, 1, stride=1, stride_axis=0)
        total = total + jnp.sum(rolled, axis=0, keepdims=True)
    out_ref[0] = total


def diagonal_sums(nears):
    heads = nears[0].shape[0]
    return pl.pallas_call(
        diagonals_kernel,
        grid=(heads,),
        in_specs=[pl.BlockSpec((1, 3, BLK, BLK), lambda h: (h, 0, 0, 0)) for _ in nears],
        out_specs=pl.BlockSpec((1, 1, SPAN), lambda h: (h, 0, 0)),
        out_shape=jax.ShapeDtypeStruct((heads, 1, SPAN), F32),
        compiler_params=params(),
        name="diagonal_sums",
    )(*nears)


def project_kernel(z_ref, x_ref, gain_ref, wq_ref, wk_ref, wv_ref, normed_ref, *rest):
    outs, held = rest[: 2 * OUTER], rest[2 * OUTER]
    values = x_ref[...]
    scale = lax.rsqrt(jnp.mean(values * values, axis=-1, keepdims=True) + epsilon)
    normed = (values * scale * gain_ref[...]).astype(BF16)
    normed_ref[...] = normed
    for i, (w_ref, factor) in enumerate(((wq_ref, LOG2E), (wk_ref, 1.0), (wv_ref, 1.0))):
        rows = jnp.dot(normed, w_ref[...], preferred_element_type=F32) * factor
        held[i] = rows.T.astype(BF16)
    for d in range(OUTER):
        group = lax.rem(z_ref[0] + d, OUTER)
        rows = pl.ds(pl.multiple_of(group * HW, HW), HW)
        outs[d][...] = held[0, rows]
        outs[OUTER + d][:HW] = held[1, rows]
        outs[OUTER + d][HW:] = held[2, rows]


def project(z, values, gain, wq, wk, wv):
    height, width = values.shape
    shapes = [jax.ShapeDtypeStruct((height, width), BF16)]
    shapes += [jax.ShapeDtypeStruct((HW, height), BF16)] * OUTER
    shapes += [jax.ShapeDtypeStruct((2 * HW, height), BF16)] * OUTER
    out = pl.pallas_call(
        project_kernel,
        in_specs=[smem()] + [whole()] * 5,
        out_specs=[whole()] * len(shapes),
        out_shape=shapes,
        scratch_shapes=[pltpu.VMEM((3, width, height), BF16)],
        compiler_params=params(),
        cost_estimate=pl.CostEstimate(flops=6 * height * width * width, bytes_accessed=6 << 20, transcendentals=0),
        name="project",
    )(z, values, gain.reshape(1, -1), wq, wk, wv)
    return out[0], out[1 : 1 + OUTER], out[1 + OUTER :]


def far_case(n, j, kb):
    if kb < n * j - 1:
        return 0
    if kb > n * j + n:
        return 2
    return None


def near_case(n, j, kb, x):
    off = kb - (n * j + x)
    return jnp.clip(off + 2, 0, 4), jnp.where(off <= -2, 0, jnp.where(off >= 2, 2, 1))


GROUP_F = 4
GROUP_B = 2


def forward_kernel(n, place_ref, len_ref, far_ref, *refs):
    q_refs, refs = refs[:OUTER], refs[OUTER:]
    k_refs, refs = refs[: n * OUTER], refs[n * OUTER :]
    v_refs, refs = refs[: n * OUTER], refs[n * OUTER :]
    tile_ref, refs = refs[0], refs[1:]
    o_refs, refs = refs[:OUTER], refs[OUTER:]
    lse_ref, ka, qa, va, acc, best = refs
    nk = OUTER * n
    head = pl.program_id(0)
    z, x = place_ref[0], place_ref[1]
    length = len_ref[place_ref[2]]
    left, right = far_ref[head, 0], far_ref[head, 1]
    one = jnp.ones((1, BLK), F32)
    lane = lax.broadcasted_iota(jnp.int32, (1, BLK), 1)
    vtail = tail(BLK, (one,)).astype(BF16)
    kmax = jnp.zeros((1, BLK), F32)
    for s in range(n):
        col = lax.rem(x + s, n)
        for d in range(OUTER):
            kb = n * lax.rem(z + d, OUTER) + col
            keys = k_refs[s * OUTER + d][...]
            keys32 = keys.astype(F32)
            kmax = jnp.maximum(kmax, jnp.sum(keys32 * keys32, axis=0, keepdims=True))
            mask = jnp.where(kb * BLK + lane < length, 0.0, -1e30)
            ka[kb] = jnp.concatenate([keys, tail(BLK, (one, one, one, mask)).astype(BF16)], axis=0).T
            va[kb, :DH] = v_refs[s * OUTER + d][...]
            va[kb, DH:] = vtail
    tails = [tail(BLK, split3(jnp.zeros((1, BLK), F32) + c) + (one,)).astype(BF16) for c in (left, 0.0, right)]
    qmax = jnp.zeros((1, BLK), F32)
    for d in range(OUTER):
        j = lax.rem(z + d, OUTER)
        queries = q_refs[d][...]
        queries32 = queries.astype(F32)
        qmax = jnp.maximum(qmax, jnp.sum(queries32 * queries32, axis=0, keepdims=True))
        for v in range(3):
            qa[v, j, :DH] = queries
            qa[v, j, DH:] = tails[v]
    bound = jnp.sqrt(jnp.max(qmax) * jnp.max(kmax)) * 1.01 + far_ref[head, 2]
    safe = bound <= 90.0
    acc[...] = jnp.zeros_like(acc)

    def scores(kb, j):
        case = far_case(n, j, kb)
        if case is not None:
            return jnp.dot(ka[kb], qa[case, j], preferred_element_type=F32)
        tile, case = near_case(n, j, kb, x)
        return jnp.dot(ka[kb], qa[case, j], preferred_element_type=F32) + tile_ref[0, tile]

    @pl.when(safe)
    def _():
        for g in range(0, nk, GROUP_F):

            @pl.when(g * BLK < length)
            def _():
                for j in range(OUTER):
                    add = acc[j]
                    for kb in range(g, g + GROUP_F):
                        p = jnp.exp2(scores(kb, j)).astype(BF16)
                        add = add + jnp.dot(va[kb], p, preferred_element_type=F32)
                    acc[j] = add

        best[...] = jnp.zeros_like(best)

    @pl.when(jnp.logical_not(safe))
    def _():
        best[...] = jnp.full(best.shape, -1e30, F32)
        for kb in range(nk):

            @pl.when(kb * BLK < length)
            def _():
                for j in range(OUTER):
                    s = scores(kb, j)
                    old = best[j]
                    new = jnp.maximum(old, jnp.max(s, axis=0, keepdims=True))
                    p = jnp.exp2(s - new).astype(BF16)
                    acc[j] = acc[j] * jnp.exp2(old - new) + jnp.dot(va[kb], p, preferred_element_type=F32)
                    best[j] = new

    for d in range(OUTER):
        j = lax.rem(z + d, OUTER)
        total = acc[j, DH : DH + 1, :]
        o_refs[d][...] = (acc[j, :DH, :] / total).astype(BF16)
        lse_ref[0, d] = best[j] + jnp.log2(total)


def backward_kernel(n, place_ref, len_ref, far_ref, *refs):
    q_refs, refs = refs[:OUTER], refs[OUTER:]
    k_refs, refs = refs[: n * OUTER], refs[n * OUTER :]
    v_refs, refs = refs[: n * OUTER], refs[n * OUTER :]
    tile_ref, refs = refs[0], refs[1:]
    o_refs, refs = refs[:OUTER], refs[OUTER:]
    do_refs, refs = refs[:OUTER], refs[OUTER:]
    lse_ref, refs = refs[0], refs[1:]
    dq_refs, refs = refs[:OUTER], refs[OUTER:]
    dk_refs, refs = refs[: n * OUTER], refs[n * OUTER :]
    dv_refs, refs = refs[: n * OUTER], refs[n * OUTER :]
    near_ref, far_sum_ref, ka, kt, va, qa, qt, da, acc, near, dk_all, dv_all = refs
    nk = OUTER * n
    head = pl.program_id(0)
    z, x = place_ref[0], place_ref[1]
    length = len_ref[place_ref[2]]
    left, right = far_ref[head, 0], far_ref[head, 1]
    one = jnp.ones((1, BLK), F32)
    lane = lax.broadcasted_iota(jnp.int32, (1, BLK), 1)
    ones3 = tail(BLK, (one, one, one)).astype(BF16)
    for s in range(n):
        col = lax.rem(x + s, n)
        for d in range(OUTER):
            kb = n * lax.rem(z + d, OUTER) + col
            keys = k_refs[s * OUTER + d][...]
            mask = jnp.where(kb * BLK + lane < length, 0.0, -1e30)
            ka[kb] = jnp.concatenate([keys, tail(BLK, (one, one, one, mask)).astype(BF16)], axis=0).T
            kt[kb] = keys
            va[kb] = jnp.concatenate([v_refs[s * OUTER + d][...], ones3], axis=0).T
    for d in range(OUTER):
        j = lax.rem(z + d, OUTER)
        lse = lse_ref[0, d]
        for v, c in enumerate((left, 0.0, right)):
            qa[v, j, :DH] = q_refs[d][...]
            qa[v, j, DH:] = tail(BLK, split3(c - lse) + (one,)).astype(BF16)
        qt[j] = q_refs[d][...]
        grads = do_refs[d][...]
        delta = jnp.sum(grads.astype(F32) * o_refs[d][...].astype(F32), axis=0, keepdims=True)
        da[j, :DH] = grads
        da[j, DH:] = tail(BLK, split3(-delta)).astype(BF16)
    acc[...] = jnp.zeros_like(acc)
    near[...] = jnp.zeros_like(near)
    row16 = lax.broadcasted_iota(jnp.int32, (16, BLK), 0)
    marks = [jnp.where(row16 == r, 1.0, 0.0).astype(BF16) for r in range(2)]

    for g in range(0, nk, GROUP_B):

        @pl.when(g * BLK < length)
        def _():
            dvs = {kb: jnp.zeros((DH, BLK), F32) for kb in range(g, g + GROUP_B)}
            dks = {kb: jnp.zeros((DH, BLK), F32) for kb in range(g, g + GROUP_B)}
            for j in range(OUTER):
                add = acc[j]
                for kb in range(g, g + GROUP_B):
                    case = far_case(n, j, kb)
                    if case is not None:
                        p = jnp.exp2(jnp.dot(ka[kb], qa[case, j], preferred_element_type=F32))
                        mark = marks[case // 2]
                    else:
                        tile, case = near_case(n, j, kb, x)
                        s = jnp.dot(ka[kb], qa[case, j], preferred_element_type=F32)
                        p = jnp.exp2(s + tile_ref[0, tile])
                        want = jnp.where(case == 1, 2, case // 2)
                        mark = jnp.where(row16 == want, 1.0, 0.0).astype(BF16)
                    ds = p * jnp.dot(va[kb], da[j], preferred_element_type=F32)
                    if far_case(n, j, kb) is None:
                        near[tile] += ds
                    p16, ds16 = p.astype(BF16), ds.astype(BF16)
                    lhs = jnp.concatenate([kt[kb], mark], axis=0)
                    add = add + jnp.dot(lhs, ds16, preferred_element_type=F32)
                    dvs[kb] += lax.dot_general(da[j, :DH], p16, NT, preferred_element_type=F32)
                    dks[kb] += lax.dot_general(qt[j], ds16, NT, preferred_element_type=F32)
                acc[j] = add
            for kb in range(g, g + GROUP_B):
                dk_all[kb] = dks[kb] * LN2
                dv_all[kb] = dvs[kb]

        @pl.when(g * BLK >= length)
        def _():
            for kb in range(g, g + GROUP_B):
                dk_all[kb] = jnp.zeros((DH, BLK), F32)
                dv_all[kb] = jnp.zeros((DH, BLK), F32)

    far = jnp.zeros((8, BLK), F32)
    for d in range(OUTER):
        j = lax.rem(z + d, OUTER)
        dq_refs[d][...] = acc[j, :DH, :].astype(BF16)
        far = far + acc[j, DH : DH + 8, :]
    far_sum_ref[0] = far
    for s in range(n):
        col = lax.rem(x + s, n)
        for d in range(OUTER):
            kb = n * lax.rem(z + d, OUTER) + col
            i = s * OUTER + d
            dk_refs[i][...] = dk_all[kb].astype(dk_refs[i].dtype)
            dv_refs[i][...] = dv_all[kb].astype(dv_refs[i].dtype)
    for i in range(3):
        near_ref[0, i] = near[i + 1]


def rows_block(base):
    return pl.BlockSpec((DH, BLK), lambda h: (base + h, 0))


def per_head(shape):
    return pl.BlockSpec((1,) + shape, lambda h: (h,) + (0,) * len(shape))


def attention_inputs(n, place, lengths, far, queries, pairs, tiles):
    specs = [smem()] * 3 + [rows_block(0)] * OUTER + [rows_block(0)] * (n * OUTER)
    specs += [rows_block(HEADS)] * (n * OUTER) + [per_head((5, BLK, BLK))]
    return specs, [place, lengths, far, *queries, *pairs, *pairs, tiles]


def attention_forward(n, place, lengths, far, queries, pairs, tiles):
    nk = n * OUTER
    specs, args = attention_inputs(n, place, lengths, far, queries, pairs, tiles)
    out = pl.pallas_call(
        functools.partial(forward_kernel, n),
        grid=(HEADS,),
        in_specs=specs,
        out_specs=[rows_block(0)] * OUTER + [per_head((OUTER, 1, BLK))],
        out_shape=[jax.ShapeDtypeStruct((HW, BLK), BF16)] * OUTER
        + [jax.ShapeDtypeStruct((HEADS, OUTER, 1, BLK), F32)],
        scratch_shapes=[
            pltpu.VMEM((nk, BLK, AUG), BF16),
            pltpu.VMEM((3, OUTER, AUG, BLK), BF16),
            pltpu.VMEM((nk, AUG, BLK), BF16),
            pltpu.VMEM((OUTER, AUG, BLK), F32),
            pltpu.VMEM((OUTER, 1, BLK), F32),
        ],
        compiler_params=params(),
        cost_estimate=pl.CostEstimate(flops=15 * 10**9, bytes_accessed=6 << 20, transcendentals=0),
        name="attention_forward",
    )(*args)
    return out[:OUTER], out[OUTER]


def attention_backward(n, place, lengths, far, queries, pairs, tiles, outs, douts, lse):
    nk = n * OUTER
    specs, args = attention_inputs(n, place, lengths, far, queries, pairs, tiles)
    specs += [rows_block(0)] * (2 * OUTER) + [per_head((OUTER, 1, BLK))]
    args += [*outs, *douts, lse]
    kinds = [F32] * OUTER + [BF16] * (nk - OUTER)
    out = pl.pallas_call(
        functools.partial(backward_kernel, n),
        grid=(HEADS,),
        in_specs=specs,
        out_specs=[rows_block(0)] * (OUTER + 2 * nk) + [per_head((3, BLK, BLK)), per_head((8, BLK))],
        out_shape=[jax.ShapeDtypeStruct((HW, BLK), BF16)] * OUTER
        + [jax.ShapeDtypeStruct((HW, BLK), kind) for kind in kinds + kinds]
        + [jax.ShapeDtypeStruct((HEADS, 3, BLK, BLK), F32), jax.ShapeDtypeStruct((HEADS, 8, BLK), F32)],
        scratch_shapes=[
            pltpu.VMEM((nk, BLK, AUG), BF16),
            pltpu.VMEM((nk, DH, BLK), BF16),
            pltpu.VMEM((nk, BLK, AUG), BF16),
            pltpu.VMEM((3, OUTER, AUG, BLK), BF16),
            pltpu.VMEM((OUTER, DH, BLK), BF16),
            pltpu.VMEM((OUTER, AUG, BLK), BF16),
            pltpu.VMEM((OUTER, AUG, BLK), F32),
            pltpu.VMEM((5, BLK, BLK), F32),
            pltpu.VMEM((nk, DH, BLK), F32),
            pltpu.VMEM((nk, DH, BLK), F32),
        ],
        compiler_params=params(),
        cost_estimate=pl.CostEstimate(flops=35 * 10**9, bytes_accessed=12 << 20, transcendentals=0),
        name="attention_backward",
    )(*args)
    dq = out[:OUTER]
    dk = out[OUTER : OUTER + nk]
    dv = out[OUTER + nk : OUTER + 2 * nk]
    return dq, dk, dv, out[-2], out[-1]


class Places:
    def __init__(self, mesh):
        self.dp = mesh.shape["dp"]
        self.seq = mesh.shape["seq"]
        self.inner = self.seq // OUTER
        self.cores = 2
        self.groups = self.dp // self.cores

    def shift_outer(self, value, d):
        n = self.inner
        pairs = [(o * n + i, (o + d) % OUTER * n + i) for o in range(OUTER) for i in range(n)]
        return lax.ppermute(value, "seq", pairs)

    def shift_inner(self, value, d):
        n = self.inner
        pairs = [(o * n + i, o * n + (i + d) % n) for o in range(OUTER) for i in range(n)]
        return lax.ppermute(value, "seq", pairs)

    def shift_core(self, value, d):
        c = self.cores
        pairs = [(g * c + i, g * c + (i + d) % c) for g in range(self.groups) for i in range(c)]
        return lax.ppermute(value, "dp", pairs)

    def shift_group(self, value, d):
        c, g = self.cores, self.groups
        pairs = [(o * c + i, (o + d) % g * c + i) for o in range(g) for i in range(c)]
        return lax.ppermute(value, "dp", pairs)


def scatter_sum(pieces, at, size, axis, shift):
    total = pieces(at).astype(F32)
    for d in range(1, size):
        part = pieces(lax.rem(at + d, size))
        total = total + shift(part, d).astype(F32)
    return total


def pick(value, index, axis):
    return lax.dynamic_index_in_dim(value, index, axis, keepdims=False)


def reduce_grad(places, grad, kind):
    rows, columns = grad.shape
    c, g, n = places.cores, places.groups, places.inner
    share = rows // places.dp
    dp, seq = lax.axis_index("dp"), lax.axis_index("seq")
    parts = grad.astype(kind).reshape(g, c, share, columns)
    held = scatter_sum(lambda i: pick(parts, i, 1), lax.rem(dp, c), c, 1, places.shift_core).astype(kind)
    held = scatter_sum(lambda i: pick(held, i, 0), dp // c, g, 0, places.shift_group).astype(kind)
    wide = columns // n
    slabs = held.reshape(share, n, wide)
    held = scatter_sum(lambda i: pick(slabs, i, 1), lax.rem(seq, n), n, 1, places.shift_inner).astype(kind)
    lines = held.reshape(OUTER, share // OUTER, wide)
    z, x = seq // n, lax.rem(seq, n)
    held = scatter_sum(lambda i: pick(lines, i, 0), z, OUTER, 0, places.shift_outer).astype(kind)
    full = jnp.zeros((OUTER, share // OUTER, wide), kind)
    full = lax.dynamic_update_index_in_dim(full, held, z, 0)
    for d in range(1, OUTER):
        full = lax.dynamic_update_index_in_dim(full, places.shift_outer(held, d), lax.rem(z + OUTER - d, OUTER), 0)
    full = full.reshape(share, wide)
    result = jnp.zeros((share, n, wide), kind)
    result = lax.dynamic_update_index_in_dim(result, full, x, 1)
    for d in range(1, n):
        result = lax.dynamic_update_index_in_dim(result, places.shift_inner(full, d), lax.rem(x + n - d, n), 1)
    return result.reshape(share, columns).astype(F32)


def ordered(parts, start):
    both = jnp.concatenate(list(parts) + list(parts), axis=0)
    size = parts[0].shape[0]
    return lax.dynamic_slice_in_dim(both, lax.rem(OUTER - start, OUTER) * size, OUTER * size, 0)


def shards(
    places,
    inputs,
    lengths,
    norm_attn,
    w_query,
    w_key,
    w_value,
    w_out,
    norm_ffn,
    w_gate,
    w_up,
    w_down,
    bucket_bias,
    cotangent,
):
    batch, height, width = inputs.shape
    n = places.inner
    seq = lax.axis_index("seq")
    z, x = seq // n, lax.rem(seq, n)
    z_arg = z.reshape(1).astype(jnp.int32)

    table = lax.dynamic_slice_in_dim(bucket_bias, z * HEADS, HEADS, 1) * LOG2E
    relative = 2 * BLK - 1 - jnp.arange(SPAN, dtype=jnp.int32)
    onehot = (bucket_of(relative)[:, None] == jnp.arange(NB, dtype=jnp.int32)[None, :]).astype(F32)
    lines = jnp.einsum("cn,nh->hc", onehot, table, precision=highest)[:, None, :]
    tiles = bias_tiles(lines)
    far = jnp.stack([table[NB // 2 - 1], table[NB - 1], jnp.max(jnp.abs(table), axis=0)], axis=1)

    normed, query_parts, pair_parts = [], [], []
    for b in range(batch):
        rows, qs, kvs = project(z_arg, inputs[b], norm_attn, w_query, w_key, w_value)
        normed.append(rows)
        own_q, own_kv, other = [qs[0]], [kvs[0]], {}
        for d in range(1, OUTER):
            back = OUTER - d
            own_kv.append(places.shift_outer(kvs[back], back))
            own_q.append(places.shift_outer(qs[back], back))
        pairs = list(own_kv)
        for s in range(1, n):
            pairs += [places.shift_inner(part, n - s) for part in own_kv]
        query_parts.append(own_q)
        pair_parts.append(pairs)
    outs, lses, attended = [], [], []
    places_arg = [jnp.stack([z, x, jnp.int32(b)]).astype(jnp.int32) for b in range(batch)]
    for b in range(batch):
        parts, lse = attention_forward(n, places_arg[b], lengths, far, query_parts[b], pair_parts[b], tiles)
        outs.append(parts)
        lses.append(lse)
        arrived = [parts[0]] + [places.shift_outer(parts[OUTER - d], OUTER - d) for d in range(1, OUTER)]
        attended.append(ordered(arrived, z))
    attended_t = jnp.stack(attended)
    normed = jnp.stack(normed)
    mixed = inputs + jnp.einsum("bes,ed->bsd", attended_t, w_out, preferred_element_type=F32)
    normed_ffn = scale_norm(mixed, norm_ffn).astype(BF16)
    gate = jnp.einsum("bsd,de->bse", normed_ffn, w_gate, preferred_element_type=F32)
    upward = jnp.einsum("bsd,de->bse", normed_ffn, w_up, preferred_element_type=F32)
    hidden = gating(gate, upward).astype(BF16)
    result = mixed + jnp.einsum("bsd,de->bse", hidden, w_down, preferred_element_type=F32)
    grad_out_low = cotangent.astype(BF16)
    grad_down = jnp.einsum("bsd,bse->de", hidden, grad_out_low, preferred_element_type=F32)
    grad_hidden = jnp.einsum("bse,de->bsd", grad_out_low, w_down, preferred_element_type=F32)
    _, gating_back = jax.vjp(gating, gate, upward)
    grad_gate_raw, grad_up_raw = gating_back(grad_hidden)
    grad_gate_low = grad_gate_raw.astype(BF16)
    grad_up_low = grad_up_raw.astype(BF16)
    grad_w_gate = jnp.einsum("bsd,bse->de", normed_ffn, grad_gate_low, preferred_element_type=F32)
    grad_w_up = jnp.einsum("bsd,bse->de", normed_ffn, grad_up_low, preferred_element_type=F32)
    grad_normed_ffn = jnp.einsum("bse,de->bsd", grad_gate_low, w_gate, preferred_element_type=F32) + jnp.einsum(
        "bse,de->bsd", grad_up_low, w_up, preferred_element_type=F32
    )
    _, second_back = jax.vjp(scale_norm, mixed, norm_ffn)
    grad_mixed_norm, grad_norm_ffn = second_back(grad_normed_ffn)
    grad_mixed = cotangent + grad_mixed_norm
    grad_mixed_low = grad_mixed.astype(BF16)
    grad_w_out = jnp.einsum("bes,bsd->ed", attended_t, grad_mixed_low, preferred_element_type=F32)
    grad_attended_t = jnp.einsum("bsd,ed->bes", grad_mixed_low, w_out, preferred_element_type=F32).astype(BF16)

    part_gate = reduce_grad(places, grad_w_gate, BF16)
    part_up = reduce_grad(places, grad_w_up, BF16)
    part_down = reduce_grad(places, grad_down, BF16)
    part_out = reduce_grad(places, grad_w_out, BF16)

    grads_q, grads_k, grads_v, nears, fars = [], [], [], [], []
    for b in range(batch):
        sent = [lax.dynamic_slice_in_dim(grad_attended_t[b], lax.rem(z + d, OUTER) * HW, HW, 0) for d in range(OUTER)]
        douts = [sent[0]] + [places.shift_outer(sent[OUTER - d], OUTER - d) for d in range(1, OUTER)]
        dq, dk, dv, near, far_sum = attention_backward(
            n, places_arg[b], lengths, far, query_parts[b], pair_parts[b], tiles, outs[b], douts, lses[b]
        )
        nears.append(near)
        fars.append(far_sum)
        dk_sum, dv_sum = [], []
        for d in range(OUTER):
            k_total, v_total = dk[d], dv[d]
            for s in range(1, n):
                k_total = k_total + places.shift_inner(dk[s * OUTER + d], s).astype(F32)
                v_total = v_total + places.shift_inner(dv[s * OUTER + d], s).astype(F32)
            dk_sum.append(k_total.astype(BF16))
            dv_sum.append(v_total.astype(BF16))
        for kept, parts in ((grads_q, dq), (grads_k, dk_sum), (grads_v, dv_sum)):
            arrived = [parts[0]] + [places.shift_outer(parts[OUTER - d], OUTER - d) for d in range(1, OUTER)]
            kept.append(ordered(arrived, z))
    grad_q, grad_k, grad_v = jnp.stack(grads_q), jnp.stack(grads_k), jnp.stack(grads_v)
    grad_w_query = jnp.einsum("bsd,bes->de", normed, grad_q, preferred_element_type=F32)
    grad_w_key = jnp.einsum("bsd,bes->de", normed, grad_k, preferred_element_type=F32)
    grad_w_value = jnp.einsum("bsd,bes->de", normed, grad_v, preferred_element_type=F32)
    part_query = reduce_grad(places, grad_w_query, BF16)
    part_key = reduce_grad(places, grad_w_key, BF16)
    part_value = reduce_grad(places, grad_w_value, BF16)
    grad_normed = (
        jnp.einsum("bes,de->bsd", grad_q, w_query, preferred_element_type=F32)
        + jnp.einsum("bes,de->bsd", grad_k, w_key, preferred_element_type=F32)
        + jnp.einsum("bes,de->bsd", grad_v, w_value, preferred_element_type=F32)
    )
    _, first_back = jax.vjp(scale_norm, inputs, norm_attn)
    grad_inputs_norm, grad_norm_attn = first_back(grad_normed)
    grad_inputs = grad_mixed + grad_inputs_norm

    lines_sum = diagonal_sums(nears)[:, 0]
    table_part = jnp.einsum("cn,hc->nh", onehot, lines_sum, precision=highest)
    far_total = sum(jnp.sum(f, axis=-1) for f in fars)
    bucket = jnp.arange(NB, dtype=jnp.int32)[:, None]
    table_part = table_part + jnp.where(bucket == NB // 2 - 1, far_total[:, 0][None, :], 0.0)
    table_part = table_part + jnp.where(bucket == NB - 1, far_total[:, 1][None, :], 0.0)
    grad_table = lax.dynamic_update_slice_in_dim(jnp.zeros((NB, H), F32), table_part, z * HEADS, 1)
    small = jnp.concatenate(
        [
            grad_norm_attn.reshape(places.dp, -1),
            grad_norm_ffn.reshape(places.dp, -1),
            grad_table.reshape(places.dp, -1),
        ],
        axis=1,
    )
    used = small.shape[1]
    small = jnp.pad(small, ((0, 0), (0, 32 * 128 - used))).reshape(places.dp * 32, 128)
    small = reduce_grad(places, small, F32).reshape(-1)
    share = width // places.dp
    return (
        result,
        grad_inputs,
        small[:share],
        small[share : 2 * share],
        part_query,
        part_key,
        part_value,
        part_out,
        part_gate,
        part_up,
        part_down,
        small[2 * share : used].reshape(NB // places.dp, H),
    )


def solution(mesh):
    rows = P("dp", "seq", None)
    share = P("dp", None)
    return jax.shard_map(
        functools.partial(shards, Places(mesh)),
        mesh=mesh,
        in_specs=(rows, P("dp")) + (P(),) * 10 + (rows,),
        out_specs=(rows, rows, P("dp"), P("dp")) + (share,) * 8,
        check_vma=False,
    )
```

time: 2410 us -> 1020 us (0.42)
  waiting for transfers between devices: 865 us -> 212 us
  local copies, waits for them, and re-layouts: 924 us -> 332 us
  matrix products: 458 us -> 64.7 us
  starting transfers between devices: 0.67 us -> 222 us
  Pallas kernels: 0 us -> 123 us
  blocking collectives: 34.1 us -> 0 us
    eq x4 -> x0, local copies, waits for them, and re-layouts: 741 us -> none  [block_onehot(): buckets[:, :, None] == jnp.arange(NB, dtype=jnp.int32)[None, None, :]]
    reduce_scatter x9 -> x0, waiting for transfers between devices: 526 us -> none  [the longest x1 163 us: shards(): lax.psum_scatter(value_terms.astype(jnp.bfloat16), 'seq', scatter_dimensi...]
    dot_general x61 -> x20, matrix products: 458 us -> 64.7 us  [the longest x1 9.85 us: shards(): jnp.einsum('bsd,de->bse', normed_ffn, w_gate, preferred_element_type=F32)]
    all_gather x2 -> x0, waiting for transfers between devices: 249 us -> none  [the longest x1 126 us: shards(): lax.all_gather(keys, 'seq', axis=1, tiled=True)]
    ppermute x0 -> x179, starting transfers between devices: none -> 222 us  [the longest x111 135 us: shift_outer(): return lax.ppermute(value, 'seq', pairs)]
    ppermute x0 -> x179, waiting for transfers between devices: none -> 212 us  [the longest x111 150 us: shift_outer(): return lax.ppermute(value, 'seq', pairs)]
    pallas_call x0 -> x11, Pallas kernels: none -> 123 us  [the longest x3 71.7 us: attention_backward(): pl.pallas_call(functools.partial(backward_kernel, n), grid=(HEADS,), in_s...]
    unnamed x98 -> x648, local copies, waits for them, and re-layouts: 37.9 us -> 155 us
  transfers between devices with their start and end apart: 12 -> 179, of which waited for: 12 -> 68; matrix products, arithmetic and copies ran while one was open for 4% -> 28% of each run, Pallas kernels for 0% -> 12%
where the time goes in v1:
time: 1020 us; the launch traced here: 1010 us
  local copies, waits for them, and re-layouts  332 us (33%)
  starting transfers between devices  222 us (22%)
  waiting for transfers between devices  212 us (21%)
  Pallas kernels  123 us (12%)
  matrix products  64.7 us (6%)
  other arithmetic  57.6 us (6%)
    unnamed x648, local copies, waits for them, and re-layouts  155 us
    ppermute x111, waiting for transfers between devices, shift_outer(): return lax.ppermute(value, 'seq', pairs)  150 us
    ppermute x111, starting transfers between devices, shift_outer(): return lax.ppermute(value, 'seq', pairs)  135 us
    pallas_call x3, Pallas kernels, attention_backward(): pl.pallas_call(functools.partial(backward_kernel, n), grid=(HEADS,), in_s...  71.7 us
    ppermute x52, starting transfers between devices, shift_inner(): return lax.ppermute(value, 'seq', pairs)  56.7 us
    dynamic_update_slice x8, local copies, waits for them, and re-layouts, reduce_grad(): lax.dynamic_update_index_in_dim(result, places.shift_inner(full, d), lax....  45.2 us
    ppermute x8, waiting for transfers between devices, shift_group(): return lax.ppermute(value, 'dp', pairs)  42.4 us
    pallas_call x3, Pallas kernels, attention_forward(): pl.pallas_call(functools.partial(forward_kernel, n), grid=(HEADS,), in_sp...  40.8 us
  transfers between devices with their start and end apart: 179, of which 68 were waited for; matrix products, arithmetic and copies ran while one was open for 28% of the time, Pallas kernels for 12%

profile of v1, /device:TPU:0, one launch (start us, length us, event | category | flops | bytes accessed | tf_op | source)
XLA Modules:
  0.0 1014.0 jit_solution(17623553542948858598)
XLA Ops:
  31.0 8.0 fusion.10
  56.2 6.0 collective-permute-start.17
  62.2 12.8 %collective-permute-done.4.refs_6_.refs_14_ = bf16[384,256]{1,0:T(8,128)(2,1)S(1)} collective-permute-done((bf16[384,256]{1,0:T(8,128)(2,1)}, bf16[384,256]{1,0:T(8,128)(2,1)S(1)}, u32[]{:S(2)}, u32[]{:S(2)}) %collective-permute-start.4) | collective-permute-done | bytes 196640 | tf_op jit(solution)/shard_map/ppermute | solution.py:446
  89.2 15.3 %attention_forward.3 = (bf16[192,256]{1,0:T(8,128)(2,1)S(1)}, bf16[192,256]{1,0:T(8,128)(2,1)S(1)}, bf16[192,256]{1,0:T(8,128)(2,1)S(1)}, bf16[192,256]{1,0:T(8,128)(2,1)S(1)}, f32[3,4,1,256]{3,2,1,0:T(1,128)S(1)}) custom-call(s32[3]{0:T(128)S(1)} %pad_add_fusion.place_ref, s32[3]{0:T(128)S(1)} %copy-done.216, f32[3,3]{1,0:T(4,128)S(1)} %pad_maximum_fusion.13.far_ref, ...), custom_call_target="tpu_custom_call" | custom-call | flops 15000000512 | bytes 6291456 | tf_op jit(solution)/shard_map/attention_forward/pallas_call | solution.py:378
  114.9 16.0 %attention_forward.4 = (bf16[192,256]{1,0:T(8,128)(2,1)S(1)}, bf16[192,256]{1,0:T(8,128)(2,1)}, bf16[192,256]{1,0:T(8,128)(2,1)}, bf16[192,256]{1,0:T(8,128)(2,1)}, f32[3,4,1,256]{3,2,1,0:T(1,128)S(1)}) custom-call(s32[3]{0:T(128)S(1)} %pad_add_fusion.2.place_ref, s32[3]{0:T(128)S(1)} %copy-done.216, f32[3,3]{1,0:T(4,128)S(1)} %pad_maximum_fusion.13.far_ref, ...), custom_call_target="tpu_custom_call" | custom-call | flops 15000000512 | bytes 6291456 | tf_op jit(solution)/shard_map/attention_forward/pallas_call | solution.py:378
  139.2 5.7 collective-permute-done.28.refs_3_
  150.3 9.5 attention_forward.5
  203.8 9.8 fusion.6
  213.7 6.0 bitcast_convert_fusion.1
  282.0 30.2 %attention_backward.3 = (bf16[192,256]{1,0:T(8,128)(2,1)S(1)}, bf16[192,256]{1,0:T(8,128)(2,1)S(1)}, bf16[192,256]{1,0:T(8,128)(2,1)S(1)}, bf16[192,256]{1,0:T(8...) custom-call(s32[3]{0:T(128)S(1)} %pad_add_fusion.place_ref, ...), custom_call_target="tpu_custom_call" | custom-call | flops 35000000512 | bytes 12582912 | tf_op jit(solution)/shard_map/attention_backward/pallas_call | solution.py:405
  328.4 23.8 %attention_backward.4 = (bf16[192,256]{1,0:T(8,128)(2,1)S(1)}, bf16[192,256]{1,0:T(8,128)(2,1)S(1)}, bf16[192,256]{1,0:T(8,128)(2,1)S(1)}, bf16[192,256]{1,0:T(8...) custom-call(s32[3]{0:T(128)S(1)} %pad_add_fusion.2.place_ref, ...), custom_call_target="tpu_custom_call" | custom-call | flops 35000000512 | bytes 12582912 | tf_op jit(solution)/shard_map/attention_backward/pallas_call | solution.py:405
  388.8 17.7 %attention_backward.5 = (bf16[192,256]{1,0:T(8,128)(2,1)S(1)}, bf16[192,256]{1,0:T(8,128)(2,1)S(1)}, bf16[192,256]{1,0:T(8,128)(2,1)S(1)}, bf16[192,256]{1,0:T(8...) custom-call(s32[3]{0:T(128)S(1)} %pad_add_fusion.3.place_ref, ...), custom_call_target="tpu_custom_call" | custom-call | flops 35000000512 | bytes 12582912 | tf_op jit(solution)/shard_map/attention_backward/pallas_call | solution.py:405
  435.8 6.3 collective-permute-done.44
  474.9 5.4 collective-permute-done.56
  613.1 21.8 %collective-permute-start.100 = (f32[32,128]{1,0:T(8,128)S(1)}, f32[32,128]{1,0:T(8,128)S(1)}, u32[]{:S(2)}, u32[]{:S(2)}) collective-permute-start(f32[32,128]{1,0:T(8,128)S(1)} %fusion.91), channel_id=1, source_target_pairs={{0,16},{8,24},{16,0},{24,8},{1,17},{9,25},{17,1},{25,9},{2,18},{10... | collective-permute-start | bytes 49160 | tf_op jit(solution)/shard_map/ppermute | solution.py:461
  768.0 5.9 collective-permute-done.125
  783.1 14.5 %collective-permute-done.170 = bf16[512,768]{0,1:T(8,128)(2,1)S(1)} collective-permute-done((bf16[512,768]{0,1:T(8,128)(2,1)S(1)}, bf16[512,768]{0,1:T(8,128)(2,1)S(1)}, u32[]{:S(2)}, u32[]{:S(2)}) %collective-permute-start.170) | collective-permute-done | bytes 786464 | tf_op jit(solution)/shard_map/ppermute | solution.py:461
  800.2 14.2 %collective-permute-done.150 = bf16[192,2048]{1,0:T(8,128)(2,1)S(1)} collective-permute-done((bf16[192,2048]{1,0:T(8,128)(2,1)S(1)}, bf16[192,2048]{1,0:T(8,128)(2,1)S(1)}, u32[]{:S(2)}, u32[]{:S(2)}) %collective-permute-start.150) | collective-permute-done | bytes 786464 | tf_op jit(solution)/shard_map/ppermute | solution.py:461
  816.4 9.3 collective-permute-done.160
  952.0 10.1 dynamic_update_slice.202
  962.5 5.3 dynamic_update_slice.196
  975.4 10.1 dynamic_update_slice.203
  988.4 5.3 dynamic_update_slice.197
  997.7 13.6 %dynamic_update_slice.191 = bf16[192,2,1024]{2,1,0:T(2,128)(2,1)} dynamic-update-slice(bf16[192,2,1024]{2,1,0:T(2,128)(2,1)} %copy-done.229, bf16[192,1,1024]{2,1,0:T(2,128)(2,1)} %copy.284, s32[]{:T(128)} %constant.461.clone.1, s32[]{:T(128)S(6)} %select_n.255, s32[]{:T(128)} %constant.461.clone.1) | dynamic-update-slice | bytes 786436 | tf_op jit(solution)/shard_map/jit(dynamic_update_index_in_dim)/dynamic_update_slice | solution.py:498
  (1276 shorter events, 727.5 us)
Async XLA Ops:
  12.6 35.6 %collective-permute-start = (bf16[192,256]{1,0:T(8,128)(2,1)}, bf16[192,256]{1,0:T(8,128)(2,1)}, u32[]{:S(2)}, u32[]{:S(2)}) collective-permute-start(bf16[192,256]{1,0:T(8,128)(2,1)} %get-tuple-element.121), channel_id=1, source_target_pairs={{0,6},{1,7},{2,0},{3,1},{4,2},{5,3},{6,4},{7,5},{8,14},{9,15},{10,... | collective-permute-start | bytes 294920 | tf_op jit(solution)/shard_map/ppermute | solution.py:446
  112.3 32.7 %collective-permute-start.32 = (bf16[384,256]{1,0:T(8,128)(2,1)S(1)}, bf16[384,256]{1,0:T(8,128)(2,1)S(1)}, u32[]{:S(2)}, u32[]{:S(2)}) collective-permute-start(bf16[384,256]{1,0:T(8,128)(2,1)S(1)} %get-tuple-element.148.refs_4_.refs_12_), channel_id=1, source_target_pairs={{0,1},{1,0},{2,3},{3,2},{4,5},{5,4},{6,7},{7,6},{8,9},{9,8},{10,11... | collective-permute-start | bytes 589832 | tf_op jit(solution)/shard_map/ppermute | solution.py:451
  244.0 530.9 %collective-permute-start.169 = (bf16[2,512,768]{1,2,0:T(8,128)(2,1)}, bf16[2,512,768]{1,2,0:T(8,128)(2,1)}, u32[]{:S(2)}, u32[]{:S(2)}) collective-permute-start(bf16[2,512,768]{1,2,0:T(8,128)(2,1)} %bitcast.500), channel_id=1, source_target_pairs={{0,8},{8,0},{16,24},{24,16},{1,9},{9,1},{17,25},{25,17},{2,10},{10... | collective-permute-start | bytes 4718600 | tf_op jit(solution)/shard_map/ppermute | solution.py:456
  251.2 417.0 %collective-permute-start.139 = (bf16[2,192,768]{2,1,0:T(8,128)(2,1)}, bf16[2,192,768]{2,1,0:T(8,128)(2,1)}, u32[]{:S(2)}, u32[]{:S(2)}) collective-permute-start(bf16[2,192,768]{2,1,0:T(8,128)(2,1)} %dynamic-slice_bitcast_fusion.5), channel_id=1, source_target_pairs={{0,8},{8,0},{16,24},{24,16},{1,9},{9,1},{17,25},{25,17},{2,10},{10... | collective-permute-start | bytes 1769480 | tf_op jit(solution)/shard_map/ppermute | solution.py:456
  267.3 54.7 %collective-permute-start.45 = (bf16[192,256]{1,0:T(8,128)(2,1)}, bf16[192,256]{1,0:T(8,128)(2,1)}, u32[]{:S(2)}, u32[]{:S(2)}) collective-permute-start(bf16[192,256]{1,0:T(8,128)(2,1)} %bitcast.22), channel_id=1, source_target_pairs={{0,6},{1,7},{2,0},{3,1},{4,2},{5,3},{6,4},{7,5},{8,14},{9,15},{10,... | collective-permute-start | bytes 294920 | tf_op jit(solution)/shard_map/ppermute | solution.py:446
  271.7 54.2 %collective-permute-start.46 = (bf16[192,256]{1,0:T(8,128)(2,1)}, bf16[192,256]{1,0:T(8,128)(2,1)}, u32[]{:S(2)}, u32[]{:S(2)}) collective-permute-start(bf16[192,256]{1,0:T(8,128)(2,1)} %bitcast.23), channel_id=1, source_target_pairs={{0,4},{1,5},{2,6},{3,7},{4,0},{5,1},{6,2},{7,3},{8,12},{9,13},{10,... | collective-permute-start | bytes 294920 | tf_op jit(solution)/shard_map/ppermute | solution.py:446
  272.9 53.5 %collective-permute-start.47 = (bf16[192,256]{1,0:T(8,128)(2,1)}, bf16[192,256]{1,0:T(8,128)(2,1)}, u32[]{:S(2)}, u32[]{:S(2)}) collective-permute-start(bf16[192,256]{1,0:T(8,128)(2,1)} %bitcast.24), channel_id=1, source_target_pairs={{0,2},{1,3},{2,4},{3,5},{4,6},{5,7},{6,0},{7,1},{8,10},{9,11},{10,... | collective-permute-start | bytes 294920 | tf_op jit(solution)/shard_map/ppermute | solution.py:446
  322.1 42.0 %collective-permute-start.51 = (bf16[192,256]{1,0:T(8,128)(2,1)}, bf16[192,256]{1,0:T(8,128)(2,1)S(1)}, u32[]{:S(2)}, u32[]{:S(2)}) collective-permute-start(bf16[192,256]{1,0:T(8,128)(2,1)} %bitcast.548), channel_id=1, source_target_pairs={{0,6},{1,7},{2,0},{3,1},{4,2},{5,3},{6,4},{7,5},{8,14},{9,15},{10,... | collective-permute-start | bytes 294920 | tf_op jit(solution)/shard_map/ppermute | solution.py:446
  325.9 40.3 %collective-permute-start.52 = (bf16[192,256]{1,0:T(8,128)(2,1)}, bf16[192,256]{1,0:T(8,128)(2,1)S(1)}, u32[]{:S(2)}, u32[]{:S(2)}) collective-permute-start(bf16[192,256]{1,0:T(8,128)(2,1)} %bitcast.547), channel_id=1, source_target_pairs={{0,4},{1,5},{2,6},{3,7},{4,0},{5,1},{6,2},{7,3},{8,12},{9,13},{10,... | collective-permute-start | bytes 294920 | tf_op jit(solution)/shard_map/ppermute | solution.py:446
  326.4 40.9 %collective-permute-start.53 = (bf16[192,256]{1,0:T(8,128)(2,1)}, bf16[192,256]{1,0:T(8,128)(2,1)S(1)}, u32[]{:S(2)}, u32[]{:S(2)}) collective-permute-start(bf16[192,256]{1,0:T(8,128)(2,1)} %bitcast.546), channel_id=1, source_target_pairs={{0,2},{1,3},{2,4},{3,5},{4,6},{5,7},{6,0},{7,1},{8,10},{9,11},{10,... | collective-permute-start | bytes 294920 | tf_op jit(solution)/shard_map/ppermute | solution.py:446
  364.7 127.6 %collective-permute-start.83 = (bf16[192,256]{1,0:T(8,128)(2,1)}, bf16[192,256]{1,0:T(8,128)(2,1)}, u32[]{:S(2)}, u32[]{:S(2)}) collective-permute-start(bf16[192,256]{1,0:T(8,128)(2,1)} %get-tuple-element.202), channel_id=1, source_target_pairs={{0,1},{1,0},{2,3},{3,2},{4,5},{5,4},{6,7},{7,6},{8,9},{9,8},{10,11... | collective-permute-start | bytes 294920 | tf_op jit(solution)/shard_map/ppermute | solution.py:451
  366.8 127.2 %collective-permute-start.81 = (bf16[192,256]{1,0:T(8,128)(2,1)}, bf16[192,256]{1,0:T(8,128)(2,1)}, u32[]{:S(2)}, u32[]{:S(2)}) collective-permute-start(bf16[192,256]{1,0:T(8,128)(2,1)} %get-tuple-element.200), channel_id=1, source_target_pairs={{0,1},{1,0},{2,3},{3,2},{4,5},{5,4},{6,7},{7,6},{8,9},{9,8},{10,11... | collective-permute-start | bytes 294920 | tf_op jit(solution)/shard_map/ppermute | solution.py:451
  368.0 61.5 %collective-permute-start.42 = (bf16[192,256]{1,0:T(8,128)(2,1)}, bf16[192,256]{1,0:T(8,128)(2,1)}, u32[]{:S(2)}, u32[]{:S(2)}) collective-permute-start(bf16[192,256]{1,0:T(8,128)(2,1)} %get-tuple-element.158), channel_id=1, source_target_pairs={{0,6},{1,7},{2,0},{3,1},{4,2},{5,3},{6,4},{7,5},{8,14},{9,15},{10,... | collective-permute-start | bytes 294920 | tf_op jit(solution)/shard_map/ppermute | solution.py:446
  691.2 85.9 %collective-permute-start.149 = (bf16[2,192,2048]{2,1,0:T(8,128)(2,1)}, bf16[2,192,2048]{2,1,0:T(8,128)(2,1)}, u32[]{:S(2)}, u32[]{:S(2)}) collective-permute-start(bf16[2,192,2048]{2,1,0:T(8,128)(2,1)} %dynamic-slice_bitcast_fusion.1), channel_id=1, source_target_pairs={{0,8},{8,0},{16,24},{24,16},{1,9},{9,1},{17,25},{25,17},{2,10},{10... | collective-permute-start | bytes 4718600 | tf_op jit(solution)/shard_map/ppermute | solution.py:456
  751.8 151.3 %collective-permute-start.148 = (bf16[192,384]{1,0:T(8,128)(2,1)}, bf16[192,384]{1,0:T(8,128)(2,1)}, u32[]{:S(2)}, u32[]{:S(2)}) collective-permute-start(bf16[192,384]{1,0:T(8,128)(2,1)} %bitcast.131), channel_id=1, source_target_pairs={{0,1},{1,0},{2,3},{3,2},{4,5},{5,4},{6,7},{7,6},{8,9},{9,8},{10,11... | collective-permute-start | bytes 442376 | tf_op jit(solution)/shard_map/ppermute | solution.py:451
  773.9 130.4 %collective-permute-start.118 = (bf16[192,384]{1,0:T(8,128)(2,1)}, bf16[192,384]{1,0:T(8,128)(2,1)}, u32[]{:S(2)}, u32[]{:S(2)}) collective-permute-start(bf16[192,384]{1,0:T(8,128)(2,1)} %bitcast.77), channel_id=1, source_target_pairs={{0,1},{1,0},{2,3},{3,2},{4,5},{5,4},{6,7},{7,6},{8,9},{9,8},{10,11... | collective-permute-start | bytes 442376 | tf_op jit(solution)/shard_map/ppermute | solution.py:451
  774.9 57.6 %collective-permute-start.126 = (bf16[48,384]{1,0:T(8,128)(2,1)}, bf16[48,384]{1,0:T(8,128)(2,1)S(1)}, u32[]{:S(2)}, u32[]{:S(2)}) collective-permute-start(bf16[48,384]{1,0:T(8,128)(2,1)} %get-tuple-element.245), channel_id=1, source_target_pairs={{0,4},{1,5},{2,6},{3,7},{4,0},{5,1},{6,2},{7,3},{8,12},{9,13},{10,... | collective-permute-start | bytes 110600 | tf_op jit(solution)/shard_map/ppermute | solution.py:446
  780.8 33.6 %collective-permute-start.150 = (bf16[192,2048]{1,0:T(8,128)(2,1)S(1)}, bf16[192,2048]{1,0:T(8,128)(2,1)S(1)}, u32[]{:S(2)}, u32[]{:S(2)}) collective-permute-start(bf16[192,2048]{1,0:T(8,128)(2,1)S(1)} %dynamic-slice_bitcast_fusion.4), channel_id=1, source_target_pairs={{0,16},{8,24},{16,0},{24,8},{1,17},{9,25},{17,1},{25,9},{2,18},{10... | collective-permute-start | bytes 2359304 | tf_op jit(solution)/shard_map/ppermute | solution.py:461
  863.4 38.6 %collective-permute-start.127 = (bf16[48,384]{1,0:T(8,128)(2,1)}, bf16[48,384]{1,0:T(8,128)(2,1)S(1)}, u32[]{:S(2)}, u32[]{:S(2)}) collective-permute-start(bf16[48,384]{1,0:T(8,128)(2,1)} %get-tuple-element.245), channel_id=1, source_target_pairs={{0,6},{1,7},{2,0},{3,1},{4,2},{5,3},{6,4},{7,5},{8,14},{9,15},{10,... | collective-permute-start | bytes 110600 | tf_op jit(solution)/shard_map/ppermute | solution.py:446
  898.2 75.3 %collective-permute-start.178 = (bf16[512,384]{1,0:T(8,128)(2,1)}, bf16[512,384]{1,0:T(8,128)(2,1)}, u32[]{:S(2)}, u32[]{:S(2)}) collective-permute-start(bf16[512,384]{1,0:T(8,128)(2,1)} %bitcast.187), channel_id=1, source_target_pairs={{0,1},{1,0},{2,3},{3,2},{4,5},{5,4},{6,7},{7,6},{8,9},{9,8},{10,11... | collective-permute-start | bytes 1179656 | tf_op jit(solution)/shard_map/ppermute | solution.py:451
  901.0 85.8 %collective-permute-start.168 = (bf16[192,1024]{1,0:T(8,128)(2,1)}, bf16[192,1024]{1,0:T(8,128)(2,1)}, u32[]{:S(2)}, u32[]{:S(2)}) collective-permute-start(bf16[192,1024]{1,0:T(8,128)(2,1)} %bitcast.167), channel_id=1, source_target_pairs={{0,1},{1,0},{2,3},{3,2},{4,5},{5,4},{6,7},{7,6},{8,9},{9,8},{10,11... | collective-permute-start | bytes 1179656 | tf_op jit(solution)/shard_map/ppermute | solution.py:451
  902.1 93.0 %collective-permute-start.158 = (bf16[192,1024]{1,0:T(8,128)(2,1)S(1)}, bf16[192,1024]{1,0:T(8,128)(2,1)}, u32[]{:S(2)}, u32[]{:S(2)}) collective-permute-start(bf16[192,1024]{1,0:T(8,128)(2,1)S(1)} %bitcast.504), channel_id=1, source_target_pairs={{0,1},{1,0},{2,3},{3,2},{4,5},{5,4},{6,7},{7,6},{8,9},{9,8},{10,11... | collective-permute-start | bytes 1179656 | tf_op jit(solution)/shard_map/ppermute | solution.py:451
  903.1 34.4 %collective-permute-start.138 = (bf16[192,384]{1,0:T(8,128)(2,1)S(1)}, bf16[192,384]{1,0:T(8,128)(2,1)S(1)}, u32[]{:S(2)}, u32[]{:S(2)}) collective-permute-start(bf16[192,384]{1,0:T(8,128)(2,1)S(1)} %bitcast.522), channel_id=1, source_target_pairs={{0,1},{1,0},{2,3},{3,2},{4,5},{5,4},{6,7},{7,6},{8,9},{9,8},{10,11... | collective-permute-start | bytes 442376 | tf_op jit(solution)/shard_map/ppermute | solution.py:451
  904.2 38.3 %collective-permute-start.128 = (bf16[192,384]{1,0:T(8,128)(2,1)S(1)}, bf16[192,384]{1,0:T(8,128)(2,1)S(1)}, u32[]{:S(2)}, u32[]{:S(2)}) collective-permute-start(bf16[192,384]{1,0:T(8,128)(2,1)S(1)} %bitcast.524), channel_id=1, source_target_pairs={{0,1},{1,0},{2,3},{3,2},{4,5},{5,4},{6,7},{7,6},{8,9},{9,8},{10,11... | collective-permute-start | bytes 442376 | tf_op jit(solution)/shard_map/ppermute | solution.py:451
  (435 other events, 5333.5 us)

commit v2 on v1

v2 whole, which is shorter than its diff:
```python
import functools

import jax
import jax.numpy as jnp
from jax import lax
from jax.experimental import pallas as pl
from jax.experimental.pallas import tpu as pltpu
from jax.sharding import PartitionSpec as P

H = 12
DH = 64
NB = 32
OUTER = 4
HEADS = H // OUTER
HW = HEADS * DH
BLK = 256
AUG = DH + 16
SPAN = 4 * BLK
LOG2E = 1.4426950408889634
LN2 = 0.6931471805599453
F32 = jnp.float32
BF16 = jnp.bfloat16
NT = (((1,), (1,)), ((), ()))
VMEM_BYTES = 56 << 20
GROUP_B = 2

epsilon = 1e-06
limits = (1, 2, 3, 4, 5, 6, 7, 8, 12, 16, 23, 32, 46, 64, 91)
highest = lax.Precision.HIGHEST


def bucket_of(relative):
    distance = jnp.abs(relative)
    count = sum(((distance >= limit).astype(jnp.int32) for limit in limits))
    return count + (relative > 0).astype(jnp.int32) * (NB // 2)


def scale_norm(values, gain):
    return values * lax.rsqrt(jnp.mean(values * values, axis=-1, keepdims=True) + epsilon) * gain


def gating(gate, upward):
    return jax.nn.gelu(gate, approximate=True) * upward


def params():
    return pltpu.CompilerParams(vmem_limit_bytes=VMEM_BYTES)


def smem():
    return pl.BlockSpec(memory_space=pltpu.SMEM)


def whole():
    return pl.BlockSpec(memory_space=pltpu.VMEM)


def split3(v):
    a = v.astype(BF16)
    r = v - a.astype(F32)
    b = r.astype(BF16)
    c = (r - b.astype(F32)).astype(BF16)
    return a.astype(F32), b.astype(F32), c.astype(F32)


def tail(width, values):
    row = lax.broadcasted_iota(jnp.int32, (16, width), 0)
    out = jnp.zeros((16, width), F32)
    for i, v in enumerate(values):
        out = jnp.where(row == i, v, out)
    return out


def tiles_kernel(line_ref, out_ref):
    out_ref[0, 0] = jnp.zeros((BLK, BLK), F32)
    out_ref[0, 4] = jnp.zeros((BLK, BLK), F32)
    line = jnp.broadcast_to(line_ref[0], (BLK, SPAN))
    for off in (-1, 0, 1):
        shift = (off * BLK - (2 * BLK - 1)) % SPAN
        rolled = pltpu.roll(line, shift, 1, stride=1, stride_axis=0)
        out_ref[0, off + 2] = rolled[:, :BLK]


def bias_tiles(lines):
    heads = lines.shape[0]
    return pl.pallas_call(
        tiles_kernel,
        grid=(heads,),
        in_specs=[pl.BlockSpec((1, 1, SPAN), lambda h: (h, 0, 0))],
        out_specs=pl.BlockSpec((1, 5, BLK, BLK), lambda h: (h, 0, 0, 0)),
        out_shape=jax.ShapeDtypeStruct((heads, 5, BLK, BLK), F32),
        compiler_params=params(),
        name="bias_tiles",
    )(lines)


def diagonals_kernel(near_ref, out_ref):
    row = lax.broadcasted_iota(jnp.int32, (BLK, BLK), 0)
    col = lax.broadcasted_iota(jnp.int32, (BLK, BLK), 1)
    flip = (row + col == BLK - 1).astype(F32)
    total = jnp.zeros((1, SPAN), F32)
    for off in (-1, 0, 1):
        flipped = jnp.dot(flip, near_ref[0, off + 2], preferred_element_type=F32, precision=highest)
        padded = jnp.concatenate([flipped, jnp.zeros((BLK, SPAN - BLK), F32)], axis=1)
        rolled = pltpu.roll(padded, (BLK - off * BLK) % SPAN, 1, stride=1, stride_axis=0)
        total = total + jnp.sum(rolled, axis=0, keepdims=True)
    out_ref[0] = total


def diagonal_sums(near):
    heads = near.shape[0]
    return pl.pallas_call(
        diagonals_kernel,
        grid=(heads,),
        in_specs=[pl.BlockSpec((1, 5, BLK, BLK), lambda h: (h, 0, 0, 0))],
        out_specs=pl.BlockSpec((1, 1, SPAN), lambda h: (h, 0, 0)),
        out_shape=jax.ShapeDtypeStruct((heads, 1, SPAN), F32),
        compiler_params=params(),
        name="diagonal_sums",
    )(near)


def peers(n, z, x):
    return [lax.rem(z + d, OUTER) * n + x for d in range(1, OUTER)] + [z * n + lax.rem(x + s, n) for s in range(1, n)]


def greet(n, z, x):
    barrier = pltpu.get_barrier_semaphore()
    for peer in peers(n, z, x):
        pl.semaphore_signal(barrier, inc=1, device_id={"seq": peer}, device_id_type=pl.DeviceIdType.MESH)
    pl.semaphore_wait(barrier, OUTER - 1 + n - 1)


def remote(src, dst, send, recv, peer):
    return pltpu.make_async_remote_copy(
        src_ref=src,
        dst_ref=dst,
        send_sem=send,
        recv_sem=recv,
        device_id={"seq": peer},
        device_id_type=pl.DeviceIdType.MESH,
    )


def far_case(n, j, kb):
    if kb < n * j - 1:
        return 0
    if kb > n * j + n:
        return 2
    return None


def near_case(n, j, kb, x):
    off = kb - (n * j + x)
    return jnp.clip(off + 2, 0, 4), jnp.where(off <= -2, 0, jnp.where(off >= 2, 2, 1))


def key_rows(keys, kb, length):
    one = jnp.ones((1, BLK), F32)
    lane = lax.broadcasted_iota(jnp.int32, (1, BLK), 1)
    mask = jnp.where(kb * BLK + lane < length, 0.0, -1e30)
    return jnp.concatenate([keys, tail(BLK, (one, one, one, mask)).astype(BF16)], axis=0).T


def forward_kernel(
    n, len_ref, far_ref, tile_ref, x_ref, gain_ref, wq_ref, wk_ref, wv_ref,
    normed_ref, own, pair, att, o_ref, lse_ref,
    send, ka, qa, va,
    z_send, z_recv, x_send, x_recv, o_send, o_recv,
):
    nk = OUTER * n
    batch = x_ref.shape[0]
    units = batch * HEADS
    me = lax.axis_index("seq")
    z, x = lax.div(me, n), lax.rem(me, n)
    greet(n, z, x)

    def z_copy(u, d):
        group = lax.rem(z + d, OUTER)
        return remote(send.at[u, group], own.at[u, z], z_send.at[u, d - 1], z_recv.at[u, d - 1], group * n + x)

    def x_copy(u, s, d):
        group = lax.rem(z + OUTER - d, OUTER)
        rows = pl.ds(DH, 2 * DH)
        peer = z * n + lax.rem(x + s, n)
        return remote(
            own.at[u, group, rows], pair.at[s - 1, u, group], x_send.at[s - 1, u, d], x_recv.at[s - 1, u, d], peer
        )

    def o_copy(u, d):
        group = lax.rem(z + d, OUTER)
        b, h = lax.div(u, HEADS), lax.rem(u, HEADS)
        rows = pl.ds(pl.multiple_of((z * HEADS + h) * DH, DH), DH)
        return remote(o_ref.at[u, group], att.at[b, rows], o_send.at[u, d - 1], o_recv.at[u, d - 1], group * n + x)

    for b in range(batch):
        values = x_ref[b]
        scale = lax.rsqrt(jnp.mean(values * values, axis=-1, keepdims=True) + epsilon)
        normed = (values * scale * gain_ref[...]).astype(BF16)
        normed_ref[b] = normed
        for i, (w_ref, factor) in enumerate(((wq_ref, LOG2E), (wk_ref, 1.0), (wv_ref, 1.0))):
            turned = (jnp.dot(normed, w_ref[...], preferred_element_type=F32) * factor).T.astype(BF16)
            for g in range(OUTER):
                for h in range(HEADS):
                    first = (g * HEADS + h) * DH
                    send[b * HEADS + h, g, i * DH : (i + 1) * DH] = turned[first : first + DH]
        for h in range(HEADS):
            u = b * HEADS + h
            for d in (2, 1, 3):
                z_copy(u, d).start()
            own[u, z] = send[u, z]
            for s in range(1, n):
                x_copy(u, s, 0).start()

    def attend(u):
        b, h = lax.div(u, HEADS), lax.rem(u, HEADS)
        length = len_ref[b]
        left, right = far_ref[h, 0], far_ref[h, 1]
        one = jnp.ones((1, BLK), F32)
        vtail = tail(BLK, (one,)).astype(BF16)
        for s in range(1, n):
            for d in range(OUTER):
                x_copy(u, s, d).wait_recv()
        for s in range(n):
            col = lax.rem(x + s, n)
            for j in range(OUTER):
                kb = n * j + col
                if s == 0:
                    keys, vals = own[u, j, DH : 2 * DH], own[u, j, 2 * DH :]
                else:
                    keys, vals = pair[n - s - 1, u, j, :DH], pair[n - s - 1, u, j, DH:]
                ka[kb] = key_rows(keys, kb, length)
                va[kb, :DH] = vals
                va[kb, DH:] = vtail

        def scores(kb, j):
            case = far_case(n, j, kb)
            if case is not None:
                return jnp.dot(ka[kb], qa[case, j], preferred_element_type=F32)
            tile, case = near_case(n, j, kb, x)
            return jnp.dot(ka[kb], qa[case, j], preferred_element_type=F32) + tile_ref[h, tile]

        for j in range(OUTER):
            for v, c in enumerate((left, 0.0, right)):
                qa[v, j, :DH] = own[u, j, :DH]
                qa[v, j, DH:] = tail(BLK, split3(jnp.zeros((1, BLK), F32) + c) + (one,)).astype(BF16)
        tops = []
        for j in range(OUTER):
            top = jnp.full((8, BLK), -1e30, F32)
            for kb in range(nk):
                top = jnp.maximum(top, jnp.max(scores(kb, j).reshape(BLK // 8, 8, BLK), axis=0))
            top = jnp.max(top, axis=0, keepdims=True)
            tops.append(top)
            for v, c in enumerate((left, 0.0, right)):
                qa[v, j, DH:] = tail(BLK, split3(c - top) + (one,)).astype(BF16)
        for j in range(OUTER):
            total = jnp.zeros((AUG, BLK), F32)
            for kb in range(nk):
                p = jnp.exp2(scores(kb, j)).astype(BF16)
                total = total + jnp.dot(va[kb], p, preferred_element_type=F32)
            weight = total[DH : DH + 1]
            o_ref[u, j] = (total[:DH] / weight).astype(BF16)
            lse_ref[u, j] = tops[j] + jnp.log2(weight)
        rows = pl.ds(pl.multiple_of((z * HEADS + h) * DH, DH), DH)
        att[b, rows] = o_ref[u, z]
        for d in (2, 1, 3):
            o_copy(u, d).start()

    def turn(u, carry):
        @pl.when(u < units)
        def _():
            for d in (1, 3, 2):
                z_copy(u, d).wait_recv()
                for s in range(1, n):
                    x_copy(u, s, d).start()

        @pl.when(u > 0)
        def _():
            attend(u - 1)

        return carry

    lax.fori_loop(0, units + 1, turn, 0)

    def finish(u, carry):
        for d in range(1, OUTER):
            z_copy(u, d).wait_send()
            o_copy(u, d).wait_send()
            o_copy(u, d).wait_recv()
        for s in range(1, n):
            for d in range(OUTER):
                x_copy(u, s, d).wait_send()
        return carry

    lax.fori_loop(0, units, finish, 0)


def attention_forward(n, lengths, far, tiles, inputs, gain, wq, wk, wv):
    batch, height, width = inputs.shape
    units, nk = batch * HEADS, n * OUTER
    dma = pltpu.SemaphoreType.DMA
    return pl.pallas_call(
        functools.partial(forward_kernel, n),
        in_specs=[smem()] * 2 + [whole()] * 6,
        out_specs=[whole()] * 6,
        out_shape=[
            jax.ShapeDtypeStruct((batch, height, width), BF16),
            jax.ShapeDtypeStruct((units, OUTER, 3 * DH, BLK), BF16),
            jax.ShapeDtypeStruct((n - 1, units, OUTER, 2 * DH, BLK), BF16),
            jax.ShapeDtypeStruct((batch, width, height), BF16),
            jax.ShapeDtypeStruct((units, OUTER, DH, BLK), BF16),
            jax.ShapeDtypeStruct((units, OUTER, 1, BLK), F32),
        ],
        scratch_shapes=[
            pltpu.VMEM((units, OUTER, 3 * DH, BLK), BF16),
            pltpu.VMEM((nk, BLK, AUG), BF16),
            pltpu.VMEM((3, OUTER, AUG, BLK), BF16),
            pltpu.VMEM((nk, AUG, BLK), BF16),
            dma((units, OUTER - 1)),
            dma((units, OUTER - 1)),
            dma((n - 1, units, OUTER)),
            dma((n - 1, units, OUTER)),
            dma((units, OUTER - 1)),
            dma((units, OUTER - 1)),
        ],
        compiler_params=pltpu.CompilerParams(
            vmem_limit_bytes=VMEM_BYTES, collective_id=0, has_side_effects=True
        ),
        cost_estimate=pl.CostEstimate(flops=45 * 10**9, bytes_accessed=24 << 20, transcendentals=0),
        name="attention_forward",
    )(lengths, far, tiles, inputs, gain.reshape(1, -1), wq, wk, wv)


def backward_kernel(
    n, len_ref, far_ref, tile_ref, own, pair, o_ref, lse_ref, dout,
    grads, near, far_sum,
    do_land, x_out, x_land, z_out, kept,
    ka, kt, va, qa, da, dk_all, dv_all,
    d_send, d_recv, x_send, x_recv, z_send, z_recv,
):
    nk = OUTER * n
    batch = dout.shape[0]
    units = batch * HEADS
    me = lax.axis_index("seq")
    z, x = lax.div(me, n), lax.rem(me, n)
    greet(n, z, x)

    def head_rows(group, h):
        return pl.ds(pl.multiple_of((group * HEADS + h) * DH, DH), DH)

    def d_copy(u, d):
        group = lax.rem(z + d, OUTER)
        b, h = lax.div(u, HEADS), lax.rem(u, HEADS)
        return remote(
            dout.at[b, head_rows(group, h)], do_land.at[u, z], d_send.at[u, d - 1], d_recv.at[u, d - 1], group * n + x
        )

    def x_copy(u, s):
        peer = z * n + lax.rem(x + s, n)
        return remote(x_out.at[s - 1, u], x_land.at[s - 1, u], x_send.at[s - 1, u], x_recv.at[s - 1, u], peer)

    def z_copy(u, d, i):
        group = lax.rem(z + d, OUTER)
        b, h = lax.div(u, HEADS), lax.rem(u, HEADS)
        return remote(
            z_out.at[u, group, pl.ds(i * DH, DH)],
            grads.at[i, b, head_rows(z, h)],
            z_send.at[u, d - 1, i],
            z_recv.at[u, d - 1, i],
            group * n + x,
        )

    def begin(u, carry):
        for d in (2, 1, 3):
            d_copy(u, d).start()
        do_land[u, z] = dout[lax.div(u, HEADS), head_rows(z, lax.rem(u, HEADS))]
        return carry

    lax.fori_loop(0, units, begin, 0)
    near[...] = jnp.zeros_like(near)
    far_sum[...] = jnp.zeros_like(far_sum)
    one = jnp.ones((1, BLK), F32)
    ones3 = tail(BLK, (one, one, one)).astype(BF16)
    row16 = lax.broadcasted_iota(jnp.int32, (16, BLK), 0)
    marks = [jnp.where(row16 == r, 1.0, 0.0).astype(BF16) for r in range(2)]

    def work(u):
        b, h = lax.div(u, HEADS), lax.rem(u, HEADS)
        length = len_ref[b]
        left, right = far_ref[h, 0], far_ref[h, 1]
        for s in range(n):
            col = lax.rem(x + s, n)
            for j in range(OUTER):
                kb = n * j + col
                if s == 0:
                    keys, vals = own[u, j, DH : 2 * DH], own[u, j, 2 * DH :]
                else:
                    keys, vals = pair[n - s - 1, u, j, :DH], pair[n - s - 1, u, j, DH:]
                ka[kb] = key_rows(keys, kb, length)
                kt[kb] = keys
                va[kb] = jnp.concatenate([vals, ones3], axis=0).T
        for d in range(1, OUTER):
            d_copy(u, d).wait_recv()
        for j in range(OUTER):
            lse = lse_ref[u, j]
            for v, c in enumerate((left, 0.0, right)):
                qa[v, j, :DH] = own[u, j, :DH]
                qa[v, j, DH:] = tail(BLK, split3(c - lse) + (one,)).astype(BF16)
            arrived = do_land[u, j]
            delta = jnp.sum(arrived.astype(F32) * o_ref[u, j].astype(F32), axis=0, keepdims=True)
            da[j, :DH] = arrived
            da[j, DH:] = tail(BLK, split3(-delta)).astype(BF16)
        dqs = [jnp.zeros((AUG, BLK), F32) for _ in range(OUTER)]
        for g in range(0, nk, GROUP_B):
            dvs = {kb: jnp.zeros((DH, BLK), F32) for kb in range(g, g + GROUP_B)}
            dks = {kb: jnp.zeros((DH, BLK), F32) for kb in range(g, g + GROUP_B)}
            for j in range(OUTER):
                for kb in range(g, g + GROUP_B):
                    case = far_case(n, j, kb)
                    if case is not None:
                        p = jnp.exp2(jnp.dot(ka[kb], qa[case, j], preferred_element_type=F32))
                        mark = marks[case // 2]
                    else:
                        tile, case = near_case(n, j, kb, x)
                        s = jnp.dot(ka[kb], qa[case, j], preferred_element_type=F32)
                        p = jnp.exp2(s + tile_ref[h, tile])
                        want = jnp.where(case == 1, 2, lax.div(case, 2))
                        mark = jnp.where(row16 == want, 1.0, 0.0).astype(BF16)
                    ds = p * jnp.dot(va[kb], da[j], preferred_element_type=F32)
                    if far_case(n, j, kb) is None:
                        near[h, tile] += ds
                    p16, ds16 = p.astype(BF16), ds.astype(BF16)
                    lhs = jnp.concatenate([kt[kb], mark], axis=0)
                    dqs[j] = dqs[j] + jnp.dot(lhs, ds16, preferred_element_type=F32)
                    dvs[kb] += lax.dot_general(da[j, :DH], p16, NT, preferred_element_type=F32)
                    dks[kb] += lax.dot_general(qa[0, j, :DH], ds16, NT, preferred_element_type=F32)
            for kb in range(g, g + GROUP_B):
                dk_all[kb] = dks[kb] * LN2
                dv_all[kb] = dvs[kb]
        far = jnp.zeros((8, BLK), F32)
        for j in range(OUTER):
            z_out[u, j, :DH] = dqs[j][:DH].astype(BF16)
            far = far + dqs[j][DH : DH + 8]
        far_sum[h] += far
        parity = lax.rem(u, 2)
        for j in range(OUTER):
            kept[parity, j, :DH] = dk_all[n * j + x]
            kept[parity, j, DH:] = dv_all[n * j + x]
            for s in range(1, n):
                kb = n * j + lax.rem(x + s, n)
                x_out[s - 1, u, j, :DH] = dk_all[kb].astype(BF16)
                x_out[s - 1, u, j, DH:] = dv_all[kb].astype(BF16)
        for s in range(1, n):
            x_copy(u, s).start()

    def hand_over(u):
        b, h = lax.div(u, HEADS), lax.rem(u, HEADS)
        parity = lax.rem(u, 2)
        for s in range(1, n):
            x_copy(u, s).wait_recv()
        for j in range(OUTER):
            total = kept[parity, j]
            for s in range(1, n):
                total = total + x_land[s - 1, u, j].astype(F32)
            z_out[u, j, DH:] = total.astype(BF16)
        for i in range(3):
            grads[i, b, head_rows(z, h)] = z_out[u, z, i * DH : (i + 1) * DH]
            for d in (2, 1, 3):
                z_copy(u, d, i).start()

    def turn(u, carry):
        @pl.when(u < units)
        def _():
            work(u)

        @pl.when(u > 0)
        def _():
            hand_over(u - 1)

        return carry

    lax.fori_loop(0, units + 1, turn, 0)

    def finish(u, carry):
        for d in range(1, OUTER):
            d_copy(u, d).wait_send()
            for i in range(3):
                z_copy(u, d, i).wait_send()
                z_copy(u, d, i).wait_recv()
        for s in range(1, n):
            x_copy(u, s).wait_send()
        return carry

    lax.fori_loop(0, units, finish, 0)


def attention_backward(n, lengths, far, tiles, own, pair, out, lse, dout):
    batch, width, height = dout.shape
    units, nk = batch * HEADS, n * OUTER
    dma = pltpu.SemaphoreType.DMA
    return pl.pallas_call(
        functools.partial(backward_kernel, n),
        in_specs=[smem()] * 2 + [whole()] * 6,
        out_specs=[whole()] * 3,
        out_shape=[
            jax.ShapeDtypeStruct((3, batch, width, height), BF16),
            jax.ShapeDtypeStruct((HEADS, 5, BLK, BLK), F32),
            jax.ShapeDtypeStruct((HEADS, 8, BLK), F32),
        ],
        scratch_shapes=[
            pltpu.VMEM((units, OUTER, DH, BLK), BF16),
            pltpu.VMEM((n - 1, units, OUTER, 2 * DH, BLK), BF16),
            pltpu.VMEM((n - 1, units, OUTER, 2 * DH, BLK), BF16),
            pltpu.VMEM((units, OUTER, 3 * DH, BLK), BF16),
            pltpu.VMEM((2, OUTER, 2 * DH, BLK), F32),
            pltpu.VMEM((nk, BLK, AUG), BF16),
            pltpu.VMEM((nk, DH, BLK), BF16),
            pltpu.VMEM((nk, BLK, AUG), BF16),
            pltpu.VMEM((3, OUTER, AUG, BLK), BF16),
            pltpu.VMEM((OUTER, AUG, BLK), BF16),
            pltpu.VMEM((nk, DH, BLK), F32),
            pltpu.VMEM((nk, DH, BLK), F32),
            dma((units, OUTER - 1)),
            dma((units, OUTER - 1)),
            dma((n - 1, units)),
            dma((n - 1, units)),
            dma((units, OUTER - 1, 3)),
            dma((units, OUTER - 1, 3)),
        ],
        compiler_params=pltpu.CompilerParams(
            vmem_limit_bytes=VMEM_BYTES, collective_id=1, has_side_effects=True
        ),
        cost_estimate=pl.CostEstimate(flops=110 * 10**9, bytes_accessed=24 << 20, transcendentals=0),
        name="attention_backward",
    )(lengths, far, tiles, own, pair, out, lse, dout)


class Places:
    def __init__(self, mesh):
        self.dp = mesh.shape["dp"]
        self.seq = mesh.shape["seq"]
        self.inner = self.seq // OUTER
        self.cores = 2
        self.groups = self.dp // self.cores

    def shift_outer(self, value, d):
        n = self.inner
        pairs = [(o * n + i, (o + d) % OUTER * n + i) for o in range(OUTER) for i in range(n)]
        return lax.ppermute(value, "seq", pairs)

    def shift_inner(self, value, d):
        n = self.inner
        pairs = [(o * n + i, o * n + (i + d) % n) for o in range(OUTER) for i in range(n)]
        return lax.ppermute(value, "seq", pairs)

    def shift_core(self, value, d):
        c = self.cores
        pairs = [(g * c + i, g * c + (i + d) % c) for g in range(self.groups) for i in range(c)]
        return lax.ppermute(value, "dp", pairs)

    def shift_group(self, value, d):
        c, g = self.cores, self.groups
        pairs = [(o * c + i, (o + d) % g * c + i) for o in range(g) for i in range(c)]
        return lax.ppermute(value, "dp", pairs)


def scatter_sum(pieces, at, size, axis, shift):
    total = pieces(at).astype(F32)
    for d in range(1, size):
        part = pieces(lax.rem(at + d, size))
        total = total + shift(part, d).astype(F32)
    return total


def pick(value, index, axis):
    return lax.dynamic_index_in_dim(value, index, axis, keepdims=False)


def reduce_grad(places, grad, kind):
    rows, columns = grad.shape
    c, g, n = places.cores, places.groups, places.inner
    share = rows // places.dp
    dp, seq = lax.axis_index("dp"), lax.axis_index("seq")
    parts = grad.astype(kind).reshape(g, c, share, columns)
    held = scatter_sum(lambda i: pick(parts, i, 1), lax.rem(dp, c), c, 1, places.shift_core).astype(kind)
    held = scatter_sum(lambda i: pick(held, i, 0), dp // c, g, 0, places.shift_group).astype(kind)
    wide = columns // n
    slabs = held.reshape(share, n, wide)
    held = scatter_sum(lambda i: pick(slabs, i, 1), lax.rem(seq, n), n, 1, places.shift_inner).astype(kind)
    lines = held.reshape(OUTER, share // OUTER, wide)
    z, x = seq // n, lax.rem(seq, n)
    held = scatter_sum(lambda i: pick(lines, i, 0), z, OUTER, 0, places.shift_outer).astype(kind)
    full = jnp.zeros((OUTER, share // OUTER, wide), kind)
    full = lax.dynamic_update_index_in_dim(full, held, z, 0)
    for d in range(1, OUTER):
        full = lax.dynamic_update_index_in_dim(full, places.shift_outer(held, d), lax.rem(z + OUTER - d, OUTER), 0)
    full = full.reshape(share, wide)
    result = jnp.zeros((share, n, wide), kind)
    result = lax.dynamic_update_index_in_dim(result, full, x, 1)
    for d in range(1, n):
        result = lax.dynamic_update_index_in_dim(result, places.shift_inner(full, d), lax.rem(x + n - d, n), 1)
    return result.reshape(share, columns).astype(F32)


def shards(
    places,
    inputs,
    lengths,
    norm_attn,
    w_query,
    w_key,
    w_value,
    w_out,
    norm_ffn,
    w_gate,
    w_up,
    w_down,
    bucket_bias,
    cotangent,
):
    batch, height, width = inputs.shape
    n = places.inner
    seq = lax.axis_index("seq")
    z, x = seq // n, lax.rem(seq, n)

    table = lax.dynamic_slice_in_dim(bucket_bias, z * HEADS, HEADS, 1) * LOG2E
    relative = 2 * BLK - 1 - jnp.arange(SPAN, dtype=jnp.int32)
    onehot = (bucket_of(relative)[:, None] == jnp.arange(NB, dtype=jnp.int32)[None, :]).astype(F32)
    lines = jnp.einsum("cn,nh->hc", onehot, table, precision=highest)[:, None, :]
    tiles = bias_tiles(lines)
    far = jnp.stack([table[NB // 2 - 1], table[NB - 1], jnp.max(jnp.abs(table), axis=0)], axis=1)

    normed, own, pair, attended_t, out, lse = attention_forward(
        n, lengths, far, tiles, inputs, norm_attn, w_query, w_key, w_value
    )
    mixed = inputs + jnp.einsum("bes,ed->bsd", attended_t, w_out, preferred_element_type=F32)
    normed_ffn = scale_norm(mixed, norm_ffn).astype(BF16)
    gate = jnp.einsum("bsd,de->bse", normed_ffn, w_gate, preferred_element_type=F32)
    upward = jnp.einsum("bsd,de->bse", normed_ffn, w_up, preferred_element_type=F32)
    hidden = gating(gate, upward).astype(BF16)
    result = mixed + jnp.einsum("bsd,de->bse", hidden, w_down, preferred_element_type=F32)
    grad_out_low = cotangent.astype(BF16)
    grad_down = jnp.einsum("bsd,bse->de", hidden, grad_out_low, preferred_element_type=F32)
    grad_hidden = jnp.einsum("bse,de->bsd", grad_out_low, w_down, preferred_element_type=F32)
    _, gating_back = jax.vjp(gating, gate, upward)
    grad_gate_raw, grad_up_raw = gating_back(grad_hidden)
    grad_gate_low = grad_gate_raw.astype(BF16)
    grad_up_low = grad_up_raw.astype(BF16)
    grad_w_gate = jnp.einsum("bsd,bse->de", normed_ffn, grad_gate_low, preferred_element_type=F32)
    grad_w_up = jnp.einsum("bsd,bse->de", normed_ffn, grad_up_low, preferred_element_type=F32)
    grad_normed_ffn = jnp.einsum("bse,de->bsd", grad_gate_low, w_gate, preferred_element_type=F32) + jnp.einsum(
        "bse,de->bsd", grad_up_low, w_up, preferred_element_type=F32
    )
    _, second_back = jax.vjp(scale_norm, mixed, norm_ffn)
    grad_mixed_norm, grad_norm_ffn = second_back(grad_normed_ffn)
    grad_mixed = cotangent + grad_mixed_norm
    grad_mixed_low = grad_mixed.astype(BF16)
    grad_w_out = jnp.einsum("bes,bsd->ed", attended_t, grad_mixed_low, preferred_element_type=F32)
    grad_attended_t = jnp.einsum("bsd,ed->bes", grad_mixed_low, w_out, preferred_element_type=F32).astype(BF16)

    part_gate = reduce_grad(places, grad_w_gate, BF16)
    part_up = reduce_grad(places, grad_w_up, BF16)
    part_down = reduce_grad(places, grad_down, BF16)
    part_out = reduce_grad(places, grad_w_out, BF16)

    grads, near, far_sum = attention_backward(n, lengths, far, tiles, own, pair, out, lse, grad_attended_t)
    grad_q, grad_k, grad_v = grads[0], grads[1], grads[2]
    grad_w_query = jnp.einsum("bsd,bes->de", normed, grad_q, preferred_element_type=F32)
    grad_w_key = jnp.einsum("bsd,bes->de", normed, grad_k, preferred_element_type=F32)
    grad_w_value = jnp.einsum("bsd,bes->de", normed, grad_v, preferred_element_type=F32)
    part_query = reduce_grad(places, grad_w_query, BF16)
    part_key = reduce_grad(places, grad_w_key, BF16)
    part_value = reduce_grad(places, grad_w_value, BF16)
    grad_normed = (
        jnp.einsum("bes,de->bsd", grad_q, w_query, preferred_element_type=F32)
        + jnp.einsum("bes,de->bsd", grad_k, w_key, preferred_element_type=F32)
        + jnp.einsum("bes,de->bsd", grad_v, w_value, preferred_element_type=F32)
    )
    _, first_back = jax.vjp(scale_norm, inputs, norm_attn)
    grad_inputs_norm, grad_norm_attn = first_back(grad_normed)
    grad_inputs = grad_mixed + grad_inputs_norm

    lines_sum = diagonal_sums(near)[:, 0]
    table_part = jnp.einsum("cn,hc->nh", onehot, lines_sum, precision=highest)
    far_total = jnp.sum(far_sum, axis=-1)
    bucket = jnp.arange(NB, dtype=jnp.int32)[:, None]
    table_part = table_part + jnp.where(bucket == NB // 2 - 1, far_total[:, 0][None, :], 0.0)
    table_part = table_part + jnp.where(bucket == NB - 1, far_total[:, 1][None, :], 0.0)
    grad_table = lax.dynamic_update_slice_in_dim(jnp.zeros((NB, H), F32), table_part, z * HEADS, 1)
    small = jnp.concatenate(
        [
            grad_norm_attn.reshape(places.dp, -1),
            grad_norm_ffn.reshape(places.dp, -1),
            grad_table.reshape(places.dp, -1),
        ],
        axis=1,
    )
    used = small.shape[1]
    small = jnp.pad(small, ((0, 0), (0, 32 * 128 - used))).reshape(places.dp * 32, 128)
    small = reduce_grad(places, small, F32).reshape(-1)
    share = width // places.dp
    return (
        result,
        grad_inputs,
        small[:share],
        small[share : 2 * share],
        part_query,
        part_key,
        part_value,
        part_out,
        part_gate,
        part_up,
        part_down,
        small[2 * share : used].reshape(NB // places.dp, H),
    )


def solution(mesh):
    rows = P("dp", "seq", None)
    share = P("dp", None)
    return jax.shard_map(
        functools.partial(shards, Places(mesh)),
        mesh=mesh,
        in_specs=(rows, P("dp")) + (P(),) * 10 + (rows,),
        out_specs=(rows, rows, P("dp"), P("dp")) + (share,) * 8,
        check_vma=False,
    )
```

time: 1020 us -> 711 us (0.70)
  local copies, waits for them, and re-layouts: 332 us -> 164 us
  starting transfers between devices: 222 us -> 82.3 us
  Pallas kernels: 123 us -> 242 us
  waiting for transfers between devices: 212 us -> 109 us
  other arithmetic: 57.6 us -> 34 us
    unnamed x648 -> x126, local copies, waits for them, and re-layouts: 155 us -> 22.8 us
    pallas_call x9 -> x2, Pallas kernels: 118 us -> 233 us  [the longest x1 117 us: attention_forward(): pl.pallas_call(functools.partial(forward_kernel, n), in_specs=[smem()] *...]
    ppermute x111 -> x48, waiting for transfers between devices: 150 us -> 57.8 us  [shift_outer(): return lax.ppermute(value, 'seq', pairs)]
    ppermute x111 -> x48, starting transfers between devices: 135 us -> 53.5 us  [shift_outer(): return lax.ppermute(value, 'seq', pairs)]
    ppermute x52 -> x16, starting transfers between devices: 56.7 us -> 16.5 us  [shift_inner(): return lax.ppermute(value, 'seq', pairs)]
    another operation x36 -> x12, local copies, waits for them, and re-layouts: 29.6 us -> 3.64 us  [the longest x6 10.1 us: shards(): attended_t = jnp.stack(attended)]
    ppermute x8, starting transfers between devices: 29 us -> 10.6 us  [shift_group(): return lax.ppermute(value, 'dp', pairs)]
    convert_element_type x18 -> x0, other arithmetic: 12.9 us -> none  [the longest x9 6.92 us: shards(): dv_sum.append(v_total.astype(BF16))]
  transfers between devices with their start and end apart: 179 -> 80, of which waited for: 68 -> 40; matrix products, arithmetic and copies ran while one was open for 28% -> 29% of each run, Pallas kernels for 12% -> 17%
where the time goes in v2:
time: 711 us; the launch traced here: 702 us
  Pallas kernels  242 us (34%)
  local copies, waits for them, and re-layouts  164 us (23%)
  waiting for transfers between devices  109 us (15%)
  starting transfers between devices  82.3 us (12%)
  matrix products  68.8 us (10%)
  other arithmetic  34 us (5%)
    pallas_call x1, Pallas kernels, attention_forward(): pl.pallas_call(functools.partial(forward_kernel, n), in_specs=[smem()] *...  117 us
    pallas_call x1, Pallas kernels, attention_backward(): pl.pallas_call(functools.partial(backward_kernel, n), in_specs=[smem()] *...  116 us
    ppermute x48, waiting for transfers between devices, shift_outer(): return lax.ppermute(value, 'seq', pairs)  57.8 us
    ppermute x48, starting transfers between devices, shift_outer(): return lax.ppermute(value, 'seq', pairs)  53.5 us
    dynamic_update_slice x8, local copies, waits for them, and re-layouts, reduce_grad(): lax.dynamic_update_index_in_dim(result, places.shift_inner(full, d), lax....  45.1 us
    ppermute x8, waiting for transfers between devices, shift_group(): return lax.ppermute(value, 'dp', pairs)  44.5 us
    dynamic_update_slice x8, local copies, waits for them, and re-layouts, reduce_grad(): result = lax.dynamic_update_index_in_dim(result, full, x, 1)  37.1 us
    unnamed x126, local copies, waits for them, and re-layouts  22.8 us
  transfers between devices with their start and end apart: 80, of which 40 were waited for; matrix products, arithmetic and copies ran while one was open for 29% of the time, Pallas kernels for 17%

profile of v2, /device:TPU:0, one launch (start us, length us, event | category | flops | bytes accessed | tf_op | source)
XLA Modules:
  0.0 702.2 jit_solution(4551781624105499403)
XLA Ops:
  7.4 117.3 %attention_forward.1 = (bf16[3,256,768]{2,1,0:T(8,128)(2,1)}, bf16[9,4,192,256]{3,2,1,0:T(8,128)(2,1)}, bf16[1,9,4,128,256]{4,3,2,1,0:T(8,128)(2,1)}, bf16[3,768...) custom-call(s32[3]{0:T(128)} %len_ref.3, f32[3,3]{1,0:T(4,128)} %pad_maximum_fusion.far_ref, ...), custom_call_target="tpu_custom_call" | custom-call | flops 44999999488 | bytes 25165824 | tf_op jit(solution)/shard_map/attention_forward/pallas_call | solution.py:302
  135.8 9.2 %fusion.6 = (bf16[3,256,2048]{2,1,0:T(8,128)(2,1)}, bf16[3,256,2048]{2,1,0:T(8,128)(2,1)}, bf16[3,256,2048]{2,1,0:T(8,128)(2,1)S(1)}) fusion(f32[3,256,2048]{2,1,0:T(8,128)S(1)} %fusion.10, f32[3,256,2048]{2,1,0:T(8,128)S(1)} %fusion.16, bf16[3,256,768]{2,1,0:T(8,128)(2,1)S(1)} %multiply_convert_fusion.2, bf16[768,2048]{1,0:T(8,128)(2,1)S(1)} %copy-done), kind=kOutput, calls=%fused_computation.8 | convolution fusion | flops 2456813568 | bytes 26345472 | tf_op jit(solution)/shard_map/bsd,de->bse/dot_general | solution.py:638
  146.7 4.0 bitcast_convert_fusion
  157.4 5.0 bitcast_convert_fusion.2
  175.2 116.2 %attention_backward.1 = (bf16[3,3,768,256]{3,2,1,0:T(8,128)(2,1)}, f32[3,5,256,256]{3,2,1,0:T(8,128)}, f32[3,8,256]{2,1,0:T(8,128)}) custom-call(s32[3]{0:T(128)} %len_ref.3, f32[3,3]{1,0:T(4,128)} %pad_maximum_fusion.far_ref, f32[3,5,256,256]{3,2,1,0:T(8,128)} %bias_tiles.1.tile_ref, bf16[9,4,192,256]{3,2,1,0:T(8,128)(2,1)} %get-tuple-element.22.own, ...), custom_call_target="tpu_custom_call" | custom-call | flops 109999996928 | bytes 25165824 | tf_op jit(solution)/shard_map/attention_backward/pallas_call | solution.py:501
  299.5 5.1 diagonal_sums.1
  306.6 6.0 multiply_reduce_fusion.1
  313.0 6.7 bitcast_convert_fusion.1
  328.6 4.0 fusion.30
  357.8 4.5 collective-permute-done.7
  384.7 4.7 collective-permute-done.41
  416.2 4.1 collective-permute-start.35
  471.5 14.4 %collective-permute-done.71 = bf16[512,768]{0,1:T(8,128)(2,1)S(1)} collective-permute-done((bf16[512,768]{0,1:T(8,128)(2,1)S(1)}, bf16[512,768]{0,1:T(8,128)(2,1)S(1)}, u32[]{:S(2)}, u32[]{:S(2)}) %collective-permute-start.71) | collective-permute-done | bytes 786464 | tf_op jit(solution)/shard_map/ppermute | solution.py:564
  488.5 14.3 %collective-permute-done.51 = bf16[192,2048]{1,0:T(8,128)(2,1)S(1)} collective-permute-done((bf16[192,2048]{1,0:T(8,128)(2,1)S(1)}, bf16[192,2048]{1,0:T(8,128)(2,1)S(1)}, u32[]{:S(2)}, u32[]{:S(2)}) %collective-permute-start.51) | collective-permute-done | bytes 786464 | tf_op jit(solution)/shard_map/ppermute | solution.py:564
  507.6 5.1 collective-permute-done.61
  559.3 4.5 collective-permute-done.76
  597.7 4.2 dynamic_update_slice.184
  606.3 4.0 dynamic_update_slice.172
  640.2 10.1 %dynamic_update_slice.202 = bf16[512,2,384]{2,1,0:T(2,128)(2,1)S(1)} dynamic-update-slice(bf16[512,2,384]{2,1,0:T(2,128)(2,1)S(1)} %broadcast_in_dim.275, bf16[512,1,384]{2,1,0:T(2,128)(2,1)S(1)} %copy.195, s32[]{:T(128)} %constant.437.clone.1, s32[]{:T(128)S(6)} %select_n.215, s32[]{:T(128)} %constant.437.clone.1) | dynamic-update-slice | bytes 786436 | tf_op jit(solution)/shard_map/jit(dynamic_update_index_in_dim)/dynamic_update_slice | solution.py:599
  650.7 5.3 dynamic_update_slice.196
  656.4 5.3 dynamic_update_slice.190
  663.6 10.1 %dynamic_update_slice.203 = bf16[512,2,384]{2,1,0:T(2,128)(2,1)S(1)} dynamic-update-slice(bf16[512,2,384]{2,1,0:T(2,128)(2,1)S(1)} %dynamic_update_slice.202, bf16[512,1,384]{2,1,0:T(2,128)(2,1)S(1)} %copy.196, s32[]{:T(128)} %constant.437.clone.1, s32[]{:T(128)S(6)} %select_n.216, s32[]{:T(128)} %constant.437.clone.1) | dynamic-update-slice | bytes 786436 | tf_op jit(solution)/shard_map/jit(dynamic_update_index_in_dim)/dynamic_update_slice | solution.py:601
  676.6 5.3 dynamic_update_slice.197
  685.9 13.5 %dynamic_update_slice.191 = bf16[192,2,1024]{2,1,0:T(2,128)(2,1)} dynamic-update-slice(bf16[192,2,1024]{2,1,0:T(2,128)(2,1)} %copy-done.17, bf16[192,1,1024]{2,1,0:T(2,128)(2,1)} %copy.181, s32[]{:T(128)} %constant.437.clone.1, s32[]{:T(128)S(6)} %select_n.216, s32[]{:T(128)} %constant.437.clone.1) | dynamic-update-slice | bytes 786436 | tf_op jit(solution)/shard_map/jit(dynamic_update_index_in_dim)/dynamic_update_slice | solution.py:601
  (458 shorter events, 316.9 us)
Async XLA Ops:
  157.3 305.1 %collective-permute-start.70 = (bf16[2,512,768]{1,2,0:T(8,128)(2,1)}, bf16[2,512,768]{1,2,0:T(8,128)(2,1)}, u32[]{:S(2)}, u32[]{:S(2)}) collective-permute-start(bf16[2,512,768]{1,2,0:T(8,128)(2,1)} %bitcast.461), channel_id=1, source_target_pairs={{0,8},{8,0},{16,24},{24,16},{1,9},{9,1},{17,25},{25,17},{2,10},{10... | collective-permute-start | bytes 4718600 | tf_op jit(solution)/shard_map/ppermute | solution.py:559
  163.8 301.6 %collective-permute-start.50 = (bf16[2,192,2048]{2,1,0:T(8,128)(2,1)}, bf16[2,192,2048]{2,1,0:T(8,128)(2,1)}, u32[]{:S(2)}, u32[]{:S(2)}) collective-permute-start(bf16[2,192,2048]{2,1,0:T(8,128)(2,1)} %dynamic-slice_bitcast_fusion.1), channel_id=1, source_target_pairs={{0,8},{8,0},{16,24},{24,16},{1,9},{9,1},{17,25},{25,17},{2,10},{10... | collective-permute-start | bytes 4718600 | tf_op jit(solution)/shard_map/ppermute | solution.py:559
  312.9 23.9 %collective-permute-start = (f32[2,32,128]{2,1,0:T(8,128)S(1)}, f32[2,32,128]{2,1,0:T(8,128)S(1)}, u32[]{:S(2)}, u32[]{:S(2)}) collective-permute-start(f32[2,32,128]{2,1,0:T(8,128)S(1)} %dynamic-slice_bitcast_fusion.32), channel_id=1, source_target_pairs={{0,8},{8,0},{16,24},{24,16},{1,9},{9,1},{17,25},{25,17},{2,10},{10... | collective-permute-start | bytes 98312 | tf_op jit(solution)/shard_map/ppermute | solution.py:559
  351.8 19.1 %collective-permute-start.30 = (bf16[2,192,768]{2,1,0:T(8,128)(2,1)}, bf16[2,192,768]{2,1,0:T(8,128)(2,1)}, u32[]{:S(2)}, u32[]{:S(2)}) collective-permute-start(bf16[2,192,768]{2,1,0:T(8,128)(2,1)} %dynamic-slice_bitcast_fusion.6), channel_id=1, source_target_pairs={{0,8},{8,0},{16,24},{24,16},{1,9},{9,1},{17,25},{25,17},{2,10},{10... | collective-permute-start | bytes 1769480 | tf_op jit(solution)/shard_map/ppermute | solution.py:559
  351.8 21.2 %collective-permute-start.40 = (bf16[2,192,768]{2,1,0:T(8,128)(2,1)}, bf16[2,192,768]{2,1,0:T(8,128)(2,1)}, u32[]{:S(2)}, u32[]{:S(2)}) collective-permute-start(bf16[2,192,768]{2,1,0:T(8,128)(2,1)} %dynamic-slice_bitcast_fusion.5), channel_id=1, source_target_pairs={{0,8},{8,0},{16,24},{24,16},{1,9},{9,1},{17,25},{25,17},{2,10},{10... | collective-permute-start | bytes 1769480 | tf_op jit(solution)/shard_map/ppermute | solution.py:559
  377.5 11.8 %collective-permute-start.41 = (bf16[192,768]{1,0:T(8,128)(2,1)}, bf16[192,768]{1,0:T(8,128)(2,1)S(1)}, u32[]{:S(2)}, u32[]{:S(2)}) collective-permute-start(bf16[192,768]{1,0:T(8,128)(2,1)} %dynamic-slice_bitcast_fusion.10), channel_id=1, source_target_pairs={{0,16},{8,24},{16,0},{24,8},{1,17},{9,25},{17,1},{25,9},{2,18},{10... | collective-permute-start | bytes 884744 | tf_op jit(solution)/shard_map/ppermute | solution.py:564
  380.0 15.8 %collective-permute-start.11 = (bf16[192,768]{1,0:T(8,128)(2,1)}, bf16[192,768]{1,0:T(8,128)(2,1)}, u32[]{:S(2)}, u32[]{:S(2)}) collective-permute-start(bf16[192,768]{1,0:T(8,128)(2,1)} %dynamic-slice_bitcast_fusion.13), channel_id=1, source_target_pairs={{0,16},{8,24},{16,0},{24,8},{1,17},{9,25},{17,1},{25,9},{2,18},{10... | collective-permute-start | bytes 884744 | tf_op jit(solution)/shard_map/ppermute | solution.py:564
  383.0 18.1 %collective-permute-start.21 = (bf16[192,768]{1,0:T(8,128)(2,1)}, bf16[192,768]{1,0:T(8,128)(2,1)}, u32[]{:S(2)}, u32[]{:S(2)}) collective-permute-start(bf16[192,768]{1,0:T(8,128)(2,1)} %dynamic-slice_bitcast_fusion.12), channel_id=1, source_target_pairs={{0,16},{8,24},{16,0},{24,8},{1,17},{9,25},{17,1},{25,9},{2,18},{10... | collective-permute-start | bytes 884744 | tf_op jit(solution)/shard_map/ppermute | solution.py:564
  392.9 11.5 %collective-permute-start.42 = (bf16[192,384]{1,0:T(8,128)(2,1)}, bf16[192,384]{1,0:T(8,128)(2,1)}, u32[]{:S(2)}, u32[]{:S(2)}) collective-permute-start(bf16[192,384]{1,0:T(8,128)(2,1)} %bitcast.447), channel_id=1, source_target_pairs={{0,1},{1,0},{2,3},{3,2},{4,5},{5,4},{6,7},{7,6},{8,9},{9,8},{10,11... | collective-permute-start | bytes 442376 | tf_op jit(solution)/shard_map/ppermute | solution.py:554
  395.8 10.9 %collective-permute-start.32 = (bf16[192,384]{1,0:T(8,128)(2,1)}, bf16[192,384]{1,0:T(8,128)(2,1)}, u32[]{:S(2)}, u32[]{:S(2)}) collective-permute-start(bf16[192,384]{1,0:T(8,128)(2,1)} %bitcast.448), channel_id=1, source_target_pairs={{0,1},{1,0},{2,3},{3,2},{4,5},{5,4},{6,7},{7,6},{8,9},{9,8},{10,11... | collective-permute-start | bytes 442376 | tf_op jit(solution)/shard_map/ppermute | solution.py:554
  433.3 35.8 %collective-permute-start.60 = (bf16[2,192,2048]{2,1,0:T(8,128)(2,1)S(1)}, bf16[2,192,2048]{2,1,0:T(8,128)(2,1)S(1)}, u32[]{:S(2)}, u32[]{:S(2)}) collective-permute-start(bf16[2,192,2048]{2,1,0:T(8,128)(2,1)S(1)} %copy-done.23), channel_id=1, source_target_pairs={{0,8},{8,0},{16,24},{24,16},{1,9},{9,1},{17,25},{25,17},{2,10},{10... | collective-permute-start | bytes 4718600 | tf_op jit(solution)/shard_map/ppermute | solution.py:559
  458.0 64.2 %collective-permute-start.17 = (bf16[48,384]{1,0:T(8,128)(2,1)}, bf16[48,384]{1,0:T(8,128)(2,1)S(1)}, u32[]{:S(2)}, u32[]{:S(2)}) collective-permute-start(bf16[48,384]{1,0:T(8,128)(2,1)} %get-tuple-element.49), channel_id=1, source_target_pairs={{0,4},{1,5},{2,6},{3,7},{4,0},{5,1},{6,2},{7,3},{8,12},{9,13},{10,... | collective-permute-start | bytes 110600 | tf_op jit(solution)/shard_map/ppermute | solution.py:549
  461.5 128.4 %collective-permute-start.18 = (bf16[48,384]{1,0:T(8,128)(2,1)}, bf16[48,384]{1,0:T(8,128)(2,1)}, u32[]{:S(2)}, u32[]{:S(2)}) collective-permute-start(bf16[48,384]{1,0:T(8,128)(2,1)} %get-tuple-element.49), channel_id=1, source_target_pairs={{0,6},{1,7},{2,0},{3,1},{4,2},{5,3},{6,4},{7,5},{8,14},{9,15},{10,... | collective-permute-start | bytes 110600 | tf_op jit(solution)/shard_map/ppermute | solution.py:549
  462.5 129.6 %collective-permute-start.49 = (bf16[192,384]{1,0:T(8,128)(2,1)}, bf16[192,384]{1,0:T(8,128)(2,1)}, u32[]{:S(2)}, u32[]{:S(2)}) collective-permute-start(bf16[192,384]{1,0:T(8,128)(2,1)} %bitcast.102), channel_id=1, source_target_pairs={{0,1},{1,0},{2,3},{3,2},{4,5},{5,4},{6,7},{7,6},{8,9},{9,8},{10,11... | collective-permute-start | bytes 442376 | tf_op jit(solution)/shard_map/ppermute | solution.py:554
  465.4 20.5 %collective-permute-start.71 = (bf16[512,768]{0,1:T(8,128)(2,1)S(1)}, bf16[512,768]{0,1:T(8,128)(2,1)S(1)}, u32[]{:S(2)}, u32[]{:S(2)}) collective-permute-start(bf16[512,768]{0,1:T(8,128)(2,1)S(1)} %dynamic-slice_bitcast_fusion.2), channel_id=1, source_target_pairs={{0,16},{8,24},{16,0},{24,8},{1,17},{9,25},{17,1},{25,9},{2,18},{10... | collective-permute-start | bytes 2359304 | tf_op jit(solution)/shard_map/ppermute | solution.py:564
  469.1 33.7 %collective-permute-start.51 = (bf16[192,2048]{1,0:T(8,128)(2,1)S(1)}, bf16[192,2048]{1,0:T(8,128)(2,1)S(1)}, u32[]{:S(2)}, u32[]{:S(2)}) collective-permute-start(bf16[192,2048]{1,0:T(8,128)(2,1)S(1)} %dynamic-slice_bitcast_fusion.4), channel_id=1, source_target_pairs={{0,16},{8,24},{16,0},{24,8},{1,17},{9,25},{17,1},{25,9},{2,18},{10... | collective-permute-start | bytes 2359304 | tf_op jit(solution)/shard_map/ppermute | solution.py:564
  485.9 26.7 %collective-permute-start.61 = (bf16[192,2048]{1,0:T(8,128)(2,1)}, bf16[192,2048]{1,0:T(8,128)(2,1)}, u32[]{:S(2)}, u32[]{:S(2)}) collective-permute-start(bf16[192,2048]{1,0:T(8,128)(2,1)} %dynamic-slice_bitcast_fusion.3), channel_id=1, source_target_pairs={{0,16},{8,24},{16,0},{24,8},{1,17},{9,25},{17,1},{25,9},{2,18},{10... | collective-permute-start | bytes 2359304 | tf_op jit(solution)/shard_map/ppermute | solution.py:564
  502.8 21.4 %collective-permute-start.72 = (bf16[512,384]{0,1:T(8,128)(2,1)}, bf16[512,384]{0,1:T(8,128)(2,1)}, u32[]{:S(2)}, u32[]{:S(2)}) collective-permute-start(bf16[512,384]{0,1:T(8,128)(2,1)} %dynamic-slice_bitcast_fusion.9), channel_id=1, source_target_pairs={{0,1},{1,0},{2,3},{3,2},{4,5},{5,4},{6,7},{7,6},{8,9},{9,8},{10,11... | collective-permute-start | bytes 1179656 | tf_op jit(solution)/shard_map/ppermute | solution.py:554
  552.2 40.6 %collective-permute-start.39 = (bf16[192,384]{1,0:T(8,128)(2,1)}, bf16[192,384]{1,0:T(8,128)(2,1)S(1)}, u32[]{:S(2)}, u32[]{:S(2)}) collective-permute-start(bf16[192,384]{1,0:T(8,128)(2,1)} %bitcast.84), channel_id=1, source_target_pairs={{0,1},{1,0},{2,3},{3,2},{4,5},{5,4},{6,7},{7,6},{8,9},{9,8},{10,11... | collective-permute-start | bytes 442376 | tf_op jit(solution)/shard_map/ppermute | solution.py:554
  586.6 75.1 %collective-permute-start.79 = (bf16[512,384]{1,0:T(8,128)(2,1)}, bf16[512,384]{1,0:T(8,128)(2,1)}, u32[]{:S(2)}, u32[]{:S(2)}) collective-permute-start(bf16[512,384]{1,0:T(8,128)(2,1)} %bitcast.158), channel_id=1, source_target_pairs={{0,1},{1,0},{2,3},{3,2},{4,5},{5,4},{6,7},{7,6},{8,9},{9,8},{10,11... | collective-permute-start | bytes 1179656 | tf_op jit(solution)/shard_map/ppermute | solution.py:554
  589.1 85.9 %collective-permute-start.69 = (bf16[192,1024]{1,0:T(8,128)(2,1)}, bf16[192,1024]{1,0:T(8,128)(2,1)}, u32[]{:S(2)}, u32[]{:S(2)}) collective-permute-start(bf16[192,1024]{1,0:T(8,128)(2,1)} %bitcast.138), channel_id=1, source_target_pairs={{0,1},{1,0},{2,3},{3,2},{4,5},{5,4},{6,7},{7,6},{8,9},{9,8},{10,11... | collective-permute-start | bytes 1179656 | tf_op jit(solution)/shard_map/ppermute | solution.py:554
  589.9 93.4 %collective-permute-start.59 = (bf16[192,1024]{1,0:T(8,128)(2,1)S(1)}, bf16[192,1024]{1,0:T(8,128)(2,1)}, u32[]{:S(2)}, u32[]{:S(2)}) collective-permute-start(bf16[192,1024]{1,0:T(8,128)(2,1)S(1)} %bitcast.465), channel_id=1, source_target_pairs={{0,1},{1,0},{2,3},{3,2},{4,5},{5,4},{6,7},{7,6},{8,9},{9,8},{10,11... | collective-permute-start | bytes 1179656 | tf_op jit(solution)/shard_map/ppermute | solution.py:554
  592.1 33.7 %collective-permute-start.29 = (bf16[192,384]{1,0:T(8,128)(2,1)S(1)}, bf16[192,384]{1,0:T(8,128)(2,1)S(1)}, u32[]{:S(2)}, u32[]{:S(2)}) collective-permute-start(bf16[192,384]{1,0:T(8,128)(2,1)S(1)} %bitcast.483), channel_id=1, source_target_pairs={{0,1},{1,0},{2,3},{3,2},{4,5},{5,4},{6,7},{7,6},{8,9},{9,8},{10,11... | collective-permute-start | bytes 442376 | tf_op jit(solution)/shard_map/ppermute | solution.py:554
  592.9 38.0 %collective-permute-start.19 = (bf16[192,384]{1,0:T(8,128)(2,1)S(1)}, bf16[192,384]{1,0:T(8,128)(2,1)S(1)}, u32[]{:S(2)}, u32[]{:S(2)}) collective-permute-start(bf16[192,384]{1,0:T(8,128)(2,1)S(1)} %bitcast.485), channel_id=1, source_target_pairs={{0,1},{1,0},{2,3},{3,2},{4,5},{5,4},{6,7},{7,6},{8,9},{9,8},{10,11... | collective-permute-start | bytes 442376 | tf_op jit(solution)/shard_map/ppermute | solution.py:554
  (111 other events, 1366.9 us)

commit v3 on v2

--- a/solution.py
+++ b/solution.py
@@ -16,6 +16,7 @@
 BLK = 256
 AUG = DH + 16
 SPAN = 4 * BLK
+LANES = 256
 LOG2E = 1.4426950408889634
 LN2 = 0.6931471805599453
 F32 = jnp.float32
@@ -535,71 +536,286 @@
     )(lengths, far, tiles, own, pair, out, lse, dout)
 
 
+def rows_of(shape, dp):
+    return shape[0] // dp * (shape[1] // LANES)
+
+
 class Places:
     def __init__(self, mesh):
         self.dp = mesh.shape["dp"]
-        self.seq = mesh.shape["seq"]
-        self.inner = self.seq // OUTER
-        self.cores = 2
-        self.groups = self.dp // self.cores
-
-    def shift_outer(self, value, d):
-        n = self.inner
-        pairs = [(o * n + i, (o + d) % OUTER * n + i) for o in range(OUTER) for i in range(n)]
-        return lax.ppermute(value, "seq", pairs)
-
-    def shift_inner(self, value, d):
-        n = self.inner
-        pairs = [(o * n + i, o * n + (i + d) % n) for o in range(OUTER) for i in range(n)]
-        return lax.ppermute(value, "seq", pairs)
-
-    def shift_core(self, value, d):
-        c = self.cores
-        pairs = [(g * c + i, g * c + (i + d) % c) for g in range(self.groups) for i in range(c)]
-        return lax.ppermute(value, "dp", pairs)
-
-    def shift_group(self, value, d):
-        c, g = self.cores, self.groups
-        pairs = [(o * c + i, (o + d) % g * c + i) for o in range(g) for i in range(c)]
-        return lax.ppermute(value, "dp", pairs)
-
-
-def scatter_sum(pieces, at, size, axis, shift):
-    total = pieces(at).astype(F32)
-    for d in range(1, size):
-        part = pieces(lax.rem(at + d, size))
-        total = total + shift(part, d).astype(F32)
-    return total
-
-
-def pick(value, index, axis):
-    return lax.dynamic_index_in_dim(value, index, axis, keepdims=False)
-
-
-def reduce_grad(places, grad, kind):
-    rows, columns = grad.shape
-    c, g, n = places.cores, places.groups, places.inner
-    share = rows // places.dp
-    dp, seq = lax.axis_index("dp"), lax.axis_index("seq")
-    parts = grad.astype(kind).reshape(g, c, share, columns)
-    held = scatter_sum(lambda i: pick(parts, i, 1), lax.rem(dp, c), c, 1, places.shift_core).astype(kind)
-    held = scatter_sum(lambda i: pick(held, i, 0), dp // c, g, 0, places.shift_group).astype(kind)
-    wide = columns // n
-    slabs = held.reshape(share, n, wide)
-    held = scatter_sum(lambda i: pick(slabs, i, 1), lax.rem(seq, n), n, 1, places.shift_inner).astype(kind)
-    lines = held.reshape(OUTER, share // OUTER, wide)
-    z, x = seq // n, lax.rem(seq, n)
-    held = scatter_sum(lambda i: pick(lines, i, 0), z, OUTER, 0, places.shift_outer).astype(kind)
-    full = jnp.zeros((OUTER, share // OUTER, wide), kind)
-    full = lax.dynamic_update_index_in_dim(full, held, z, 0)
-    for d in range(1, OUTER):
-        full = lax.dynamic_update_index_in_dim(full, places.shift_outer(held, d), lax.rem(z + OUTER - d, OUTER), 0)
-    full = full.reshape(share, wide)
-    result = jnp.zeros((share, n, wide), kind)
-    result = lax.dynamic_update_index_in_dim(result, full, x, 1)
-    for d in range(1, n):
-        result = lax.dynamic_update_index_in_dim(result, places.shift_inner(full, d), lax.rem(x + n - d, n), 1)
-    return result.reshape(share, columns).astype(F32)
+        self.groups = self.dp // 2
+        self.inner = mesh.shape["seq"] // OUTER
+
+
+class Sum:
+    def __init__(self, places, shapes):
+        self.p = places
+        self.shapes = shapes
+        self.grain = places.inner * OUTER * 16
+        used = sum(rows_of(s, places.dp) for s in shapes)
+        self.total = -(-used // (2 * self.grain)) * 2 * self.grain
+        half = self.total // 2
+        self.lines = [(0, half, True), (half, half, False)]
+        self.starts = []
+        at = 0
+        for s in shapes:
+            self.starts.append(at)
+            at += rows_of(s, places.dp)
+        self.used = at
+
+    def scratch(self):
+        p, dma = self.p, pltpu.SemaphoreType.DMA
+        g, n, half = p.groups, p.inner, self.total // 2
+        out = [pltpu.VMEM((2, g, s[0] // p.dp, s[1]), BF16) for s in self.shapes]
+        out += [
+            pltpu.VMEM((g, self.total, LANES), BF16),
+            pltpu.VMEM((g - 1, half, LANES), BF16),
+            pltpu.VMEM((g - 1, half // n, LANES), BF16),
+            pltpu.VMEM((n - 1, half // n, LANES), BF16),
+            pltpu.VMEM((n - 1, g, half // n, LANES), BF16),
+            pltpu.VMEM((2, OUTER - 1, half // n // OUTER, LANES), BF16),
+            dma((len(self.shapes), g, 3)),
+            dma((2, g - 1, 2)),
+            dma((2, n - 1, g, 2)),
+            dma((2, OUTER - 1, 2)),
+            dma((2, OUTER - 1, 2)),
+            dma((2, OUTER, n - 1, 2)),
+        ]
+        return out
+
+    def bind(self, grads, full, refs):
+        count = len(self.shapes)
+        self.grads, self.full = grads, full
+        self.land = refs[:count]
+        (self.held, self.y_first, self.y_second, self.x_second, self.x_first, self.z_land,
+         self.c_sem, self.y_sem, self.x_sem, self.z_sem, self.az_sem, self.ax_sem) = refs[count:]
+        dp, seq = lax.axis_index("dp"), lax.axis_index("seq")
+        n = self.p.inner
+        self.core, self.group = lax.rem(dp, 2), lax.div(dp, 2)
+        self.z, self.x = lax.div(seq, n), lax.rem(seq, n)
+        return self
+
+    def copy(self, src, dst, sems, **peer):
+        return pltpu.make_async_remote_copy(
+            src_ref=src, dst_ref=dst, send_sem=sems[0], recv_sem=sems[1],
+            device_id=peer, device_id_type=pl.DeviceIdType.MESH,
+        )
+
+    def core_copies(self):
+        out = []
+        for m, shape in enumerate(self.shapes):
+            share = shape[0] // self.p.dp
+            for g in range(self.p.groups):
+                first = pl.multiple_of((g * 2 + 1 - self.core) * share, 16)
+                sems = self.c_sem.at[m, g, 0], self.c_sem.at[m, g, 1]
+                peer = self.group * 2 + 1 - self.core
+                out.append(self.copy(self.grads[m].at[pl.ds(first, share)], self.land[m].at[0, g], sems, dp=peer))
+        return out
+
+    def own_copies(self):
+        out = []
+        for m, shape in enumerate(self.shapes):
+            share = shape[0] // self.p.dp
+            for g in range(self.p.groups):
+                first = pl.multiple_of((g * 2 + self.core) * share, 16)
+                out.append(
+                    pltpu.make_async_copy(
+                        self.grads[m].at[pl.ds(first, share)], self.land[m].at[1, g], self.c_sem.at[m, g, 2]
+                    )
+                )
+        return out
+
+    def part(self, line, x):
+        first, rows, _ = self.lines[line]
+        size = rows // self.p.inner
+        return pl.ds(pl.multiple_of(first + x * size, 16), size)
+
+    def quarter(self, line, x, z):
+        first, rows, _ = self.lines[line]
+        size = rows // self.p.inner
+        small = size // OUTER
+        return pl.ds(pl.multiple_of(first + x * size + z * small, 16), small)
+
+    def y_copies(self, line):
+        first, rows, y_first = self.lines[line]
+        out = []
+        for t in range(1, self.p.groups):
+            other = lax.rem(self.group + t, self.p.groups)
+            where = pl.ds(first, rows) if y_first else self.part(line, self.x)
+            land = self.y_first if y_first else self.y_second
+            sems = self.y_sem.at[line, t - 1, 0], self.y_sem.at[line, t - 1, 1]
+            out.append(self.copy(self.held.at[other, where], land.at[t - 1], sems, dp=other * 2 + self.core))
+        return out
+
+    def x_copies(self, line):
+        first, rows, y_first = self.lines[line]
+        n, out = self.p.inner, []
+        for s in range(1, n):
+            other = lax.rem(self.x + s, n)
+            where = self.part(line, other)
+            for g in range(1 if y_first else self.p.groups):
+                sems = self.x_sem.at[line, s - 1, g, 0], self.x_sem.at[line, s - 1, g, 1]
+                if y_first:
+                    src, dst = self.held.at[self.group, where], self.x_second.at[s - 1]
+                else:
+                    src, dst = self.held.at[g, where], self.x_first.at[s - 1, g]
+                out.append(self.copy(src, dst, sems, seq=self.z * n + other))
+        return out
+
+    def z_copies(self, line):
+        out = []
+        for d in (2, 1, 3):
+            other = lax.rem(self.z + d, OUTER)
+            sems = self.z_sem.at[line, d - 1, 0], self.z_sem.at[line, d - 1, 1]
+            src = self.held.at[self.group, self.quarter(line, self.x, other)]
+            out.append(self.copy(src, self.z_land.at[line, d - 1], sems, seq=other * self.p.inner + self.x))
+        return out
+
+    def az_copies(self, line, steps=(1, 2, 3)):
+        out = []
+        for d in steps:
+            other = lax.rem(self.z + d, OUTER)
+            sems = self.az_sem.at[line, d - 1, 0], self.az_sem.at[line, d - 1, 1]
+            where = self.quarter(line, self.x, self.z)
+            out.append(self.copy(self.full.at[where], self.full.at[where], sems, seq=other * self.p.inner + self.x))
+        return out
+
+    def ax_copies(self, line, d):
+        n, out = self.p.inner, []
+        where = self.quarter(line, self.x, lax.rem(self.z + OUTER - d, OUTER))
+        for s in range(1, n):
+            other = lax.rem(self.x + s, n)
+            sems = self.ax_sem.at[line, d, s - 1, 0], self.ax_sem.at[line, d, s - 1, 1]
+            out.append(self.copy(self.full.at[where], self.full.at[where], sems, seq=self.z * n + other))
+        return out
+
+
+    def step_core(self):
+        for c in self.core_copies() + self.own_copies():
+            c.start()
+
+    def step_first(self):
+        for c in self.core_copies():
+            c.wait_recv()
+        for c in self.own_copies():
+            c.wait()
+        for m, shape in enumerate(self.shapes):
+            share = shape[0] // self.p.dp
+            for g in range(self.p.groups):
+                for block in range(shape[1] // LANES):
+                    columns = slice(block * LANES, (block + 1) * LANES)
+                    first = self.starts[m] + block * share
+                    total = self.land[m][0, g, :, columns].astype(F32) + self.land[m][1, g, :, columns].astype(F32)
+                    self.held[g, first : first + share] = total.astype(BF16)
+        if self.used < self.total:
+            blank = jnp.zeros((self.p.groups, self.total - self.used, LANES), BF16)
+            self.held[:, self.used :] = blank
+        for c in self.y_copies(0) + self.x_copies(1):
+            c.start()
+
+    def add(self, g, where, arrived):
+        total = self.held[g, where].astype(F32)
+        for a in arrived:
+            total = total + a.astype(F32)
+        self.held[g, where] = total.astype(BF16)
+
+    def step_second(self):
+        for c in self.y_copies(0) + self.x_copies(1):
+            c.wait_recv()
+        first, rows, _ = self.lines[0]
+        self.add(self.group, pl.ds(first, rows), [self.y_first[t] for t in range(self.p.groups - 1)])
+        for g in range(self.p.groups):
+            self.add(g, self.part(1, self.x), [self.x_first[s, g] for s in range(self.p.inner - 1)])
+        for c in self.x_copies(0) + self.y_copies(1):
+            c.start()
+
+    def step_z(self):
+        for c in self.x_copies(0) + self.y_copies(1):
+            c.wait_recv()
+        self.add(self.group, self.part(0, self.x), [self.x_second[s] for s in range(self.p.inner - 1)])
+        self.add(self.group, self.part(1, self.x), [self.y_second[t] for t in range(self.p.groups - 1)])
+        for line in range(2):
+            for c in self.z_copies(line):
+                c.start()
+
+    def step_gather(self):
+        for line in range(2):
+            for c in self.z_copies(line):
+                c.wait_recv()
+            where = self.quarter(line, self.x, self.z)
+            total = self.held[self.group, where].astype(F32)
+            for d in range(OUTER - 1):
+                total = total + self.z_land[line, d].astype(F32)
+            self.full[where] = total.astype(BF16)
+            for c in self.az_copies(line) + self.ax_copies(line, 0):
+                c.start()
+
+    def step_forward(self):
+        for d in (1, 3, 2):
+            for line in range(2):
+                self.az_copies(line, (d,))[0].wait_recv()
+                for c in self.ax_copies(line, d):
+                    c.start()
+
+    def step_end(self):
+        for line in range(2):
+            for d in range(OUTER):
+                for c in self.ax_copies(line, d):
+                    c.wait()
+            for c in self.az_copies(line) + self.z_copies(line) + self.y_copies(line) + self.x_copies(line):
+                c.wait_send()
+        for c in self.core_copies():
+            c.wait_send()
+
+    def unpack(self, outs):
+        for m, shape in enumerate(self.shapes):
+            share = shape[0] // self.p.dp
+            for block in range(shape[1] // LANES):
+                first = self.starts[m] + block * share
+                outs[m][:, block * LANES : (block + 1) * LANES] = self.full[first : first + share].astype(F32)
+
+    def greet(self):
+        p = self.p
+        barrier = pltpu.get_barrier_semaphore()
+        mesh = pl.DeviceIdType.MESH
+        pl.semaphore_signal(barrier, inc=1, device_id={"dp": self.group * 2 + 1 - self.core}, device_id_type=mesh)
+        for t in range(1, p.groups):
+            other = lax.rem(self.group + t, p.groups) * 2 + self.core
+            pl.semaphore_signal(barrier, inc=1, device_id={"dp": other}, device_id_type=mesh)
+        for peer in peers(p.inner, self.z, self.x):
+            pl.semaphore_signal(barrier, inc=1, device_id={"seq": peer}, device_id_type=mesh)
+        pl.semaphore_wait(barrier, 1 + p.groups - 1 + OUTER - 1 + p.inner - 1)
+
+
+def sum_kernel(job, *refs):
+    count = len(job.shapes)
+    grads, outs, refs = refs[:count], refs[count : 2 * count], refs[2 * count :]
+    job.bind(grads, refs[0], refs[1:])
+    job.greet()
+    job.step_core()
+    job.step_first()
+    job.step_second()
+    job.step_z()
+    job.step_gather()
+    job.step_forward()
+    job.step_end()
+    job.unpack(outs)
+
+
+def sum_grads(places, grads, collective_id):
+    job = Sum(places, [g.shape for g in grads])
+    count = len(grads)
+    return pl.pallas_call(
+        functools.partial(sum_kernel, job),
+        in_specs=[pl.BlockSpec(memory_space=pl.ANY)] * count,
+        out_specs=[whole()] * count,
+        out_shape=[jax.ShapeDtypeStruct((g.shape[0] // places.dp, g.shape[1]), F32) for g in grads],
+        scratch_shapes=[pltpu.VMEM((job.total, LANES), BF16)] + job.scratch(),
+        compiler_params=pltpu.CompilerParams(
+            vmem_limit_bytes=VMEM_BYTES, collective_id=collective_id, has_side_effects=True
+        ),
+        name="sum_grads",
+    )(*grads)
 
 
 def shards(
@@ -658,19 +874,11 @@
     grad_w_out = jnp.einsum("bes,bsd->ed", attended_t, grad_mixed_low, preferred_element_type=F32)
     grad_attended_t = jnp.einsum("bsd,ed->bes", grad_mixed_low, w_out, preferred_element_type=F32).astype(BF16)
 
-    part_gate = reduce_grad(places, grad_w_gate, BF16)
-    part_up = reduce_grad(places, grad_w_up, BF16)
-    part_down = reduce_grad(places, grad_down, BF16)
-    part_out = reduce_grad(places, grad_w_out, BF16)
-
     grads, near, far_sum = attention_backward(n, lengths, far, tiles, own, pair, out, lse, grad_attended_t)
     grad_q, grad_k, grad_v = grads[0], grads[1], grads[2]
     grad_w_query = jnp.einsum("bsd,bes->de", normed, grad_q, preferred_element_type=F32)
     grad_w_key = jnp.einsum("bsd,bes->de", normed, grad_k, preferred_element_type=F32)
     grad_w_value = jnp.einsum("bsd,bes->de", normed, grad_v, preferred_element_type=F32)
-    part_query = reduce_grad(places, grad_w_query, BF16)
-    part_key = reduce_grad(places, grad_w_key, BF16)
-    part_value = reduce_grad(places, grad_w_value, BF16)
     grad_normed = (
         jnp.einsum("bes,de->bsd", grad_q, w_query, preferred_element_type=F32)
         + jnp.einsum("bes,de->bsd", grad_k, w_key, preferred_element_type=F32)
@@ -696,8 +904,10 @@
         axis=1,
     )
     used = small.shape[1]
-    small = jnp.pad(small, ((0, 0), (0, 32 * 128 - used))).reshape(places.dp * 32, 128)
-    small = reduce_grad(places, small, F32).reshape(-1)
+    small = jnp.pad(small, ((0, 0), (0, 16 * LANES - used))).reshape(places.dp * 16, LANES)
+    wide = [g.astype(BF16) for g in (grad_w_query, grad_w_key, grad_w_value, grad_w_out, grad_w_gate, grad_w_up, grad_down, small)]
+    part_query, part_key, part_value, part_out, part_gate, part_up, part_down, small = sum_grads(places, wide, 2)
+    small = small.reshape(-1)
     share = width // places.dp
     return (
         result,

time: 711 us -> 526 us (0.74)
  the two profiles are of different devices: /device:TPU:0 before, /device:TPU:18 now
where the time goes in v3:
time: 526 us; the launch traced here: 518 us
  Pallas kernels  423 us (80%)
  matrix products  66 us (13%)
  local copies, waits for them, and re-layouts  19.7 us (4%)
  other arithmetic  7.41 us (1%)
    pallas_call x1, Pallas kernels, sum_grads(): pl.pallas_call(functools.partial(sum_kernel, job), in_specs=[pl.BlockSpec...  186 us
    pallas_call x1, Pallas kernels, attention_forward(): pl.pallas_call(functools.partial(forward_kernel, n), in_specs=[smem()] *...  115 us
    pallas_call x1, Pallas kernels, attention_backward(): pl.pallas_call(functools.partial(backward_kernel, n), in_specs=[smem()] *...  114 us
    unnamed x92, local copies, waits for them, and re-layouts  15.3 us
    dot_general x1, matrix products, shards(): jnp.einsum('bsd,de->bse', normed_ffn, w_gate, preferred_element_type=F32)  11.7 us

profile of v3, /device:TPU:18, one launch (start us, length us, event | category | flops | bytes accessed | tf_op | source)
XLA Modules:
  0.0 517.7 jit_solution(17937812678568418250)
XLA Ops:
  2.8 3.3 bias_tiles.1.tile_ref
  7.5 115.0 %attention_forward.1 = (bf16[3,256,768]{2,1,0:T(8,128)(2,1)}, bf16[9,4,192,256]{3,2,1,0:T(8,128)(2,1)}, bf16[1,9,4,128,256]{4,3,2,1,0:T(8,128)(2,1)}, bf16[3,768...) custom-call(s32[3]{0:T(128)} %len_ref.3, f32[3,3]{1,0:T(4,128)} %pad_maximum_fusion.far_ref, ...), custom_call_target="tpu_custom_call" | custom-call | flops 44999999488 | bytes 25165824 | tf_op jit(solution)/shard_map/attention_forward/pallas_call | solution.py:303
  122.5 2.5 multiply_reduce_fusion.5
  125.3 2.4 copy-done.30
  127.8 4.5 fusion.13
  132.4 4.5 fusion.7
  136.9 11.7 %fusion.6 = (bf16[3,256,2048]{2,1,0:T(8,128)(2,1)S(1)}, bf16[3,256,2048]{2,1,0:T(8,128)(2,1)S(1)}, bf16[3,256,2048]{2,1,0:T(8,128)(2,1)}) fusion(f32[3,256,2048]{2,1,0:T(8,128)} %fusion.7, f32[3,256,2048]{2,1,0:T(8,128)} %fusion.13, bf16[3,256,768]{2,1,0:T(8,128)(2,1)S(1)} %multiply_convert_fusion.2, bf16[768,2048]{1,0:T(8,128)(2,1)S(1)} %copy-done), kind=kOutput, calls=%fused_computation.8 | convolution fusion | flops 2456813568 | bytes 26345472 | tf_op jit(solution)/shard_map/bsd,de->bse/dot_general | solution.py:854
  148.6 2.6 fusion.11
  151.3 3.0 multiply_reduce_fusion
  154.9 2.1 fusion.27.dout
  157.1 114.1 %attention_backward.1 = (bf16[3,3,768,256]{3,2,1,0:T(8,128)(2,1)}, f32[3,5,256,256]{3,2,1,0:T(8,128)}, f32[3,8,256]{2,1,0:T(8,128)}) custom-call(s32[3]{0:T(128)} %len_ref.3, f32[3,3]{1,0:T(4,128)} %pad_maximum_fusion.far_ref, f32[3,5,256,256]{3,2,1,0:T(8,128)} %bias_tiles.1.tile_ref, bf16[9,4,192,256]{3,2,1,0:T(8,128)(2,1)} %get-tuple-element.30.own, ...), custom_call_target="tpu_custom_call" | custom-call | flops 109999996928 | bytes 25165824 | tf_op jit(solution)/shard_map/attention_backward/pallas_call | solution.py:502
  271.2 5.2 %diagonal_sums.1 = f32[3,1,1024]{2,1,0:T(1,128)} custom-call(f32[3,5,256,256]{3,2,1,0:T(8,128)} %get-tuple-element.36.near_ref), custom_call_target="tpu_custom_call" | custom-call | tf_op jit(solution)/shard_map/diagonal_sums/pallas_call | solution.py:113
  278.5 2.5 fusion.31
  284.1 3.0 multiply_reduce_fusion.1
  288.0 3.9 bitcast_convert_fusion.4.refs_2_
  291.9 2.1 bitcast_convert_fusion.5.refs_1_
  294.1 2.1 bitcast_convert_fusion.6.refs_0_
  296.7 4.1 bitcast_convert_fusion.1.refs_5_
  300.8 4.0 bitcast_convert_fusion.2.refs_4_
  304.8 2.1 bitcast_convert_fusion.3.refs_3_
  307.9 4.3 bitcast_convert_fusion.refs_6_
  312.2 185.7 %sum_grads.1 = (f32[192,768]{1,0:T(8,128)}, f32[192,768]{1,0:T(8,128)}, f32[192,768]{1,0:T(8,128)}, f32[192,768]{1,0:T(8,128)}, f32[192,2048]{1,0:T(8,128)}, /*i...) custom-call(bf16[768,768]{1,0:T(8,128)(2,1)} %bitcast_convert_fusion.6.refs_0_, ...), custom_call_target="tpu_custom_call" | custom-call | tf_op jit(solution)/shard_map/sum_grads/pallas_call | solution.py:808
  499.9 4.5 fusion.20
  505.7 4.0 fusion.24
  (122 shorter events, 22.8 us)
Async XLA Ops:
  0.6 136.2 %copy-start = (bf16[768,2048]{1,0:T(8,128)(2,1)S(1)}, bf16[768,2048]{1,0:T(8,128)(2,1)}, u32[]{:S(2)}) copy-start(bf16[768,2048]{1,0:T(8,128)(2,1)} %param.21) | copy-start | bytes 9437188
  0.7 6.2 %copy-start.24 = (f32[768]{0:T(1024)S(1)}, f32[768]{0:T(1024)}, u32[]{:S(2)}) copy-start(f32[768]{0:T(1024)} %param.15) | copy-start | bytes 9220
  1.7 4.4 copy-start.28
  7.5 115.0 %copy-start.2 = (f32[3,256,768]{2,1,0:T(8,128)S(1)}, f32[3,256,768]{2,1,0:T(8,128)}, u32[]{:S(2)}) copy-start(f32[3,256,768]{2,1,0:T(8,128)} %x_ref.1) | copy-start | bytes 7077892
  7.5 115.0 %copy-start.15 = (bf16[768,768]{1,0:T(8,128)(2,1)S(1)}, bf16[768,768]{1,0:T(8,128)(2,1)}, u32[]{:S(2)}) copy-start(bf16[768,768]{1,0:T(8,128)(2,1)} %param.19) | copy-start | bytes 3538948
  125.0 29.3 %copy-start.4 = (f32[3,256,768]{2,1,0:T(8,128)}, f32[3,256,768]{2,1,0:T(8,128)S(1)}, u32[]{:S(2)}) copy-start(f32[3,256,768]{2,1,0:T(8,128)S(1)} %get-tuple-element.62) | copy-start | bytes 7077892
  127.8 9.1 %copy-start.13 = (bf16[3,256,768]{2,1,0:T(8,128)(2,1)}, bf16[3,256,768]{2,1,0:T(8,128)(2,1)S(1)}, u32[]{:S(2)}) copy-start(bf16[3,256,768]{2,1,0:T(8,128)(2,1)S(1)} %multiply_convert_fusion.2) | copy-start | bytes 3538948
  127.8 4.5 copy-start.8
  127.8 4.6 copy-start.31
  271.2 5.3 %copy-start.26 = (f32[3,8,256]{2,1,0:T(8,128)S(1)}, f32[3,8,256]{2,1,0:T(8,128)}, u32[]{:S(2)}) copy-start(f32[3,8,256]{2,1,0:T(8,128)} %get-tuple-element.37) | copy-start | bytes 73732
  271.2 5.5 %copy-start.29 = (s32[1024]{0:T(1024)S(1)}, s32[1024]{0:T(1024)}, u32[]{:S(2)}) copy-start(s32[1024]{0:T(1024)} %copy-done.28) | copy-start | bytes 12292
  271.2 7.3 %copy-start.33 = (bf16[768,768]{1,0:T(8,128)(2,1)S(1)}, bf16[768,768]{1,0:T(8,128)(2,1)}, u32[]{:S(2)}) copy-start(bf16[768,768]{1,0:T(8,128)(2,1)} %wk_ref.1) | copy-start | bytes 3538948
  288.0 3.9 copy-start.23
  288.0 3.9 copy-start.37
  296.7 4.1 copy-start.36
  300.8 4.1 copy-start.7
  300.8 4.1 copy-start.17
  499.9 4.5 copy-start.5
  499.9 4.5 copy-start.32
  499.9 5.8 %copy-start.39 = (bf16[3,256,2048]{2,1,0:T(8,128)(2,1)S(1)}, bf16[3,256,2048]{2,1,0:T(8,128)(2,1)}, u32[]{:S(2)}) copy-start(bf16[3,256,2048]{2,1,0:T(8,128)(2,1)} %get-tuple-element.56) | copy-start | bytes 9437188
  505.7 4.0 copy-start.21
  505.7 4.8 copy-start.20
  505.7 5.7 %copy-start.19 = (f32[192,768]{1,0:T(8,128)S(1)}, f32[192,768]{1,0:T(8,128)}, u32[]{:S(2)}) copy-start(f32[192,768]{1,0:T(8,128)} %get-tuple-element.85) | copy-start | bytes 1769476
  509.7 3.3 copy-start.12
  (18 other events, 41.7 us)

commit v4 on v2

v4 whole, which is shorter than its diff:
```python
import functools

import jax
import jax.numpy as jnp
import numpy as np
from jax import lax
from jax.experimental import pallas as pl
from jax.experimental.pallas import tpu as pltpu
from jax.sharding import PartitionSpec as P

H = 12
DH = 64
NB = 32
OUTER = 4
HEADS = H // OUTER
HW = HEADS * DH
BLK = 256
AUG = DH + 16
SPAN = 4 * BLK
LANES = 256
LOG2E = 1.4426950408889634
LN2 = 0.6931471805599453
F32 = jnp.float32
BF16 = jnp.bfloat16
NT = (((1,), (1,)), ((), ()))
VMEM_BYTES = 62 << 20
GROUP = 8
TILES = 4

epsilon = 1e-06
limits = (1, 2, 3, 4, 5, 6, 7, 8, 12, 16, 23, 32, 46, 64, 91)
highest = lax.Precision.HIGHEST


def bucket_lines():
    relative = 2 * BLK - 1 - np.arange(SPAN)
    count = sum((np.abs(relative) >= limit).astype(np.int32) for limit in limits)
    bucket = count + (relative > 0).astype(np.int32) * (NB // 2)
    return (bucket[None, :] == np.arange(NB)[:, None]).astype(np.float32)


ONEHOT = bucket_lines()


def params():
    return pltpu.CompilerParams(vmem_limit_bytes=VMEM_BYTES)


def smem():
    return pl.BlockSpec(memory_space=pltpu.SMEM)


def anywhere():
    return pl.BlockSpec(memory_space=pl.ANY)


def whole():
    return pl.BlockSpec(memory_space=pltpu.VMEM)


def split3(v):
    a = v.astype(BF16)
    r = v - a.astype(F32)
    b = r.astype(BF16)
    c = (r - b.astype(F32)).astype(BF16)
    return a.astype(F32), b.astype(F32), c.astype(F32)


def tail(width, values):
    row = lax.broadcasted_iota(jnp.int32, (16, width), 0)
    out = jnp.zeros((16, width), F32)
    for i, v in enumerate(values):
        out = jnp.where(row == i, v, out)
    return out


def peers(n, z, x):
    return [lax.rem(z + d, OUTER) * n + x for d in range(1, OUTER)] + [z * n + lax.rem(x + s, n) for s in range(1, n)]


class Places:
    def __init__(self, mesh):
        self.dp = mesh.shape["dp"]
        self.groups = self.dp // 2
        self.inner = mesh.shape["seq"] // OUTER


def remote(src, dst, sems, **peer):
    return pltpu.make_async_remote_copy(
        src_ref=src,
        dst_ref=dst,
        send_sem=sems[0],
        recv_sem=sems[1],
        device_id=peer,
        device_id_type=pl.DeviceIdType.MESH,
    )


class Rows:
    def __init__(self, places, shapes):
        self.p = places
        self.shapes = shapes
        grain = places.inner * OUTER * 16
        self.blocks = []
        at = 0
        for m, (rows, columns) in enumerate(shapes):
            share = rows // places.dp
            for block in range(columns // LANES):
                self.blocks.append((m, block, at, share))
                at += share
        self.used = at
        self.total = -(-at // (2 * grain)) * 2 * grain
        self.half = self.total // 2
        self.size = self.half // places.inner
        self.small = self.size // OUTER

    def part(self, line, x):
        return pl.ds(pl.multiple_of(line * self.half + x * self.size, 16), self.size)

    def quarter(self, line, x, z):
        return pl.ds(pl.multiple_of(line * self.half + x * self.size + z * self.small, 16), self.small)


def add_to(ref, arrived):
    if len(arrived) == 1:
        ref[...] = ref[...] + arrived[0]
        return
    total = ref[...].astype(F32)
    for a in arrived:
        total = total + a.astype(F32)
    ref[...] = total.astype(BF16)


class Scatter:
    def __init__(self, rows, y_first):
        self.rows = rows
        self.y_first = y_first

    def scratch(self):
        r, p, dma = self.rows, self.rows.p, pltpu.SemaphoreType.DMA
        g, n = p.groups, p.inner
        out = [pltpu.VMEM((g, r.total, LANES), BF16), pltpu.VMEM((g, r.total, LANES), BF16)]
        for y_first in self.y_first:
            out.append(pltpu.VMEM((g - 1, r.half if y_first else r.size, LANES), BF16))
            out.append(pltpu.VMEM((n - 1, 1 if y_first else g, r.size, LANES), BF16))
        return out + [dma((len(r.blocks), g, 3)), dma((2, g - 1, 2)), dma((2, n - 1, g, 2))]

    count = 9

    def bind(self, grads, refs):
        self.grads = grads
        self.held, self.land, self.c_sem, self.y_sem, self.x_sem = refs[0], refs[1], refs[6], refs[7], refs[8]
        self.y_land, self.x_land = (refs[2], refs[4]), (refs[3], refs[5])
        dp, seq = lax.axis_index("dp"), lax.axis_index("seq")
        n = self.rows.p.inner
        self.core, self.group = lax.rem(dp, 2), lax.div(dp, 2)
        self.z, self.x = lax.div(seq, n), lax.rem(seq, n)

    def source(self, i, g, core):
        m, block, at, share = self.rows.blocks[i]
        first = pl.multiple_of((g * 2 + core) * share, 16)
        return self.grads[m].at[pl.ds(first, share), pl.ds(block * LANES, LANES)], pl.ds(at, share)

    def picked(self, chosen):
        return [i for i, b in enumerate(self.rows.blocks) if chosen is None or b[0] in chosen]

    def core_copies(self, chosen=None):
        for i in self.picked(chosen):
            for g in range(self.rows.p.groups):
                src, where = self.source(i, g, 1 - self.core)
                sems = self.c_sem.at[i, g, 0], self.c_sem.at[i, g, 1]
                yield remote(src, self.land.at[g, where], sems, dp=self.group * 2 + 1 - self.core)

    def own_copies(self, chosen=None):
        for i in self.picked(chosen):
            for g in range(self.rows.p.groups):
                src, where = self.source(i, g, self.core)
                yield pltpu.make_async_copy(src, self.held.at[g, where], self.c_sem.at[i, g, 2])

    def y_copies(self, line):
        r = self.rows
        for t in range(1, r.p.groups):
            other = lax.rem(self.group + t, r.p.groups)
            where = pl.ds(line * r.half, r.half) if self.y_first[line] else r.part(line, self.x)
            sems = self.y_sem.at[line, t - 1, 0], self.y_sem.at[line, t - 1, 1]
            yield remote(self.held.at[other, where], self.y_land[line].at[t - 1], sems, dp=other * 2 + self.core)

    def x_copies(self, line):
        r = self.rows
        n = r.p.inner
        for s in range(1, n):
            other = lax.rem(self.x + s, n)
            where = r.part(line, other)
            for g in range(1 if self.y_first[line] else r.p.groups):
                sems = self.x_sem.at[line, s - 1, g, 0], self.x_sem.at[line, s - 1, g, 1]
                src = self.held.at[self.group if self.y_first[line] else g, where]
                yield remote(src, self.x_land[line].at[s - 1, g], sems, seq=self.z * n + other)

    def hop(self, line, which):
        return self.y_copies(line) if (which == 0) == self.y_first[line] else self.x_copies(line)


    def step_core(self, chosen=None):
        for c in self.core_copies(chosen):
            c.start()
        for c in self.own_copies(chosen):
            c.start()

    def step_first(self):
        r = self.rows
        for c in self.core_copies():
            c.wait_recv()
        for c in self.own_copies():
            c.wait()
        for line in range(2):
            for g in range(r.p.groups):
                first, last = line * r.half, min((line + 1) * r.half, r.used)
                where = pl.ds(first, last - first)
                add_to(self.held.at[g, where], [self.land[g, where]])
                if last < (line + 1) * r.half:
                    self.held[g, last : (line + 1) * r.half] = jnp.zeros(((line + 1) * r.half - last, LANES), BF16)
            for c in self.hop(line, 0):
                c.start()

    def step_second(self, line):
        r = self.rows
        for c in self.hop(line, 0):
            c.wait_recv()
        if self.y_first[line]:
            arrived = [self.y_land[line][t] for t in range(r.p.groups - 1)]
            add_to(self.held.at[self.group, pl.ds(line * r.half, r.half)], arrived)
        else:
            for g in range(r.p.groups):
                arrived = [self.x_land[line][s, g] for s in range(r.p.inner - 1)]
                add_to(self.held.at[g, r.part(line, self.x)], arrived)
        for c in self.hop(line, 1):
            c.start()

    def step_third(self, line):
        r = self.rows
        for c in self.hop(line, 1):
            c.wait_recv()
        if self.y_first[line]:
            arrived = [self.x_land[line][s, 0] for s in range(r.p.inner - 1)]
        else:
            arrived = [self.y_land[line][t] for t in range(r.p.groups - 1)]
        add_to(self.held.at[self.group, r.part(line, self.x)], arrived)

    def part(self, line):
        return self.held.at[self.group, self.rows.part(line, self.x)]

    def end(self):
        for c in self.core_copies():
            c.wait_send()
        for line in range(2):
            for which in range(2):
                for c in self.hop(line, which):
                    c.wait_send()


class Spread:
    def __init__(self, rows):
        self.rows = rows

    def scratch(self):
        r, dma = self.rows, pltpu.SemaphoreType.DMA
        return [
            pltpu.VMEM((2, 3, r.small, LANES), BF16),
            dma((2, 3, 2)),
            dma((2, 3, 2)),
            dma((2, OUTER, r.p.inner - 1, 2)),
        ]

    count = 4

    def bind(self, piece, full, refs):
        self.piece, self.full = piece, full
        self.land, self.s_sem, self.g_sem, self.x_sem = refs
        seq = lax.axis_index("seq")
        n = self.rows.p.inner
        self.z, self.x = lax.div(seq, n), lax.rem(seq, n)
        self.near = self.z + 1 - 2 * lax.rem(self.z, 2)
        self.two = lax.rem(self.z + 2, OUTER)
        self.across = lax.rem(self.near + 2, OUTER)

    def copy(self, src, dst, sems, group):
        return remote(src, dst, sems, seq=group * self.rows.p.inner + self.x)

    def sum_copy(self, line, i):
        piece = self.piece(line, (self.near, self.across, self.two)[i])
        sems = self.s_sem.at[line, i, 0], self.s_sem.at[line, i, 1]
        return self.copy(piece, self.land.at[line, i], sems, self.two if i == 2 else self.near)

    def z_copy(self, line, i):
        where = self.rows.quarter(line, self.x, self.two if i == 2 else self.z)
        sems = self.g_sem.at[line, i, 0], self.g_sem.at[line, i, 1]
        return self.copy(self.full.at[where], self.full.at[where], sems, self.two if i == 0 else self.near)

    def x_copies(self, line, c):
        n = self.rows.p.inner
        where = self.rows.quarter(line, self.x, c)
        for s in range(1, n):
            sems = self.x_sem.at[line, c, s - 1, 0], self.x_sem.at[line, c, s - 1, 1]
            yield remote(self.full.at[where], self.full.at[where], sems, seq=self.z * n + lax.rem(self.x + s, n))

    def spread(self, line, c):
        for s in self.x_copies(line, c):
            s.start()

    def step_pair(self, line):
        self.sum_copy(line, 0).start()
        self.sum_copy(line, 1).start()

    def step_two(self, line):
        for i, c in ((0, self.z), (1, self.two)):
            self.sum_copy(line, i).wait_recv()
            add_to(self.piece(line, c), [self.land[line, i]])
        self.sum_copy(line, 2).start()

    def step_back(self, line):
        self.sum_copy(line, 2).wait_recv()
        where = self.rows.quarter(line, self.x, self.z)
        self.full[where] = self.piece(line, self.z)[...] + self.land[line, 2]
        self.z_copy(line, 0).start()
        self.z_copy(line, 1).start()
        self.spread(line, self.z)

    def step_rest(self, line):
        self.z_copy(line, 0).wait_recv()
        self.z_copy(line, 2).start()
        self.spread(line, self.two)
        self.z_copy(line, 1).wait_recv()
        self.spread(line, self.near)

    def step_last(self, line):
        self.z_copy(line, 2).wait_recv()
        self.spread(line, self.across)

    def end(self):
        for line in range(2):
            for c in range(OUTER):
                for s in self.x_copies(line, c):
                    s.wait_send()
                    s.wait_recv()
            for i in range(3):
                self.sum_copy(line, i).wait_send()
                self.z_copy(line, i).wait_send()


def greet_all(places):
    dp, seq = lax.axis_index("dp"), lax.axis_index("seq")
    n = places.inner
    core, group = lax.rem(dp, 2), lax.div(dp, 2)
    barrier = pltpu.get_barrier_semaphore()
    mesh = pl.DeviceIdType.MESH
    pl.semaphore_signal(barrier, inc=1, device_id={"dp": group * 2 + 1 - core}, device_id_type=mesh)
    for t in range(1, places.groups):
        other = lax.rem(group + t, places.groups) * 2 + core
        pl.semaphore_signal(barrier, inc=1, device_id={"dp": other}, device_id_type=mesh)
    for peer in peers(n, lax.div(seq, n), lax.rem(seq, n)):
        pl.semaphore_signal(barrier, inc=1, device_id={"seq": peer}, device_id_type=mesh)
    pl.semaphore_wait(barrier, 1 + places.groups - 1 + OUTER - 1 + n - 1)


SMALL = 16


def last_kernel(early, late, *refs):
    count = 11
    sources, (gain_ref, ffn_ref), refs = refs[:count], refs[count : count + 2], refs[count + 2 :]
    grad_in, full_early, full_late, refs = refs[0], refs[1], refs[2], refs[3:]
    slots, load_sem, refs = refs[:count], refs[count], refs[count + 1 :]
    loads = [pltpu.make_async_copy(src, dst, load_sem.at[i]) for i, (src, dst) in enumerate(zip(sources, slots))]
    for c in loads:
        c.start()
    held, grads, normed_t, wq_ref, wk_ref, wv_ref, x_ref, mixed_ref, near, far_sum, onehot = slots
    gq, gk, gv, small, refs = refs[0], refs[1], refs[2], refs[3], refs[4:]
    p = late.p
    scatter, spread_early, spread_late = Scatter(late, (True, False)), Spread(early), Spread(late)
    scatter.bind((gq, gk, gv, small), refs[: Scatter.count])
    refs = refs[Scatter.count :]

    def early_piece(line, c):
        return held.at[line, pl.ds(pl.multiple_of(c * early.small, 16), early.small)]

    def late_piece(line, c):
        return scatter.held.at[scatter.group, late.quarter(line, scatter.x, c)]

    spread_early.bind(early_piece, full_early, refs[: Spread.count])
    spread_late.bind(late_piece, full_late, refs[Spread.count :])
    greet_all(p)
    loads[0].wait()
    for line in range(2):
        spread_early.step_pair(line)
    for c in loads[1:]:
        c.wait()
    batch, height, width = x_ref.shape
    for i, out in enumerate((gq, gk, gv)):
        total = jnp.zeros((width, width), F32)
        for b in range(batch):
            total = total + lax.dot_general(normed_t[b], grads[i, b], NT, preferred_element_type=F32)
        out[...] = total.astype(BF16)
        scatter.step_core((i,))
    gain = gain_ref[...]
    gain_sum = jnp.zeros((1, width), F32)
    for b in range(batch):
        back = jnp.dot(wq_ref[...], grads[0, b], preferred_element_type=F32)
        back = back + jnp.dot(wk_ref[...], grads[1, b], preferred_element_type=F32)
        back = (back + jnp.dot(wv_ref[...], grads[2, b], preferred_element_type=F32)).T
        values = x_ref[b]
        scale = lax.rsqrt(jnp.mean(values * values, axis=-1, keepdims=True) + epsilon)
        gain_sum = gain_sum + jnp.sum(back * values * scale, axis=0, keepdims=True)
        u = back * gain
        along = jnp.mean(u * values, axis=-1, keepdims=True)
        grad_in[b] = mixed_ref[b] + scale * (u - values * (scale * scale * along))
    row = lax.broadcasted_iota(jnp.int32, (BLK, BLK), 0)
    col = lax.broadcasted_iota(jnp.int32, (BLK, BLK), 1)
    flip = (row + col == BLK - 1).astype(F32)
    bucket = lax.broadcasted_iota(jnp.int32, (NB, 1), 0)
    head_lane = lax.broadcasted_iota(jnp.int32, (NB, LANES), 1)
    table = jnp.zeros((NB, LANES), F32)
    for h in range(HEADS):
        line = jnp.zeros((1, SPAN), F32)
        for off in (-1, 0, 1):
            flipped = jnp.dot(flip, near[h, off + 2], preferred_element_type=F32, precision=highest)
            padded = jnp.concatenate([flipped, jnp.zeros((BLK, SPAN - BLK), F32)], axis=1)
            rolled = pltpu.roll(padded, (BLK - off * BLK) % SPAN, 1, stride=1, stride_axis=0)
            line = line + jnp.sum(rolled, axis=0, keepdims=True)
        column = jnp.sum(onehot[...] * line, axis=1, keepdims=True)
        sides = jnp.sum(far_sum[h], axis=1, keepdims=True)
        column = column + jnp.where(bucket == NB // 2 - 1, sides[0:1], 0.0) + jnp.where(bucket == NB - 1, sides[1:2], 0.0)
        table = jnp.where(head_lane == scatter.z * HEADS + h, column, table)
    share, buckets = width // p.dp, NB // p.dp
    for i in range(p.dp):
        block = [v[:, i * share : (i + 1) * share] for v in (gain_sum, ffn_ref[...])]
        block = [jnp.concatenate([v, jnp.zeros((1, LANES - share), F32)], axis=1) for v in block]
        block += [table[i * buckets : (i + 1) * buckets], jnp.zeros((SMALL - 2 - buckets, LANES), F32)]
        small[i * SMALL : (i + 1) * SMALL] = jnp.concatenate(block, axis=0).astype(BF16)
    scatter.step_core((3,))
    for line in range(2):
        spread_early.step_two(line)
    scatter.step_first()
    for line in range(2):
        spread_early.step_back(line)
    for line in range(2):
        scatter.step_second(line)
    for line in range(2):
        spread_early.step_rest(line)
    for line in range(2):
        scatter.step_third(line)
        spread_late.step_pair(line)
    for line in range(2):
        spread_early.step_last(line)
    for line in range(2):
        spread_late.step_two(line)
    for line in range(2):
        spread_late.step_back(line)
    for line in range(2):
        spread_late.step_rest(line)
    for line in range(2):
        spread_late.step_last(line)
    spread_early.end()
    spread_late.end()
    scatter.end()


def last_grads(early, late, loaded, gain, ffn):
    inputs = loaded[6]
    width = inputs.shape[-1]
    return pl.pallas_call(
        functools.partial(last_kernel, early, late),
        in_specs=[anywhere()] * len(loaded) + [whole()] * 2,
        out_specs=[whole()] * 3,
        out_shape=[jax.ShapeDtypeStruct(inputs.shape, F32)]
        + [jax.ShapeDtypeStruct((r.total, LANES), BF16) for r in (early, late)],
        scratch_shapes=[pltpu.VMEM(v.shape, v.dtype) for v in loaded]
        + [pltpu.SemaphoreType.DMA((len(loaded),))]
        + [pltpu.VMEM((width, width), BF16)] * 3
        + [pltpu.VMEM((late.p.dp * SMALL, LANES), BF16)]
        + Scatter(late, (True, False)).scratch()
        + Spread(early).scratch()
        + Spread(late).scratch(),
        compiler_params=pltpu.CompilerParams(
            vmem_limit_bytes=VMEM_BYTES, collective_id=2, has_side_effects=True
        ),
        name="last_grads",
    )(*loaded, gain.reshape(1, -1), ffn.reshape(1, -1))


def unpack_kernel(all_rows, *refs):
    fulls, outs = refs[: len(all_rows)], list(refs[len(all_rows) :])
    *_, (_, _, first, _) = all_rows[-1].blocks
    share = outs[-3].shape[1]
    buckets, heads = outs[-1].shape
    outs[-3][...] = fulls[-1][first : first + SMALL].astype(F32)[0:1, :share]
    outs[-2][...] = fulls[-1][first : first + SMALL].astype(F32)[1:2, :share]
    outs[-1][...] = fulls[-1][first : first + SMALL].astype(F32)[2 : 2 + buckets, :heads]
    outs = outs[:-3] + [None]
    for rows, full in zip(all_rows, fulls):
        for m, block, at, share in rows.blocks:
            if outs[m] is not None:
                outs[m][:, block * LANES : (block + 1) * LANES] = full[at : at + share].astype(F32)
        outs = outs[len(rows.shapes) :]


def unpack(all_rows, fulls, width):
    dp = all_rows[0].p.dp
    shapes = [(height // dp, columns) for r in all_rows for height, columns in r.shapes][:-1]
    shapes += [(1, width // dp)] * 2 + [(NB // dp, H)]
    return pl.pallas_call(
        functools.partial(unpack_kernel, all_rows),
        in_specs=[whole()] * len(fulls),
        out_specs=[whole()] * len(shapes),
        out_shape=[jax.ShapeDtypeStruct(s, F32) for s in shapes],
        compiler_params=params(),
        name="unpack",
    )(*fulls)


def greet(n, z, x):
    barrier = pltpu.get_barrier_semaphore()
    for peer in peers(n, z, x):
        pl.semaphore_signal(barrier, inc=1, device_id={"seq": peer}, device_id_type=pl.DeviceIdType.MESH)
    pl.semaphore_wait(barrier, OUTER - 1 + n - 1)


def far_case(n, j, kb):
    if kb < n * j - 1:
        return 0
    if kb > n * j + n:
        return 2
    return None


def near_case(n, j, kb, x):
    off = kb - (n * j + x)
    near = jnp.logical_and(off >= -1, off <= 1)
    return jnp.where(near, off + 2, 0), jnp.where(off <= -2, 0, jnp.where(off >= 2, 2, 1))


def key_rows(keys, kb, length):
    one = jnp.ones((1, BLK), F32)
    lane = lax.broadcasted_iota(jnp.int32, (1, BLK), 1)
    mask = jnp.where(kb * BLK + lane < length, 0.0, -1e30)
    return jnp.concatenate([keys, tail(BLK, (one, one, one, mask)).astype(BF16)], axis=0).T


def forward_kernel(
    n, len_ref, table_ref, onehot_ref, x_ref, gain_ref, wq_ref, wk_ref, wv_ref,
    normed_ref, own, pair, att, o_ref, lse_ref, tile_ref, far_ref,
    send, ka, qa, va,
    z_send, z_recv, x_send, x_recv, o_send, o_recv,
):
    nk = OUTER * n
    batch = x_ref.shape[0]
    units = batch * HEADS
    me = lax.axis_index("seq")
    z, x = lax.div(me, n), lax.rem(me, n)
    greet(n, z, x)

    def z_copy(u, d):
        group = lax.rem(z + d, OUTER)
        sems = z_send.at[u, d - 1], z_recv.at[u, d - 1]
        return remote(send.at[u, group], own.at[u, z], sems, seq=group * n + x)

    def x_copy(u, s, d):
        group = lax.rem(z + OUTER - d, OUTER)
        rows = pl.ds(DH, 2 * DH)
        peer = z * n + lax.rem(x + s, n)
        sems = x_send.at[s - 1, u, d], x_recv.at[s - 1, u, d]
        return remote(own.at[u, group, rows], pair.at[s - 1, u, group], sems, seq=peer)

    def o_copy(u, d):
        group = lax.rem(z + d, OUTER)
        b, h = lax.div(u, HEADS), lax.rem(u, HEADS)
        rows = pl.ds(pl.multiple_of((z * HEADS + h) * DH, DH), DH)
        sems = o_send.at[u, d - 1], o_recv.at[u, d - 1]
        return remote(o_ref.at[u, group], att.at[b, rows], sems, seq=group * n + x)

    for b in range(batch):
        values = x_ref[b]
        scale = lax.rsqrt(jnp.mean(values * values, axis=-1, keepdims=True) + epsilon)
        normed = (values * scale * gain_ref[...]).astype(BF16)
        normed_ref[b] = normed.T
        for i, (w_ref, factor) in enumerate(((wq_ref, LOG2E), (wk_ref, 1.0), (wv_ref, 1.0))):
            turned = (jnp.dot(normed, w_ref[...], preferred_element_type=F32) * factor).T.astype(BF16)
            for g in range(OUTER):
                for h in range(HEADS):
                    first = (g * HEADS + h) * DH
                    send[b * HEADS + h, g, i * DH : (i + 1) * DH] = turned[first : first + DH]
        for h in range(HEADS):
            u = b * HEADS + h
            for d in (2, 1, 3):
                z_copy(u, d).start()
            own[u, z] = send[u, z]
            for s in range(1, n):
                x_copy(u, s, 0).start()

    head_lane = lax.broadcasted_iota(jnp.int32, (NB, H), 1)
    for h in range(HEADS):
        chosen = jnp.where(head_lane == z * HEADS + h, table_ref[...], 0.0)
        column = jnp.sum(chosen, axis=1, keepdims=True) * LOG2E
        line = jnp.broadcast_to(jnp.sum(onehot_ref[...] * column, axis=0, keepdims=True), (BLK, SPAN))
        tile_ref[h, 0] = jnp.zeros((BLK, BLK), F32)
        for off in (-1, 0, 1):
            shift = (off * BLK - (2 * BLK - 1)) % SPAN
            tile_ref[h, off + 2] = pltpu.roll(line, shift, 1, stride=1, stride_axis=0)[:, :BLK]
        far_ref[h, 0] = jnp.broadcast_to(column[NB // 2 - 1 : NB // 2], (1, BLK))
        far_ref[h, 1] = jnp.broadcast_to(column[NB - 1 :], (1, BLK))

    def attend(u):
        b, h = lax.div(u, HEADS), lax.rem(u, HEADS)
        length = len_ref[b]
        left, right = far_ref[h, 0], far_ref[h, 1]
        one = jnp.ones((1, BLK), F32)
        vtail = tail(BLK, (one,)).astype(BF16)
        for s in range(1, n):
            for d in range(OUTER):
                x_copy(u, s, d).wait_recv()
        for s in range(n):
            col = lax.rem(x + s, n)
            for j in range(OUTER):
                kb = n * j + col
                if s == 0:
                    keys, vals = own[u, j, DH : 2 * DH], own[u, j, 2 * DH :]
                else:
                    keys, vals = pair[n - s - 1, u, j, :DH], pair[n - s - 1, u, j, DH:]
                ka[kb] = key_rows(keys, kb, length)
                columns = pl.ds(pl.multiple_of(kb * BLK, BLK), BLK)
                va[:DH, columns] = vals
                va[DH:, columns] = vtail

        def scores(kb, j):
            case = far_case(n, j, kb)
            if case is not None:
                return jnp.dot(ka[kb], qa[case, j], preferred_element_type=F32)
            tile, case = near_case(n, j, kb, x)
            return jnp.dot(ka[kb], qa[case, j], preferred_element_type=F32) + tile_ref[h, tile]

        for j in range(OUTER):
            for v, c in enumerate((left, 0.0 * one, right)):
                qa[v, j, :DH] = own[u, j, :DH]
                qa[v, j, DH:] = tail(BLK, split3(c) + (one,)).astype(BF16)
        tops = []
        for j in range(OUTER):
            top = jnp.full((8, BLK), -1e30, F32)
            for kb in range(nk):
                top = jnp.maximum(top, jnp.max(scores(kb, j).reshape(BLK // 8, 8, BLK), axis=0))
            top = jnp.max(top, axis=0, keepdims=True)
            tops.append(top)
            for v, c in enumerate((left, 0.0, right)):
                qa[v, j, DH:] = tail(BLK, split3(c - top) + (one,)).astype(BF16)
        for j in range(OUTER):
            weights = [jnp.exp2(scores(kb, j)).astype(BF16) for kb in range(nk)]
            total = jnp.dot(va[...], jnp.concatenate(weights, axis=0), preferred_element_type=F32)
            weight = total[DH : DH + 1]
            o_ref[u, j] = (total[:DH] / weight).astype(BF16)
            lse_ref[u, j] = tops[j] + jnp.log2(weight)
        rows = pl.ds(pl.multiple_of((z * HEADS + h) * DH, DH), DH)
        att[b, rows] = o_ref[u, z]
        for d in (2, 1, 3):
            o_copy(u, d).start()

    def turn(u, carry):
        @pl.when(u < units)
        def _():
            for d in (1, 3, 2):
                z_copy(u, d).wait_recv()
                for s in range(1, n):
                    x_copy(u, s, d).start()

        @pl.when(u > 0)
        def _():
            attend(u - 1)

        return carry

    lax.fori_loop(0, units + 1, turn, 0)

    def finish(u, carry):
        for d in range(1, OUTER):
            z_copy(u, d).wait_send()
            o_copy(u, d).wait_send()
            o_copy(u, d).wait_recv()
        for s in range(1, n):
            for d in range(OUTER):
                x_copy(u, s, d).wait_send()
        return carry

    lax.fori_loop(0, units, finish, 0)


def attention_forward(n, lengths, table, onehot, inputs, gain, wq, wk, wv):
    batch, height, width = inputs.shape
    units, nk = batch * HEADS, n * OUTER
    dma = pltpu.SemaphoreType.DMA
    return pl.pallas_call(
        functools.partial(forward_kernel, n),
        in_specs=[smem()] + [whole()] * 7,
        out_specs=[whole()] * 8,
        out_shape=[
            jax.ShapeDtypeStruct((batch, width, height), BF16),
            jax.ShapeDtypeStruct((units, OUTER, 3 * DH, BLK), BF16),
            jax.ShapeDtypeStruct((n - 1, units, OUTER, 2 * DH, BLK), BF16),
            jax.ShapeDtypeStruct((batch, width, height), BF16),
            jax.ShapeDtypeStruct((units, OUTER, DH, BLK), BF16),
            jax.ShapeDtypeStruct((units, OUTER, 1, BLK), F32),
            jax.ShapeDtypeStruct((HEADS, TILES, BLK, BLK), F32),
            jax.ShapeDtypeStruct((HEADS, 2, 1, BLK), F32),
        ],
        scratch_shapes=[
            pltpu.VMEM((units, OUTER, 3 * DH, BLK), BF16),
            pltpu.VMEM((nk, BLK, AUG), BF16),
            pltpu.VMEM((3, OUTER, AUG, BLK), BF16),
            pltpu.VMEM((AUG, nk * BLK), BF16),
            dma((units, OUTER - 1)),
            dma((units, OUTER - 1)),
            dma((n - 1, units, OUTER)),
            dma((n - 1, units, OUTER)),
            dma((units, OUTER - 1)),
            dma((units, OUTER - 1)),
        ],
        compiler_params=pltpu.CompilerParams(
            vmem_limit_bytes=VMEM_BYTES, collective_id=0, has_side_effects=True
        ),
        cost_estimate=pl.CostEstimate(flops=45 * 10**9, bytes_accessed=24 << 20, transcendentals=0),
        name="attention_forward",
    )(lengths, table, onehot, inputs, gain.reshape(1, -1), wq, wk, wv)


def backward_kernel(
    n, early, len_ref, far_ref, tile_ref, own, pair, o_ref, lse_ref, dout, *refs
):
    count = len(early.shapes)
    weights, refs = refs[:count], refs[count:]
    (grads, near, far_sum, parts, own_slot, pair_slot, load_sem,
    do_land, x_out, x_land, z_out, kept,
    ka, kt, va, qa, da, dk_all, dv_all,
    d_send, d_recv, x_send, x_recv, z_send, z_recv) = refs[: -Scatter.count]
    scatter = Scatter(early, (True, True))
    scatter.bind(weights, refs[-Scatter.count :])
    nk = OUTER * n
    batch = dout.shape[0]
    units = batch * HEADS
    x_slots, z_slots = staging(n, units)
    me = lax.axis_index("seq")
    z, x = lax.div(me, n), lax.rem(me, n)
    greet_all(early.p)
    scatter.step_core()

    def head_rows(group, h):
        return pl.ds(pl.multiple_of((group * HEADS + h) * DH, DH), DH)

    def d_copy(u, d):
        group = lax.rem(z + d, OUTER)
        b, h = lax.div(u, HEADS), lax.rem(u, HEADS)
        sems = d_send.at[u, d - 1], d_recv.at[u, d - 1]
        return remote(dout.at[b, head_rows(group, h)], do_land.at[u, z], sems, seq=group * n + x)

    def x_copy(u, s):
        peer = z * n + lax.rem(x + s, n)
        sems = x_send.at[s - 1, u], x_recv.at[s - 1, u]
        return remote(x_out.at[s - 1, lax.rem(u, x_slots)], x_land.at[s - 1, u], sems, seq=peer)

    def z_copy(u, d, i):
        group = lax.rem(z + d, OUTER)
        b, h = lax.div(u, HEADS), lax.rem(u, HEADS)
        sems = z_send.at[u, d - 1, i], z_recv.at[u, d - 1, i]
        src, dst = z_out.at[lax.rem(u, z_slots), group, pl.ds(i * DH, DH)], grads.at[i, b, head_rows(z, h)]
        return remote(src, dst, sems, seq=group * n + x)

    def loads(u):
        slot = lax.rem(u, 2)
        yield pltpu.make_async_copy(own.at[u], own_slot.at[slot], load_sem.at[slot, 0])
        for s in range(1, n):
            yield pltpu.make_async_copy(pair.at[s - 1, u], pair_slot.at[slot, s - 1], load_sem.at[slot, s])

    for c in loads(0):
        c.start()

    def begin(u, carry):
        for d in (2, 1, 3):
            d_copy(u, d).start()
        do_land[u, z] = dout[lax.div(u, HEADS), head_rows(z, lax.rem(u, HEADS))]
        return carry

    lax.fori_loop(0, units, begin, 0)
    near[...] = jnp.zeros_like(near)
    far_sum[...] = jnp.zeros_like(far_sum)
    one = jnp.ones((1, BLK), F32)
    ones3 = tail(BLK, (one, one, one)).astype(BF16)
    row16 = lax.broadcasted_iota(jnp.int32, (16, BLK), 0)
    marks = [jnp.where(row16 == r, 1.0, 0.0).astype(BF16) for r in range(2)]

    def work(u):
        b, h = lax.div(u, HEADS), lax.rem(u, HEADS)
        length = len_ref[b]
        left, right = far_ref[h, 0], far_ref[h, 1]
        slot = lax.rem(u, 2)
        for c in loads(u):
            c.wait()

        @pl.when(u + 1 < units)
        def _():
            for c in loads(u + 1):
                c.start()

        for s in range(n):
            col = lax.rem(x + s, n)
            for j in range(OUTER):
                kb = n * j + col
                if s == 0:
                    keys, vals = own_slot[slot, j, DH : 2 * DH], own_slot[slot, j, 2 * DH :]
                else:
                    keys, vals = pair_slot[slot, n - s - 1, j, :DH], pair_slot[slot, n - s - 1, j, DH:]
                ka[kb] = key_rows(keys, kb, length)
                kt[kb] = keys
                va[kb] = jnp.concatenate([vals, ones3], axis=0).T
        for d in range(1, OUTER):
            d_copy(u, d).wait_recv()
        for j in range(OUTER):
            lse = lse_ref[u, j]
            for v, c in enumerate((left, 0.0, right)):
                qa[v, j, :DH] = own_slot[slot, j, :DH]
                qa[v, j, DH:] = tail(BLK, split3(c - lse) + (one,)).astype(BF16)
            arrived = do_land[u, j]
            delta = jnp.sum(arrived.astype(F32) * o_ref[u, j].astype(F32), axis=0, keepdims=True)
            da[j, :DH] = arrived
            da[j, DH:] = tail(BLK, split3(-delta)).astype(BF16)
        dqs = [None] * OUTER
        for g in range(0, nk, GROUP):
            blocks = range(g, g + GROUP)
            ps, dss = {}, {}
            for j in range(OUTER):
                left_side = []
                for kb in blocks:
                    case = far_case(n, j, kb)
                    if case is not None:
                        p = jnp.exp2(jnp.dot(ka[kb], qa[case, j], preferred_element_type=F32))
                        mark = marks[case // 2]
                    else:
                        tile, case = near_case(n, j, kb, x)
                        s = jnp.dot(ka[kb], qa[case, j], preferred_element_type=F32)
                        p = jnp.exp2(s + tile_ref[h, tile])
                        want = jnp.where(case == 1, 2, lax.div(case, 2))
                        mark = jnp.where(row16 == want, 1.0, 0.0).astype(BF16)
                    ds = p * jnp.dot(va[kb], da[j], preferred_element_type=F32)
                    if far_case(n, j, kb) is None:
                        near[h, tile] += ds
                    ps[kb, j], dss[kb, j] = p.astype(BF16), ds.astype(BF16)
                    left_side.append(jnp.concatenate([kt[kb], mark], axis=0))
                right_side = jnp.concatenate([dss[kb, j] for kb in blocks], axis=0)
                dq = jnp.dot(jnp.concatenate(left_side, axis=1), right_side, preferred_element_type=F32)
                dqs[j] = dq if g == 0 else dqs[j] + dq
            for kb in blocks:
                dv, dk = jnp.zeros((DH, BLK), F32), jnp.zeros((DH, BLK), F32)
                for j in range(OUTER):
                    dv = dv + lax.dot_general(da[j, :DH], ps[kb, j], NT, preferred_element_type=F32)
                    dk = dk + lax.dot_general(qa[0, j, :DH], dss[kb, j], NT, preferred_element_type=F32)
                dk_all[kb] = dk * LN2
                dv_all[kb] = dv
        @pl.when(u >= z_slots)
        def _():
            for d in range(1, OUTER):
                for i in range(3):
                    z_copy(u - z_slots, d, i).wait_send()

        @pl.when(u >= x_slots)
        def _():
            for s in range(1, n):
                x_copy(u - x_slots, s).wait_send()

        far = jnp.zeros((8, BLK), F32)
        for j in range(OUTER):
            z_out[lax.rem(u, z_slots), j, :DH] = dqs[j][:DH].astype(BF16)
            far = far + dqs[j][DH : DH + 8]
        far_sum[h] += far
        parity = lax.rem(u, 2)
        for j in range(OUTER):
            kept[parity, j, :DH] = dk_all[n * j + x]
            kept[parity, j, DH:] = dv_all[n * j + x]
            for s in range(1, n):
                kb = n * j + lax.rem(x + s, n)
                x_out[s - 1, lax.rem(u, x_slots), j, :DH] = dk_all[kb].astype(BF16)
                x_out[s - 1, lax.rem(u, x_slots), j, DH:] = dv_all[kb].astype(BF16)
        for s in range(1, n):
            x_copy(u, s).start()

    def hand_over(u):
        b, h = lax.div(u, HEADS), lax.rem(u, HEADS)
        parity = lax.rem(u, 2)
        for s in range(1, n):
            x_copy(u, s).wait_recv()
        for j in range(OUTER):
            total = kept[parity, j]
            for s in range(1, n):
                total = total + x_land[s - 1, u, j].astype(F32)
            z_out[lax.rem(u, z_slots), j, DH:] = total.astype(BF16)
        for i in range(3):
            grads[i, b, head_rows(z, h)] = z_out[lax.rem(u, z_slots), z, i * DH : (i + 1) * DH]
            for d in (2, 1, 3):
                z_copy(u, d, i).start()

    def turn(u, carry):
        @pl.when(u < units)
        def _():
            work(u)

        @pl.when(u > 0)
        def _():
            hand_over(u - 1)

        pl.when(u == 0)(scatter.step_first)
        for line in range(2):
            pl.when(u == 4 + 3 * line)(functools.partial(scatter.step_second, line))

        return carry

    lax.fori_loop(0, units + 1, turn, 0)

    def finish(u, carry):
        for d in range(1, OUTER):
            d_copy(u, d).wait_send()
            for i in range(3):
                z_copy(u, d, i).wait_recv()

                @pl.when(u >= units - z_slots)
                def _():
                    z_copy(u, d, i).wait_send()

        @pl.when(u >= units - x_slots)
        def _():
            for s in range(1, n):
                x_copy(u, s).wait_send()

        return carry

    lax.fori_loop(0, units, finish, 0)
    for line in range(2):
        scatter.step_third(line)
        parts[line] = scatter.part(line)[...]
    scatter.end()


def staging(n, units):
    return (units, units) if n <= 2 else (2, 4)


def attention_backward(n, early, lengths, far, tiles, own, pair, out, lse, dout, weights):
    batch, width, height = dout.shape
    units, nk = batch * HEADS, n * OUTER
    dma = pltpu.SemaphoreType.DMA
    x_slots, z_slots = staging(n, units)
    return pl.pallas_call(
        functools.partial(backward_kernel, n, early),
        in_specs=[smem()] + [whole()] * 2 + [anywhere()] * 2 + [whole()] * 3 + [anywhere()] * len(weights),
        out_specs=[whole()] * 4,
        out_shape=[
            jax.ShapeDtypeStruct((3, batch, width, height), BF16),
            jax.ShapeDtypeStruct((HEADS, TILES, BLK, BLK), F32),
            jax.ShapeDtypeStruct((HEADS, 8, BLK), F32),
            jax.ShapeDtypeStruct((2, early.size, LANES), BF16),
        ],
        scratch_shapes=[
            pltpu.VMEM((2, OUTER, 3 * DH, BLK), BF16),
            pltpu.VMEM((2, n - 1, OUTER, 2 * DH, BLK), BF16),
            dma((2, n)),
            pltpu.VMEM((units, OUTER, DH, BLK), BF16),
            pltpu.VMEM((n - 1, x_slots, OUTER, 2 * DH, BLK), BF16),
            pltpu.VMEM((n - 1, units, OUTER, 2 * DH, BLK), BF16),
            pltpu.VMEM((z_slots, OUTER, 3 * DH, BLK), BF16),
            pltpu.VMEM((2, OUTER, 2 * DH, BLK), F32),
            pltpu.VMEM((nk, BLK, AUG), BF16),
            pltpu.VMEM((nk, DH, BLK), BF16),
            pltpu.VMEM((nk, BLK, AUG), BF16),
            pltpu.VMEM((3, OUTER, AUG, BLK), BF16),
            pltpu.VMEM((OUTER, AUG, BLK), BF16),
            pltpu.VMEM((nk, DH, BLK), F32),
            pltpu.VMEM((nk, DH, BLK), F32),
            dma((units, OUTER - 1)),
            dma((units, OUTER - 1)),
            dma((n - 1, units)),
            dma((n - 1, units)),
            dma((units, OUTER - 1, 3)),
            dma((units, OUTER - 1, 3)),
        ]
        + Scatter(early, (True, True)).scratch(),
        compiler_params=pltpu.CompilerParams(
            vmem_limit_bytes=VMEM_BYTES, collective_id=1, has_side_effects=True
        ),
        cost_estimate=pl.CostEstimate(flops=110 * 10**9, bytes_accessed=24 << 20, transcendentals=0),
        name="attention_backward",
    )(lengths, far, tiles, own, pair, out, lse, dout, *weights)


FF_STEP = 512


def middle_kernel(
    x_ref, att_ref, cot_ref, gain_ref, w_out, w_gate, w_up, w_down,
    result, grad_mixed, dout, d_gain, d_out, d_gate, d_up, d_down,
    wo, wg, wu, wd, att, low, hidden, g_gate, g_up, s_out, s_gate, s_up, s_down, kept, in_sem, out_sem,
):
    tokens, width = x_ref.shape
    batch = att_ref.shape[0]
    ff = w_gate.shape[1]
    loads = [
        pltpu.make_async_copy(src, dst, in_sem.at[i])
        for i, (src, dst) in enumerate(((w_out, wo), (w_gate, wg), (w_up, wu), (w_down, wd)))
    ]
    stores = [
        pltpu.make_async_copy(src, dst, out_sem.at[i])
        for i, (src, dst) in enumerate(((s_out, d_out), (s_gate, d_gate), (s_up, d_up), (s_down, d_down)))
    ]
    for c in loads:
        c.start()
    height = tokens // batch
    for b in range(batch):
        att[b * height : (b + 1) * height] = att_ref[b].T
    low[...] = cot_ref[...].astype(BF16)
    loads[0].wait()
    mixed = x_ref[...] + jnp.dot(att[...], wo[...], preferred_element_type=F32)
    kept[...] = mixed
    result[...] = mixed
    scale = lax.rsqrt(jnp.mean(mixed * mixed, axis=-1, keepdims=True) + epsilon)
    normed = (mixed * scale * gain_ref[...]).astype(BF16)
    att[...] = normed
    for c in loads[1:]:
        c.wait()
    root = 0.7978845608028654
    for at in range(0, ff, FF_STEP):
        part = slice(at, at + FF_STEP)
        gate = jnp.dot(att[...], wg[:, part], preferred_element_type=F32)
        upward = jnp.dot(att[...], wu[:, part], preferred_element_type=F32)
        g_hidden = lax.dot_general(low[...], wd[part], NT, preferred_element_type=F32)
        square = gate * gate
        t = jnp.tanh(root * gate * (1.0 + 0.044715 * square))
        half = 0.5 * (1.0 + t)
        act = gate * half
        slope = half + 0.5 * gate * (1.0 - t * t) * (root * (1.0 + 3.0 * 0.044715 * square))
        hidden[:, part] = (act * upward).astype(BF16)
        g_gate[:, part] = (g_hidden * upward * slope).astype(BF16)
        g_up[:, part] = (g_hidden * act).astype(BF16)
    result[...] += jnp.dot(hidden[...], wd[...], preferred_element_type=F32)
    d_normed = lax.dot_general(g_gate[...], wg[...], NT, preferred_element_type=F32)
    d_normed = d_normed + lax.dot_general(g_up[...], wu[...], NT, preferred_element_type=F32)
    mixed = kept[...]
    scale = lax.rsqrt(jnp.mean(mixed * mixed, axis=-1, keepdims=True) + epsilon)
    d_gain[...] = jnp.sum(d_normed * mixed * scale, axis=0, keepdims=True)
    u = d_normed * gain_ref[...]
    along = jnp.mean(u * mixed, axis=-1, keepdims=True)
    d_mixed = cot_ref[...] + scale * (u - mixed * (scale * scale * along))
    grad_mixed[...] = d_mixed
    d_low = d_mixed.astype(BF16)
    turned = lax.dot_general(wo[...], d_low, NT, preferred_element_type=F32).astype(BF16)
    for b in range(batch):
        dout[b] = turned[:, b * height : (b + 1) * height]
    total = jnp.zeros((width, width), F32)
    for b in range(batch):
        total = total + jnp.dot(att_ref[b], d_low[b * height : (b + 1) * height], preferred_element_type=F32)
    s_out[...] = total.astype(BF16)
    stores[0].start()
    normed_t = att[...].T
    for src, dst, store in ((g_gate, s_gate, stores[1]), (g_up, s_up, stores[2])):
        for at in range(0, ff, FF_STEP):
            part = slice(at, at + FF_STEP)
            dst[:, part] = jnp.dot(normed_t, src[:, part], preferred_element_type=F32).astype(BF16)
        store.start()
    for at in range(0, ff, FF_STEP):
        part = slice(at, at + FF_STEP)
        s_down[part] = jnp.dot(hidden[:, part].T, low[...], preferred_element_type=F32).astype(BF16)
    stores[3].start()
    for c in stores:
        c.wait()


def middle(inputs, att, cotangent, gain, w_out, w_gate, w_up, w_down):
    batch, height, width = inputs.shape
    tokens, ff = batch * height, w_gate.shape[1]
    weights = (w_out, w_gate, w_up, w_down)
    flat = (tokens, width)
    out = pl.pallas_call(
        middle_kernel,
        in_specs=[whole()] * 4 + [anywhere()] * 4,
        out_specs=[whole()] * 4 + [anywhere()] * 4,
        out_shape=[
            jax.ShapeDtypeStruct(flat, F32),
            jax.ShapeDtypeStruct(flat, F32),
            jax.ShapeDtypeStruct((batch, width, height), BF16),
            jax.ShapeDtypeStruct((1, width), F32),
        ]
        + [jax.ShapeDtypeStruct(w.shape, BF16) for w in weights],
        scratch_shapes=[pltpu.VMEM(w.shape, BF16) for w in weights]
        + [pltpu.VMEM(flat, BF16)] * 2
        + [pltpu.VMEM((tokens, ff), BF16)] * 3
        + [pltpu.VMEM(w.shape, BF16) for w in weights]
        + [pltpu.VMEM(flat, F32)]
        + [pltpu.SemaphoreType.DMA((4,))] * 2,
        compiler_params=params(),
        cost_estimate=pl.CostEstimate(flops=25 * 10**9, bytes_accessed=32 << 20, transcendentals=0),
        name="middle",
    )(inputs.reshape(flat), att, cotangent.reshape(flat), gain.reshape(1, -1), *weights)
    return out[0].reshape(inputs.shape), out[1].reshape(inputs.shape), out[2], out[3], out[4:]


def shards(
    places,
    inputs,
    lengths,
    norm_attn,
    w_query,
    w_key,
    w_value,
    w_out,
    norm_ffn,
    w_gate,
    w_up,
    w_down,
    bucket_bias,
    cotangent,
):
    batch, height, width = inputs.shape
    n = places.inner
    onehot = jnp.asarray(ONEHOT)
    normed_t, own, pair, attended_t, out, lse, tiles, far = attention_forward(
        n, lengths, bucket_bias, onehot, inputs, norm_attn, w_query, w_key, w_value
    )
    result, grad_mixed, grad_attended_t, grad_norm_ffn, weights = middle(
        inputs, attended_t, cotangent, norm_ffn, w_out, w_gate, w_up, w_down
    )
    early = Rows(places, [g.shape for g in weights])
    grads, near, far_sum, parts = attention_backward(
        n, early, lengths, far, tiles, own, pair, out, lse, grad_attended_t, weights
    )
    shapes = [w_query.shape, w_key.shape, w_value.shape, (places.dp * SMALL, LANES)]
    late = Rows(places, shapes)
    loaded = (
        parts, grads, normed_t, w_query, w_key, w_value, inputs, grad_mixed, near, far_sum, onehot
    )
    grad_inputs, full_early, full_late = last_grads(early, late, loaded, norm_attn, grad_norm_ffn)
    part_out, part_gate, part_up, part_down, part_query, part_key, part_value, part_attn, part_ffn, part_table = unpack(
        (early, late), (full_early, full_late), width
    )
    return (
        result,
        grad_inputs,
        part_attn.reshape(-1),
        part_ffn.reshape(-1),
        part_query,
        part_key,
        part_value,
        part_out,
        part_gate,
        part_up,
        part_down,
        part_table,
    )


def solution(mesh):
    rows = P("dp", "seq", None)
    share = P("dp", None)
    return jax.shard_map(
        functools.partial(shards, Places(mesh)),
        mesh=mesh,
        in_specs=(rows, P("dp")) + (P(),) * 10 + (rows,),
        out_specs=(rows, rows, P("dp"), P("dp")) + (share,) * 8,
        check_vma=False,
    )
```

time: 711 us -> 375 us (0.53)
  local copies, waits for them, and re-layouts: 164 us -> 7.14 us
  Pallas kernels: 242 us -> 361 us
  waiting for transfers between devices: 109 us -> 0 us
  starting transfers between devices: 82.3 us -> 0 us
  matrix products: 68.8 us -> 0 us
  other arithmetic: 34 us -> 0 us
    pallas_call x4 -> x5, Pallas kernels: 242 us -> 361 us  [the longest x1 118 us: attention_forward(): pl.pallas_call(functools.partial(forward_kernel, n), in_specs=[smem()] +...]
    ppermute x80 -> x0, waiting for transfers between devices: 109 us -> none  [the longest x48 57.8 us: shift_outer(): return lax.ppermute(value, 'seq', pairs)]
    dynamic_update_slice x41 -> x0, local copies, waits for them, and re-layouts: 91.1 us -> none  [the longest x8 45.1 us: reduce_grad(): lax.dynamic_update_index_in_dim(result, places.shift_inner(full, d), lax....]
    ppermute x80 -> x0, starting transfers between devices: 82.3 us -> none  [the longest x48 53.5 us: shift_outer(): return lax.ppermute(value, 'seq', pairs)]
    dot_general x20 -> x0, matrix products: 68.8 us -> none  [the longest x1 9.23 us: shards(): jnp.einsum('bsd,de->bse', normed_ffn, w_gate, preferred_element_type=F32)]
    convert_element_type x22 -> x0, other arithmetic: 20.2 us -> none  [the longest x7 8.6 us: reduce_grad(): scatter_sum(lambda i: pick(parts, i, 1), lax.rem(dp, c), c, 1, places.shi...]
    unnamed x126 -> x2, local copies, waits for them, and re-layouts: 22.8 us -> 4.6 us
    broadcast_in_dim x20 -> x0, local copies, waits for them, and re-layouts: 16.3 us -> none  [the longest x7 7.95 us: reduce_grad(): lax.dynamic_update_index_in_dim(result, places.shift_inner(full, d), lax....]
  transfers between devices with their start and end apart: 80 -> 0, of which waited for: 40 -> 0; matrix products, arithmetic and copies ran while one was open for 29% -> 0% of each run, Pallas kernels for 17% -> 0%
where the time goes in v4:
time: 375 us; the launch traced here: 369 us
  Pallas kernels  361 us (96%)
  local copies, waits for them, and re-layouts  7.14 us (2%)
    pallas_call x1, Pallas kernels, attention_forward(): pl.pallas_call(functools.partial(forward_kernel, n), in_specs=[smem()] +...  118 us
    pallas_call x1, Pallas kernels, attention_backward(): pl.pallas_call(functools.partial(backward_kernel, n, early), in_specs=[sm...  114 us
    pallas_call x1, Pallas kernels, last_grads(): pl.pallas_call(functools.partial(last_kernel, early, late), in_specs=[any...  85.2 us
    pallas_call x1, Pallas kernels, middle(): pl.pallas_call(middle_kernel, in_specs=[whole()] * 4 + [anywhere()] * 4,...  38.7 us

profile of v4, /device:TPU:0, one launch (start us, length us, event | category | flops | bytes accessed | tf_op | source)
XLA Modules:
  0.0 369.0 jit_solution(8370817356384066379)
XLA Ops:
  0.6 1.3 reshape.50.gain_ref.refs_11_
  1.9 1.3 reshape.52.gain_ref
  3.2 1.4 copy.26.table_ref
  4.6 117.5 %attention_forward.1 = (bf16[3,768,256]{2,1,0:T(8,128)(2,1)}, bf16[9,4,192,256]{3,2,1,0:T(8,128)(2,1)}, bf16[1,9,4,128,256]{4,3,2,1,0:T(8,128)(2,1)}, bf16[3,768...) custom-call(s32[3]{0:T(128)} %len_ref.3, ...), custom_call_target="tpu_custom_call" | custom-call | flops 44999999488 | bytes 25165824 | tf_op jit(solution)/shard_map/attention_forward/pallas_call | solution.py:697
  122.1 38.7 %middle.1 = (f32[768,768]{1,0:T(8,128)}, f32[768,768]{1,0:T(8,128)}, bf16[3,768,256]{2,1,0:T(8,128)(2,1)}, f32[1,768]{1,0:T(1,128)}, bf16[768,768]{1,0:T(8,128)(...) custom-call(f32[768,768]{1,0:T(8,128)} %bitcast.6, ...), custom_call_target="tpu_custom_call" | custom-call | flops 24999999488 | bytes 33554432 | tf_op jit(solution)/shard_map/middle/pallas_call | solution.py:1082
  160.8 114.2 %attention_backward.1 = (bf16[3,3,768,256]{3,2,1,0:T(8,128)(2,1)}, f32[3,4,256,256]{3,2,1,0:T(8,128)}, f32[3,8,256]{2,1,0:T(8,128)}, bf16[2,1344,256]{2,1,0:T(8,128)(2,1)}) custom-call(s32[3]{0:T(128)} %len_ref.3, f32[3,2,1,256]{3,2,1,0:T(1,128)} %get-tuple-element.47.far_ref, f32[3,4,256,256]{3,2,1,0:T(8,128)} %get-tuple-element.48.tile_ref, ...), custom_call_target="tpu_custom_call" | custom-call | flops 109999996928 | bytes 25165824 | tf_op jit(solution)/shard_map/attention_backward/pallas_call | solution.py:954
  275.0 85.2 %last_grads.1 = (f32[3,256,768]{2,1,0:T(8,128)}, bf16[5376,256]{1,0:T(8,128)(2,1)}, bf16[1792,256]{1,0:T(8,128)(2,1)}) custom-call(bf16[2,1344,256]{2,1,0:T(8,128)(2,1)} %get-tuple-element.58.refs_0_, bf16[3,3,768,256]{3,2,1,0:T(8,128)(2,1)} %get-tuple-element.59.refs_1_, bf16[3,768,256]{2,1,0:T(8,128)(2,1)} %get-tuple-element.60.refs_2_, ...), custom_call_target="tpu_custom_call" | custom-call | tf_op jit(solution)/shard_map/last_grads/pallas_call | solution.py:470
  360.3 5.0 %unpack.1 = (f32[192,768]{1,0:T(8,128)}, f32[192,2048]{1,0:T(8,128)}, f32[192,2048]{1,0:T(8,128)}, f32[512,768]{1,0:T(8,128)}, f32[192,768]{1,0:T(8,128)}, /*ind...) custom-call(bf16[5376,256]{1,0:T(8,128)(2,1)} %get-tuple-element.66.refs_0_, ...), custom_call_target="tpu_custom_call" | custom-call | tf_op jit(solution)/shard_map/unpack/pallas_call | solution.py:510
  365.3 3.2 copy.28

commit v5 on v4

--- a/solution.py
+++ b/solution.py
@@ -14,10 +14,12 @@
 OUTER = 4
 HEADS = H // OUTER
 HW = HEADS * DH
+HALF = 2 * HW
 BLK = 256
 AUG = DH + 16
 SPAN = 4 * BLK
 LANES = 256
+LANE = 128
 LOG2E = 1.4426950408889634
 LN2 = 0.6931471805599453
 F32 = jnp.float32
@@ -76,6 +78,11 @@
 
 def peers(n, z, x):
     return [lax.rem(z + d, OUTER) * n + x for d in range(1, OUTER)] + [z * n + lax.rem(x + s, n) for s in range(1, n)]
+
+
+def around(z):
+    near = z + 1 - 2 * lax.rem(z, 2)
+    return near, lax.rem(z + 2, OUTER), lax.rem(near + 2, OUTER)
 
 
 class Places:
@@ -97,28 +104,39 @@
 
 
 class Rows:
-    def __init__(self, places, shapes):
+    def __init__(self, places, shapes, lanes, lines):
         self.p = places
         self.shapes = shapes
+        self.lanes = lanes
+        self.lines = range(lines)
         grain = places.inner * OUTER * 16
         self.blocks = []
         at = 0
         for m, (rows, columns) in enumerate(shapes):
             share = rows // places.dp
-            for block in range(columns // LANES):
+            for block in range(columns // lanes):
                 self.blocks.append((m, block, at, share))
                 at += share
         self.used = at
-        self.total = -(-at // (2 * grain)) * 2 * grain
-        self.half = self.total // 2
-        self.size = self.half // places.inner
-        self.small = self.size // OUTER
+        grains = max(-(-at // grain), lines)
+        self.total = grains * grain
+        cuts = [grains * line // lines * grain for line in range(lines + 1)]
+        self.start = cuts[:-1]
+        self.span = [b - a for a, b in zip(cuts[:-1], cuts[1:])]
+        self.size = [v // places.inner for v in self.span]
+        self.small = [v // OUTER for v in self.size]
+        self.part_start = [v // places.inner for v in self.start]
+        self.part_total = self.total // places.inner
+
+    def line(self, line):
+        return pl.ds(self.start[line], self.span[line])
 
     def part(self, line, x):
-        return pl.ds(pl.multiple_of(line * self.half + x * self.size, 16), self.size)
+        return pl.ds(pl.multiple_of(self.start[line] + x * self.size[line], 16), self.size[line])
 
     def quarter(self, line, x, z):
-        return pl.ds(pl.multiple_of(line * self.half + x * self.size + z * self.small, 16), self.small)
+        first = self.start[line] + x * self.size[line] + z * self.small[line]
+        return pl.ds(pl.multiple_of(first, 16), self.small[line])
 
 
 def add_to(ref, arrived):
@@ -135,22 +153,22 @@
     def __init__(self, rows, y_first):
         self.rows = rows
         self.y_first = y_first
+        self.count = 5 + 2 * len(rows.lines)
 
     def scratch(self):
         r, p, dma = self.rows, self.rows.p, pltpu.SemaphoreType.DMA
-        g, n = p.groups, p.inner
-        out = [pltpu.VMEM((g, r.total, LANES), BF16), pltpu.VMEM((g, r.total, LANES), BF16)]
-        for y_first in self.y_first:
-            out.append(pltpu.VMEM((g - 1, r.half if y_first else r.size, LANES), BF16))
-            out.append(pltpu.VMEM((n - 1, 1 if y_first else g, r.size, LANES), BF16))
-        return out + [dma((len(r.blocks), g, 3)), dma((2, g - 1, 2)), dma((2, n - 1, g, 2))]
-
-    count = 9
+        g, n, lines = p.groups, p.inner, len(r.lines)
+        out = [pltpu.VMEM((g, r.total, r.lanes), BF16), pltpu.VMEM((g, r.total, r.lanes), BF16)]
+        for line, y_first in enumerate(self.y_first):
+            out.append(pltpu.VMEM((g - 1, r.span[line] if y_first else r.size[line], r.lanes), BF16))
+            out.append(pltpu.VMEM((n - 1, 1 if y_first else g, r.size[line], r.lanes), BF16))
+        return out + [dma((len(r.blocks), g, 3)), dma((lines, g - 1, 2)), dma((lines, n - 1, g, 2))]
 
     def bind(self, grads, refs):
         self.grads = grads
-        self.held, self.land, self.c_sem, self.y_sem, self.x_sem = refs[0], refs[1], refs[6], refs[7], refs[8]
-        self.y_land, self.x_land = (refs[2], refs[4]), (refs[3], refs[5])
+        self.held, self.land = refs[:2]
+        self.c_sem, self.y_sem, self.x_sem = refs[-3:]
+        self.y_land, self.x_land = refs[2:-3:2], refs[3:-3:2]
         dp, seq = lax.axis_index("dp"), lax.axis_index("seq")
         n = self.rows.p.inner
         self.core, self.group = lax.rem(dp, 2), lax.div(dp, 2)
@@ -159,7 +177,7 @@
     def source(self, i, g, core):
         m, block, at, share = self.rows.blocks[i]
         first = pl.multiple_of((g * 2 + core) * share, 16)
-        return self.grads[m].at[pl.ds(first, share), pl.ds(block * LANES, LANES)], pl.ds(at, share)
+        return self.grads[m].at[pl.ds(first, share), pl.ds(block * self.rows.lanes, self.rows.lanes)], pl.ds(at, share)
 
     def picked(self, chosen):
         return [i for i, b in enumerate(self.rows.blocks) if chosen is None or b[0] in chosen]
@@ -181,7 +199,7 @@
         r = self.rows
         for t in range(1, r.p.groups):
             other = lax.rem(self.group + t, r.p.groups)
-            where = pl.ds(line * r.half, r.half) if self.y_first[line] else r.part(line, self.x)
+            where = r.line(line) if self.y_first[line] else r.part(line, self.x)
             sems = self.y_sem.at[line, t - 1, 0], self.y_sem.at[line, t - 1, 1]
             yield remote(self.held.at[other, where], self.y_land[line].at[t - 1], sems, dp=other * 2 + self.core)
 
@@ -206,21 +224,26 @@
         for c in self.own_copies(chosen):
             c.start()
 
-    def step_first(self):
+    def step_first(self, begin):
         r = self.rows
         for c in self.core_copies():
             c.wait_recv()
         for c in self.own_copies():
             c.wait()
-        for line in range(2):
+        for line in r.lines:
+            end = r.start[line] + r.span[line]
+            first, last = r.start[line], min(end, r.used)
             for g in range(r.p.groups):
-                first, last = line * r.half, min((line + 1) * r.half, r.used)
                 where = pl.ds(first, last - first)
                 add_to(self.held.at[g, where], [self.land[g, where]])
-                if last < (line + 1) * r.half:
-                    self.held[g, last : (line + 1) * r.half] = jnp.zeros(((line + 1) * r.half - last, LANES), BF16)
-            for c in self.hop(line, 0):
-                c.start()
+                if last < end:
+                    self.held[g, last:end] = jnp.zeros((end - last, r.lanes), BF16)
+            if line in begin:
+                self.start_first(line)
+
+    def start_first(self, line):
+        for c in self.hop(line, 0):
+            c.start()
 
     def step_second(self, line):
         r = self.rows
@@ -228,7 +251,7 @@
             c.wait_recv()
         if self.y_first[line]:
             arrived = [self.y_land[line][t] for t in range(r.p.groups - 1)]
-            add_to(self.held.at[self.group, pl.ds(line * r.half, r.half)], arrived)
+            add_to(self.held.at[self.group, r.line(line)], arrived)
         else:
             for g in range(r.p.groups):
                 arrived = [self.x_land[line][s, g] for s in range(r.p.inner - 1)]
@@ -252,36 +275,33 @@
     def end(self):
         for c in self.core_copies():
             c.wait_send()
-        for line in range(2):
+        for line in self.rows.lines:
             for which in range(2):
                 for c in self.hop(line, which):
                     c.wait_send()
 
 
 class Spread:
-    def __init__(self, rows):
+    def __init__(self, rows, halves=False):
         self.rows = rows
+        self.halves = halves
 
     def scratch(self):
         r, dma = self.rows, pltpu.SemaphoreType.DMA
-        return [
-            pltpu.VMEM((2, 3, r.small, LANES), BF16),
-            dma((2, 3, 2)),
-            dma((2, 3, 2)),
-            dma((2, OUTER, r.p.inner - 1, 2)),
-        ]
+        lines = len(r.lines)
+        land = (lines, 1, max(r.size) // 2, r.lanes) if self.halves else (lines, 3, max(r.small), r.lanes)
+        sems = dma((lines, 3, 2))
+        return [pltpu.VMEM(land, BF16), sems, sems, dma((lines, OUTER, r.p.inner - 1, 2))]
 
     count = 4
 
-    def bind(self, piece, full, refs):
-        self.piece, self.full = piece, full
+    def bind(self, piece, target, refs):
+        self.piece, self.target = piece, target
         self.land, self.s_sem, self.g_sem, self.x_sem = refs
         seq = lax.axis_index("seq")
         n = self.rows.p.inner
         self.z, self.x = lax.div(seq, n), lax.rem(seq, n)
-        self.near = self.z + 1 - 2 * lax.rem(self.z, 2)
-        self.two = lax.rem(self.z + 2, OUTER)
-        self.across = lax.rem(self.near + 2, OUTER)
+        self.near, self.two, self.across = around(self.z)
 
     def copy(self, src, dst, sems, group):
         return remote(src, dst, sems, seq=group * self.rows.p.inner + self.x)
@@ -289,19 +309,26 @@
     def sum_copy(self, line, i):
         piece = self.piece(line, (self.near, self.across, self.two)[i])
         sems = self.s_sem.at[line, i, 0], self.s_sem.at[line, i, 1]
-        return self.copy(piece, self.land.at[line, i], sems, self.two if i == 2 else self.near)
+        return self.copy(piece, self.landing(line, i), sems, self.two if i == 2 else self.near)
+
+    def landing(self, line, i):
+        rows = self.rows.size[line] // 2 if self.halves else self.rows.small[line]
+        return self.land.at[line, i, pl.ds(0, rows)]
+
+    def sums(self, line):
+        return [self.sum_copy(line, i) for i in range(1 if self.halves else 3)]
 
     def z_copy(self, line, i):
-        where = self.rows.quarter(line, self.x, self.two if i == 2 else self.z)
+        where = self.target(line, self.two if i == 2 else self.z)
         sems = self.g_sem.at[line, i, 0], self.g_sem.at[line, i, 1]
-        return self.copy(self.full.at[where], self.full.at[where], sems, self.two if i == 0 else self.near)
+        return self.copy(where, where, sems, self.two if i == 0 else self.near)
 
     def x_copies(self, line, c):
         n = self.rows.p.inner
-        where = self.rows.quarter(line, self.x, c)
+        where = self.target(line, c)
         for s in range(1, n):
             sems = self.x_sem.at[line, c, s - 1, 0], self.x_sem.at[line, c, s - 1, 1]
-            yield remote(self.full.at[where], self.full.at[where], sems, seq=self.z * n + lax.rem(self.x + s, n))
+            yield remote(where, where, sems, seq=self.z * n + lax.rem(self.x + s, n))
 
     def spread(self, line, c):
         for s in self.x_copies(line, c):
@@ -309,18 +336,19 @@
 
     def step_pair(self, line):
         self.sum_copy(line, 0).start()
-        self.sum_copy(line, 1).start()
+        if not self.halves:
+            self.sum_copy(line, 1).start()
 
     def step_two(self, line):
         for i, c in ((0, self.z), (1, self.two)):
             self.sum_copy(line, i).wait_recv()
-            add_to(self.piece(line, c), [self.land[line, i]])
+            add_to(self.piece(line, c), [self.landing(line, i)[...]])
         self.sum_copy(line, 2).start()
 
     def step_back(self, line):
-        self.sum_copy(line, 2).wait_recv()
-        where = self.rows.quarter(line, self.x, self.z)
-        self.full[where] = self.piece(line, self.z)[...] + self.land[line, 2]
+        last = 0 if self.halves else 2
+        self.sum_copy(line, last).wait_recv()
+        self.target(line, self.z)[...] = self.piece(line, self.z)[...] + self.landing(line, last)[...]
         self.z_copy(line, 0).start()
         self.z_copy(line, 1).start()
         self.spread(line, self.z)
@@ -337,13 +365,14 @@
         self.spread(line, self.across)
 
     def end(self):
-        for line in range(2):
+        for line in self.rows.lines:
             for c in range(OUTER):
                 for s in self.x_copies(line, c):
                     s.wait_send()
                     s.wait_recv()
+            for c in self.sums(line):
+                c.wait_send()
             for i in range(3):
-                self.sum_copy(line, i).wait_send()
                 self.z_copy(line, i).wait_send()
 
 
@@ -366,47 +395,66 @@
 
 
 def last_kernel(early, late, *refs):
-    count = 11
+    count = 13
     sources, (gain_ref, ffn_ref), refs = refs[:count], refs[count : count + 2], refs[count + 2 :]
     grad_in, full_early, full_late, refs = refs[0], refs[1], refs[2], refs[3:]
     slots, load_sem, refs = refs[:count], refs[count], refs[count + 1 :]
-    loads = [pltpu.make_async_copy(src, dst, load_sem.at[i]) for i, (src, dst) in enumerate(zip(sources, slots))]
+    p = late.p
+    scatter, spread_early, spread_late = Scatter(late, (True, False)), Spread(early), Spread(late, True)
+    (gq, gk, gv, small, arriving, n_sem), refs = refs[:6], refs[6:]
+    scatter.bind((gq, gk, gv, small), refs[: scatter.count])
+    refs = refs[scatter.count :]
+    z, x = scatter.z, scatter.x
+    columns = half_columns(z)
+    loads = []
+    for i, (src, dst) in enumerate(zip(sources, slots)):
+        loads.append(pltpu.make_async_copy(src.at[:, columns] if 3 <= i < 6 else src, dst, load_sem.at[i]))
     for c in loads:
         c.start()
-    held, grads, normed_t, wq_ref, wk_ref, wv_ref, x_ref, mixed_ref, near, far_sum, onehot = slots
-    gq, gk, gv, small, refs = refs[0], refs[1], refs[2], refs[3], refs[4:]
-    p = late.p
-    scatter, spread_early, spread_late = Scatter(late, (True, False)), Spread(early), Spread(late)
-    scatter.bind((gq, gk, gv, small), refs[: Scatter.count])
-    refs = refs[Scatter.count :]
+    held, grads, normed_t, wq_ref, wk_ref, wv_ref, x_ref, mixed_ref, near, far_sum, onehot, other, leaving = slots
 
     def early_piece(line, c):
-        return held.at[line, pl.ds(pl.multiple_of(c * early.small, 16), early.small)]
-
-    def late_piece(line, c):
-        return scatter.held.at[scatter.group, late.quarter(line, scatter.x, c)]
-
-    spread_early.bind(early_piece, full_early, refs[: Spread.count])
-    spread_late.bind(late_piece, full_late, refs[Spread.count :])
+        first = pl.multiple_of(early.part_start[line] + c * early.small[line], 16)
+        return held.at[pl.ds(first, early.small[line])]
+
+    def late_rows(line, c):
+        size = late.size[line] // 2
+        first = late.start[line] + x * late.size[line] + lax.rem(c, 2) * size
+        return pl.ds(pl.multiple_of(first, 16), size)
+
+    spread_early.bind(early_piece, lambda line, c: full_early.at[early.quarter(line, x, c)], refs[: Spread.count])
+    spread_late.bind(
+        lambda line, c: scatter.held.at[scatter.group, late_rows(line, c)],
+        lambda line, c: full_late.at[lax.div(c, 2), late_rows(line, c)],
+        refs[Spread.count :],
+    )
+    two = spread_early.two
+    n_copy = remote(leaving, arriving, (n_sem.at[0], n_sem.at[1]), seq=two * p.inner + x)
     greet_all(p)
     loads[0].wait()
-    for line in range(2):
+    loads[-1].wait()
+    n_copy.start()
+    for line in early.lines:
         spread_early.step_pair(line)
-    for c in loads[1:]:
+    for c in loads[1:-1]:
         c.wait()
     batch, height, width = x_ref.shape
     for i, out in enumerate((gq, gk, gv)):
-        total = jnp.zeros((width, width), F32)
+        total = jnp.zeros((width, HALF), F32)
         for b in range(batch):
-            total = total + lax.dot_general(normed_t[b], grads[i, b], NT, preferred_element_type=F32)
+            for block in range(2):
+                total = total + lax.dot_general(normed_t[block, b], grads[i, b, block], NT, preferred_element_type=F32)
         out[...] = total.astype(BF16)
         scatter.step_core((i,))
     gain = gain_ref[...]
     gain_sum = jnp.zeros((1, width), F32)
     for b in range(batch):
-        back = jnp.dot(wq_ref[...], grads[0, b], preferred_element_type=F32)
-        back = back + jnp.dot(wk_ref[...], grads[1, b], preferred_element_type=F32)
-        back = (back + jnp.dot(wv_ref[...], grads[2, b], preferred_element_type=F32)).T
+        back = jnp.dot(wq_ref[...], grads[0, b, 0], preferred_element_type=F32)
+        back = back + jnp.dot(wk_ref[...], grads[1, b, 0], preferred_element_type=F32)
+        back = back + jnp.dot(wv_ref[...], grads[2, b, 0], preferred_element_type=F32)
+        if b == batch - 1:
+            n_copy.wait_recv()
+        back = (back + (arriving if b == batch - 1 else other.at[b])[...].astype(F32)).T
         values = x_ref[b]
         scale = lax.rsqrt(jnp.mean(values * values, axis=-1, keepdims=True) + epsilon)
         gain_sum = gain_sum + jnp.sum(back * values * scale, axis=0, keepdims=True)
@@ -417,8 +465,8 @@
     col = lax.broadcasted_iota(jnp.int32, (BLK, BLK), 1)
     flip = (row + col == BLK - 1).astype(F32)
     bucket = lax.broadcasted_iota(jnp.int32, (NB, 1), 0)
-    head_lane = lax.broadcasted_iota(jnp.int32, (NB, LANES), 1)
-    table = jnp.zeros((NB, LANES), F32)
+    head_lane = lax.broadcasted_iota(jnp.int32, (NB, LANE), 1)
+    table = jnp.zeros((NB, LANE), F32)
     for h in range(HEADS):
         line = jnp.zeros((1, SPAN), F32)
         for off in (-1, 0, 1):
@@ -429,57 +477,73 @@
         column = jnp.sum(onehot[...] * line, axis=1, keepdims=True)
         sides = jnp.sum(far_sum[h], axis=1, keepdims=True)
         column = column + jnp.where(bucket == NB // 2 - 1, sides[0:1], 0.0) + jnp.where(bucket == NB - 1, sides[1:2], 0.0)
-        table = jnp.where(head_lane == scatter.z * HEADS + h, column, table)
+        table = jnp.where(head_lane == z * HEADS + h, column, table)
     share, buckets = width // p.dp, NB // p.dp
     for i in range(p.dp):
-        block = [v[:, i * share : (i + 1) * share] for v in (gain_sum, ffn_ref[...])]
-        block = [jnp.concatenate([v, jnp.zeros((1, LANES - share), F32)], axis=1) for v in block]
-        block += [table[i * buckets : (i + 1) * buckets], jnp.zeros((SMALL - 2 - buckets, LANES), F32)]
+        block = []
+        for v in (gain_sum, ffn_ref[...]):
+            for first, last in gain_rows(share):
+                v_row = v[:, i * share + first : i * share + last]
+                block.append(jnp.concatenate([v_row, jnp.zeros((1, LANE - (last - first)), F32)], axis=1) if last - first < LANE else v_row)
+        block.append(table[i * buckets : (i + 1) * buckets])
+        block.append(jnp.zeros((SMALL - 2 * len(gain_rows(share)) - buckets, LANE), F32))
         small[i * SMALL : (i + 1) * SMALL] = jnp.concatenate(block, axis=0).astype(BF16)
     scatter.step_core((3,))
-    for line in range(2):
+    for line in early.lines:
         spread_early.step_two(line)
-    scatter.step_first()
-    for line in range(2):
+    scatter.step_first(late.lines)
+    for line in early.lines:
         spread_early.step_back(line)
-    for line in range(2):
+    for line in late.lines:
         scatter.step_second(line)
-    for line in range(2):
+    for line in early.lines:
         spread_early.step_rest(line)
-    for line in range(2):
+    for line in late.lines:
         scatter.step_third(line)
         spread_late.step_pair(line)
-    for line in range(2):
+    for line in early.lines:
         spread_early.step_last(line)
-    for line in range(2):
-        spread_late.step_two(line)
-    for line in range(2):
+    for line in late.lines:
         spread_late.step_back(line)
-    for line in range(2):
+    for line in late.lines:
         spread_late.step_rest(line)
-    for line in range(2):
+    for line in late.lines:
         spread_late.step_last(line)
+    n_copy.wait_send()
     spread_early.end()
     spread_late.end()
     scatter.end()
 
 
+def gain_rows(share):
+    return [(at, min(at + LANE, share)) for at in range(0, share, LANE)]
+
+
+def half_columns(z):
+    return pl.ds(pl.multiple_of(lax.div(z, 2) * HALF, LANE), HALF)
+
+
 def last_grads(early, late, loaded, gain, ffn):
     inputs = loaded[6]
     width = inputs.shape[-1]
+    shapes = [(width, HALF) if 3 <= i < 6 else v.shape for i, v in enumerate(loaded)]
     return pl.pallas_call(
         functools.partial(last_kernel, early, late),
         in_specs=[anywhere()] * len(loaded) + [whole()] * 2,
         out_specs=[whole()] * 3,
-        out_shape=[jax.ShapeDtypeStruct(inputs.shape, F32)]
-        + [jax.ShapeDtypeStruct((r.total, LANES), BF16) for r in (early, late)],
-        scratch_shapes=[pltpu.VMEM(v.shape, v.dtype) for v in loaded]
+        out_shape=[
+            jax.ShapeDtypeStruct(inputs.shape, F32),
+            jax.ShapeDtypeStruct((early.total, early.lanes), BF16),
+            jax.ShapeDtypeStruct((2, late.total, late.lanes), BF16),
+        ],
+        scratch_shapes=[pltpu.VMEM(shape, v.dtype) for shape, v in zip(shapes, loaded)]
         + [pltpu.SemaphoreType.DMA((len(loaded),))]
-        + [pltpu.VMEM((width, width), BF16)] * 3
-        + [pltpu.VMEM((late.p.dp * SMALL, LANES), BF16)]
+        + [pltpu.VMEM((width, HALF), BF16)] * 3
+        + [pltpu.VMEM((late.p.dp * SMALL, LANE), BF16)]
+        + [pltpu.VMEM(loaded[-1].shape, BF16), pltpu.SemaphoreType.DMA((2,))]
         + Scatter(late, (True, False)).scratch()
         + Spread(early).scratch()
-        + Spread(late).scratch(),
+        + Spread(late, True).scratch(),
         compiler_params=pltpu.CompilerParams(
             vmem_limit_bytes=VMEM_BYTES, collective_id=2, has_side_effects=True
         ),
@@ -487,34 +551,38 @@
     )(*loaded, gain.reshape(1, -1), ffn.reshape(1, -1))
 
 
-def unpack_kernel(all_rows, *refs):
-    fulls, outs = refs[: len(all_rows)], list(refs[len(all_rows) :])
-    *_, (_, _, first, _) = all_rows[-1].blocks
-    share = outs[-3].shape[1]
-    buckets, heads = outs[-1].shape
-    outs[-3][...] = fulls[-1][first : first + SMALL].astype(F32)[0:1, :share]
-    outs[-2][...] = fulls[-1][first : first + SMALL].astype(F32)[1:2, :share]
-    outs[-1][...] = fulls[-1][first : first + SMALL].astype(F32)[2 : 2 + buckets, :heads]
-    outs = outs[:-3] + [None]
-    for rows, full in zip(all_rows, fulls):
-        for m, block, at, share in rows.blocks:
-            if outs[m] is not None:
-                outs[m][:, block * LANES : (block + 1) * LANES] = full[at : at + share].astype(F32)
-        outs = outs[len(rows.shapes) :]
-
-
-def unpack(all_rows, fulls, width):
-    dp = all_rows[0].p.dp
-    shapes = [(height // dp, columns) for r in all_rows for height, columns in r.shapes][:-1]
-    shapes += [(1, width // dp)] * 2 + [(NB // dp, H)]
+def unpack_kernel(early, late, full_early, full_late, *outs):
+    for m, block, at, share in early.blocks:
+        outs[m][:, block * LANES : (block + 1) * LANES] = full_early[at : at + share].astype(F32)
+    outs = outs[len(early.shapes) :]
+    for m, block, at, share in late.blocks[:-1]:
+        for half in range(2):
+            first = half * HALF + block * LANE
+            outs[m][:, first : first + LANE] = full_late[half, at : at + share].astype(F32)
+    *_, (_, _, first, _) = late.blocks
+    d_attn, d_ffn, d_table = outs[len(late.shapes) - 1 :]
+    small = full_late[0, first : first + SMALL].astype(F32) + full_late[1, first : first + SMALL].astype(F32)
+    at = 0
+    for out in (d_attn, d_ffn):
+        for begin, end in gain_rows(out.shape[1]):
+            out[:, begin:end] = small[at : at + 1, : end - begin]
+            at += 1
+    buckets, heads = d_table.shape
+    d_table[...] = small[at : at + buckets, :heads]
+
+
+def unpack(early, late, full_early, full_late, width):
+    dp = early.p.dp
+    shapes = [(height // dp, columns) for height, columns in early.shapes]
+    shapes += [(width // dp, width)] * 3 + [(1, width // dp)] * 2 + [(NB // dp, H)]
     return pl.pallas_call(
-        functools.partial(unpack_kernel, all_rows),
-        in_specs=[whole()] * len(fulls),
+        functools.partial(unpack_kernel, early, late),
+        in_specs=[whole()] * 2,
         out_specs=[whole()] * len(shapes),
         out_shape=[jax.ShapeDtypeStruct(s, F32) for s in shapes],
         compiler_params=params(),
         name="unpack",
-    )(*fulls)
+    )(full_early, full_late)
 
 
 def greet(n, z, x):
@@ -548,8 +616,8 @@
 def forward_kernel(
     n, len_ref, table_ref, onehot_ref, x_ref, gain_ref, wq_ref, wk_ref, wv_ref,
     normed_ref, own, pair, att, o_ref, lse_ref, tile_ref, far_ref,
-    send, ka, qa, va,
-    z_send, z_recv, x_send, x_recv, o_send, o_recv,
+    here, there, send, ka, qa, va,
+    n_send, n_recv, z_send, z_recv, x_send, x_recv, o_send, o_recv,
 ):
     nk = OUTER * n
     batch = x_ref.shape[0]
@@ -558,17 +626,23 @@
     z, x = lax.div(me, n), lax.rem(me, n)
     greet(n, z, x)
 
-    def z_copy(u, d):
-        group = lax.rem(z + d, OUTER)
-        sems = z_send.at[u, d - 1], z_recv.at[u, d - 1]
-        return remote(send.at[u, group], own.at[u, z], sems, seq=group * n + x)
-
-    def x_copy(u, s, d):
-        group = lax.rem(z + OUTER - d, OUTER)
+    near, two, across = around(z)
+    groups = (z, two, near, across)
+    low = lax.rem(z, 2) == 0
+    columns = half_columns(z)
+
+    def n_copy(b):
+        return remote(here.at[b], there.at[b], (n_send.at[b], n_recv.at[b]), seq=two * n + x)
+
+    def z_copy(u, i):
+        sems = z_send.at[u, i], z_recv.at[u, i]
+        return remote(send.at[u, i], own.at[u, groups[i]], sems, seq=near * n + x)
+
+    def x_copy(u, s, i):
         rows = pl.ds(DH, 2 * DH)
+        sems = x_send.at[s - 1, u, i], x_recv.at[s - 1, u, i]
         peer = z * n + lax.rem(x + s, n)
-        sems = x_send.at[s - 1, u, d], x_recv.at[s - 1, u, d]
-        return remote(own.at[u, group, rows], pair.at[s - 1, u, group], sems, seq=peer)
+        return remote(own.at[u, groups[i], rows], pair.at[s - 1, u, groups[i]], sems, seq=peer)
 
     def o_copy(u, d):
         group = lax.rem(z + d, OUTER)
@@ -580,21 +654,32 @@
     for b in range(batch):
         values = x_ref[b]
         scale = lax.rsqrt(jnp.mean(values * values, axis=-1, keepdims=True) + epsilon)
-        normed = (values * scale * gain_ref[...]).astype(BF16)
-        normed_ref[b] = normed.T
-        for i, (w_ref, factor) in enumerate(((wq_ref, LOG2E), (wk_ref, 1.0), (wv_ref, 1.0))):
-            turned = (jnp.dot(normed, w_ref[...], preferred_element_type=F32) * factor).T.astype(BF16)
-            for g in range(OUTER):
-                for h in range(HEADS):
-                    first = (g * HEADS + h) * DH
-                    send[b * HEADS + h, g, i * DH : (i + 1) * DH] = turned[first : first + DH]
+        here[b] = (values * scale * gain_ref[...]).astype(BF16)
+        if b == 0:
+            n_copy(0).start()
+
+    def project(b, i):
+        normed = (here, there)[i][b]
+        normed_ref[i, b] = normed.T
+        for m, (w_ref, factor) in enumerate(((wq_ref, LOG2E), (wk_ref, 1.0), (wv_ref, 1.0))):
+            turned = (jnp.dot(normed, w_ref[:, columns], preferred_element_type=F32) * factor).T.astype(BF16)
+            for h in range(HEADS):
+                first, second = turned[h * DH : (h + 1) * DH], turned[HW + h * DH : HW + (h + 1) * DH]
+                rows = slice(m * DH, (m + 1) * DH)
+                own[b * HEADS + h, groups[i], rows] = jnp.where(low, first, second)
+                send[b * HEADS + h, i, rows] = jnp.where(low, second, first)
         for h in range(HEADS):
-            u = b * HEADS + h
-            for d in (2, 1, 3):
-                z_copy(u, d).start()
-            own[u, z] = send[u, z]
             for s in range(1, n):
-                x_copy(u, s, 0).start()
+                x_copy(b * HEADS + h, s, i).start()
+
+    def start_near(b, i):
+        for h in range(HEADS):
+            z_copy(b * HEADS + h, i).start()
+
+    for b in range(batch):
+        project(b, 0)
+        if b == 0:
+            start_near(0, 0)
 
     head_lane = lax.broadcasted_iota(jnp.int32, (NB, H), 1)
     for h in range(HEADS):
@@ -615,8 +700,8 @@
         one = jnp.ones((1, BLK), F32)
         vtail = tail(BLK, (one,)).astype(BF16)
         for s in range(1, n):
-            for d in range(OUTER):
-                x_copy(u, s, d).wait_recv()
+            for i in range(OUTER):
+                x_copy(u, s, i).wait_recv()
         for s in range(n):
             col = lax.rem(x + s, n)
             for j in range(OUTER):
@@ -658,16 +743,43 @@
             lse_ref[u, j] = tops[j] + jnp.log2(weight)
         rows = pl.ds(pl.multiple_of((z * HEADS + h) * DH, DH), DH)
         att[b, rows] = o_ref[u, z]
+        @pl.when(u >= held_back)
+        def _():
+            start_o(u)
+
+    held_back = units - HEADS - 1
+
+    def start_o(u):
         for d in (2, 1, 3):
             o_copy(u, d).start()
 
     def turn(u, carry):
+        @pl.when(jnp.logical_and(u < units, lax.rem(u, HEADS) == 0))
+        def _():
+            b = lax.div(u, HEADS)
+            n_copy(b).wait_recv()
+
+            @pl.when(b == batch - 1)
+            def _():
+                lax.fori_loop(0, held_back, lambda u, c: (start_o(u), c)[1], 0)
+
+            @pl.when(b + 1 < batch)
+            def _():
+                n_copy(b + 1).start()
+
+            project(b, 1)
+            start_near(b, 1)
+
+            @pl.when(b + 1 < batch)
+            def _():
+                start_near(b + 1, 0)
+
         @pl.when(u < units)
         def _():
-            for d in (1, 3, 2):
-                z_copy(u, d).wait_recv()
+            for i in range(2):
+                z_copy(u, i).wait_recv()
                 for s in range(1, n):
-                    x_copy(u, s, d).start()
+                    x_copy(u, s, 2 + i).start()
 
         @pl.when(u > 0)
         def _():
@@ -679,15 +791,18 @@
 
     def finish(u, carry):
         for d in range(1, OUTER):
-            z_copy(u, d).wait_send()
             o_copy(u, d).wait_send()
             o_copy(u, d).wait_recv()
+        for i in range(2):
+            z_copy(u, i).wait_send()
         for s in range(1, n):
-            for d in range(OUTER):
-                x_copy(u, s, d).wait_send()
+            for i in range(OUTER):
+                x_copy(u, s, i).wait_send()
         return carry
 
     lax.fori_loop(0, units, finish, 0)
+    for b in range(batch):
+        n_copy(b).wait_send()
 
 
 def attention_forward(n, lengths, table, onehot, inputs, gain, wq, wk, wv):
@@ -699,7 +814,7 @@
         in_specs=[smem()] + [whole()] * 7,
         out_specs=[whole()] * 8,
         out_shape=[
-            jax.ShapeDtypeStruct((batch, width, height), BF16),
+            jax.ShapeDtypeStruct((2, batch, width, height), BF16),
             jax.ShapeDtypeStruct((units, OUTER, 3 * DH, BLK), BF16),
             jax.ShapeDtypeStruct((n - 1, units, OUTER, 2 * DH, BLK), BF16),
             jax.ShapeDtypeStruct((batch, width, height), BF16),
@@ -709,12 +824,16 @@
             jax.ShapeDtypeStruct((HEADS, 2, 1, BLK), F32),
         ],
         scratch_shapes=[
-            pltpu.VMEM((units, OUTER, 3 * DH, BLK), BF16),
+            pltpu.VMEM((batch, height, width), BF16),
+            pltpu.VMEM((batch, height, width), BF16),
+            pltpu.VMEM((units, 2, 3 * DH, BLK), BF16),
             pltpu.VMEM((nk, BLK, AUG), BF16),
             pltpu.VMEM((3, OUTER, AUG, BLK), BF16),
             pltpu.VMEM((AUG, nk * BLK), BF16),
-            dma((units, OUTER - 1)),
-            dma((units, OUTER - 1)),
+            dma((batch,)),
+            dma((batch,)),
+            dma((units, 2)),
+            dma((units, 2)),
             dma((n - 1, units, OUTER)),
             dma((n - 1, units, OUTER)),
             dma((units, OUTER - 1)),
@@ -728,25 +847,36 @@
     )(lengths, table, onehot, inputs, gain.reshape(1, -1), wq, wk, wv)
 
 
+def early_scatter(early):
+    return Scatter(early, (True,) * len(early.lines))
+
+
 def backward_kernel(
     n, early, len_ref, far_ref, tile_ref, own, pair, o_ref, lse_ref, dout, *refs
 ):
+    scatter = early_scatter(early)
     count = len(early.shapes)
     weights, refs = refs[:count], refs[count:]
-    (grads, near, far_sum, parts, own_slot, pair_slot, load_sem,
+    projections, refs = refs[:3], refs[3:]
+    (grads, near, far_sum, parts, other, leaving, w_half, other_out, w_sem, n_send, n_recv, own_slot, pair_slot, load_sem,
     do_land, x_out, x_land, z_out, kept,
     ka, kt, va, qa, da, dk_all, dv_all,
-    d_send, d_recv, x_send, x_recv, z_send, z_recv) = refs[: -Scatter.count]
-    scatter = Scatter(early, (True, True))
-    scatter.bind(weights, refs[-Scatter.count :])
+    d_send, d_recv, x_send, x_recv, z_send, z_recv) = refs[: -scatter.count]
+    scatter.bind(weights, refs[-scatter.count :])
     nk = OUTER * n
     batch = dout.shape[0]
     units = batch * HEADS
     x_slots, z_slots = staging(n, units)
     me = lax.axis_index("seq")
     z, x = lax.div(me, n), lax.rem(me, n)
+    near_z, two, across = around(z)
+    low = lax.rem(z, 2) * HW
     greet_all(early.p)
     scatter.step_core()
+    columns = half_columns(z)
+    w_loads = [pltpu.make_async_copy(w.at[:, columns], w_half.at[m], w_sem.at[m]) for m, w in enumerate(projections)]
+    for c in w_loads:
+        c.start()
 
     def head_rows(group, h):
         return pl.ds(pl.multiple_of((group * HEADS + h) * DH, DH), DH)
@@ -760,14 +890,21 @@
     def x_copy(u, s):
         peer = z * n + lax.rem(x + s, n)
         sems = x_send.at[s - 1, u], x_recv.at[s - 1, u]
-        return remote(x_out.at[s - 1, lax.rem(u, x_slots)], x_land.at[s - 1, u], sems, seq=peer)
-
-    def z_copy(u, d, i):
-        group = lax.rem(z + d, OUTER)
+        return remote(
+            x_out.at[s - 1, lax.rem(u, x_slots)], x_land.at[s - 1, lax.rem(u, X_LAND)], sems, seq=peer
+        )
+
+    def half_rows(h):
+        return pl.ds(pl.multiple_of(low + h * DH, DH), DH)
+
+    def z_copy(u, i, m):
         b, h = lax.div(u, HEADS), lax.rem(u, HEADS)
-        sems = z_send.at[u, d - 1, i], z_recv.at[u, d - 1, i]
-        src, dst = z_out.at[lax.rem(u, z_slots), group, pl.ds(i * DH, DH)], grads.at[i, b, head_rows(z, h)]
-        return remote(src, dst, sems, seq=group * n + x)
+        sems = z_send.at[u, i, m], z_recv.at[u, i, m]
+        src, dst = z_out.at[lax.rem(u, z_slots), i, pl.ds(m * DH, DH)], grads.at[m, b, i, half_rows(h)]
+        return remote(src, dst, sems, seq=near_z * n + x)
+
+    def n_copy(b):
+        return remote(other_out.at[b], other.at[b], (n_send.at[b], n_recv.at[b]), seq=two * n + x)
 
     def loads(u):
         slot = lax.rem(u, 2)
@@ -778,9 +915,14 @@
     for c in loads(0):
         c.start()
 
-    def begin(u, carry):
+    def start_d(u):
         for d in (2, 1, 3):
             d_copy(u, d).start()
+
+    start_d(0)
+    start_d(1)
+
+    def begin(u, carry):
         do_land[u, z] = dout[lax.div(u, HEADS), head_rows(z, lax.rem(u, HEADS))]
         return carry
 
@@ -804,6 +946,10 @@
         def _():
             for c in loads(u + 1):
                 c.start()
+
+        @pl.when(u + 2 < units)
+        def _():
+            start_d(u + 2)
 
         for s in range(n):
             col = lax.rem(x + s, n)
@@ -859,12 +1005,6 @@
                     dk = dk + lax.dot_general(qa[0, j, :DH], dss[kb, j], NT, preferred_element_type=F32)
                 dk_all[kb] = dk * LN2
                 dv_all[kb] = dv
-        @pl.when(u >= z_slots)
-        def _():
-            for d in range(1, OUTER):
-                for i in range(3):
-                    z_copy(u - z_slots, d, i).wait_send()
-
         @pl.when(u >= x_slots)
         def _():
             for s in range(1, n):
@@ -872,13 +1012,13 @@
 
         far = jnp.zeros((8, BLK), F32)
         for j in range(OUTER):
-            z_out[lax.rem(u, z_slots), j, :DH] = dqs[j][:DH].astype(BF16)
             far = far + dqs[j][DH : DH + 8]
         far_sum[h] += far
         parity = lax.rem(u, 2)
         for j in range(OUTER):
-            kept[parity, j, :DH] = dk_all[n * j + x]
-            kept[parity, j, DH:] = dv_all[n * j + x]
+            kept[parity, j, :DH] = dqs[j][:DH]
+            kept[parity, j, DH : 2 * DH] = dk_all[n * j + x]
+            kept[parity, j, 2 * DH :] = dv_all[n * j + x]
             for s in range(1, n):
                 kb = n * j + lax.rem(x + s, n)
                 x_out[s - 1, lax.rem(u, x_slots), j, :DH] = dk_all[kb].astype(BF16)
@@ -891,42 +1031,84 @@
         parity = lax.rem(u, 2)
         for s in range(1, n):
             x_copy(u, s).wait_recv()
-        for j in range(OUTER):
-            total = kept[parity, j]
-            for s in range(1, n):
-                total = total + x_land[s - 1, u, j].astype(F32)
-            z_out[lax.rem(u, z_slots), j, DH:] = total.astype(BF16)
-        for i in range(3):
-            grads[i, b, head_rows(z, h)] = z_out[lax.rem(u, z_slots), z, i * DH : (i + 1) * DH]
-            for d in (2, 1, 3):
-                z_copy(u, d, i).start()
+
+        @pl.when(u >= z_slots)
+        def _():
+            for i in range(2):
+                for m in range(3):
+                    z_copy(u - z_slots, i, m).wait_send()
+
+        for i, (mine, theirs) in enumerate(((z, near_z), (two, across))):
+            for j, stays in ((mine, True), (theirs, False)):
+                rest = kept[parity, j, DH:]
+                for s in range(1, n):
+                    rest = rest + x_land[s - 1, lax.rem(u, X_LAND), j].astype(F32)
+                total = jnp.concatenate([kept[parity, j, :DH], rest], axis=0).astype(BF16)
+                if stays:
+                    for m in range(3):
+                        grads[m, b, i, half_rows(h)] = total[m * DH : (m + 1) * DH]
+                else:
+                    z_out[lax.rem(u, z_slots), i] = total
+            for m in range(3):
+                z_copy(u, i, m).start()
+
+    def combine(b):
+        for h in range(HEADS):
+            for i in range(2):
+                for m in range(3):
+                    z_copy(b * HEADS + h, i, m).wait_recv()
+        total = jnp.dot(w_half[0], grads[0, b, 1], preferred_element_type=F32)
+        total = total + jnp.dot(w_half[1], grads[1, b, 1], preferred_element_type=F32)
+        total = total + jnp.dot(w_half[2], grads[2, b, 1], preferred_element_type=F32)
+        @pl.when(b < batch - 1)
+        def _():
+            other_out[b] = total.astype(BF16)
+            n_copy(b).start()
+
+        @pl.when(b == batch - 1)
+        def _():
+            leaving[...] = total.astype(BF16)
 
     def turn(u, carry):
         @pl.when(u < units)
         def _():
             work(u)
 
-        @pl.when(u > 0)
+        @pl.when(jnp.logical_and(u > 0, u <= units))
         def _():
             hand_over(u - 1)
 
-        pl.when(u == 0)(scatter.step_first)
-        for line in range(2):
-            pl.when(u == 4 + 3 * line)(functools.partial(scatter.step_second, line))
+        @pl.when(jnp.logical_and(u > HEADS, lax.rem(u - 1, HEADS) == 0))
+        def _():
+            combine(lax.div(u - 1, HEADS) - 1)
+
+        @pl.when(u == 0)
+        def _():
+            scatter.step_first((0,))
+
+        for line in early.lines:
+
+            @pl.when(u == 2 * line + 2)
+            def _():
+                scatter.step_second(line)
+                if line + 1 < len(early.lines):
+                    scatter.start_first(line + 1)
 
         return carry
 
-    lax.fori_loop(0, units + 1, turn, 0)
+    for c in w_loads:
+        c.wait()
+    lax.fori_loop(0, units + 2, turn, 0)
 
     def finish(u, carry):
         for d in range(1, OUTER):
             d_copy(u, d).wait_send()
-            for i in range(3):
-                z_copy(u, d, i).wait_recv()
-
-                @pl.when(u >= units - z_slots)
-                def _():
-                    z_copy(u, d, i).wait_send()
+
+        @pl.when(u >= units - z_slots)
+        def _():
+            for i in range(2):
+                for m in range(3):
+                    z_copy(u, i, m).wait_send()
 
         @pl.when(u >= units - x_slots)
         def _():
@@ -936,9 +1118,12 @@
         return carry
 
     lax.fori_loop(0, units, finish, 0)
-    for line in range(2):
+    for b in range(batch - 1):
+        n_copy(b).wait_send()
+        n_copy(b).wait_recv()
+    for line in early.lines:
         scatter.step_third(line)
-        parts[line] = scatter.part(line)[...]
+        parts[early.part_start[line] : early.part_start[line] + early.size[line]] = scatter.part(line)[...]
     scatter.end()
 
 
@@ -946,30 +1131,40 @@
     return (units, units) if n <= 2 else (2, 4)
 
 
-def attention_backward(n, early, lengths, far, tiles, own, pair, out, lse, dout, weights):
+X_LAND = 4
+
+
+def attention_backward(n, early, lengths, far, tiles, own, pair, out, lse, dout, weights, projections):
     batch, width, height = dout.shape
     units, nk = batch * HEADS, n * OUTER
     dma = pltpu.SemaphoreType.DMA
     x_slots, z_slots = staging(n, units)
     return pl.pallas_call(
         functools.partial(backward_kernel, n, early),
-        in_specs=[smem()] + [whole()] * 2 + [anywhere()] * 2 + [whole()] * 3 + [anywhere()] * len(weights),
-        out_specs=[whole()] * 4,
+        in_specs=[smem()] + [whole()] * 2 + [anywhere()] * 2 + [whole()] * 3 + [anywhere()] * (len(weights) + 3),
+        out_specs=[whole()] * 6,
         out_shape=[
-            jax.ShapeDtypeStruct((3, batch, width, height), BF16),
+            jax.ShapeDtypeStruct((3, batch, 2, HALF, height), BF16),
             jax.ShapeDtypeStruct((HEADS, TILES, BLK, BLK), F32),
             jax.ShapeDtypeStruct((HEADS, 8, BLK), F32),
-            jax.ShapeDtypeStruct((2, early.size, LANES), BF16),
+            jax.ShapeDtypeStruct((early.part_total, LANES), BF16),
+            jax.ShapeDtypeStruct((batch - 1, width, height), BF16),
+            jax.ShapeDtypeStruct((width, height), BF16),
         ],
         scratch_shapes=[
+            pltpu.VMEM((3, width, HALF), BF16),
+            pltpu.VMEM((batch - 1, width, height), BF16),
+            dma((3,)),
+            dma((batch - 1,)),
+            dma((batch - 1,)),
             pltpu.VMEM((2, OUTER, 3 * DH, BLK), BF16),
             pltpu.VMEM((2, n - 1, OUTER, 2 * DH, BLK), BF16),
             dma((2, n)),
             pltpu.VMEM((units, OUTER, DH, BLK), BF16),
             pltpu.VMEM((n - 1, x_slots, OUTER, 2 * DH, BLK), BF16),
-            pltpu.VMEM((n - 1, units, OUTER, 2 * DH, BLK), BF16),
-            pltpu.VMEM((z_slots, OUTER, 3 * DH, BLK), BF16),
-            pltpu.VMEM((2, OUTER, 2 * DH, BLK), F32),
+            pltpu.VMEM((n - 1, X_LAND, OUTER, 2 * DH, BLK), BF16),
+            pltpu.VMEM((z_slots, 2, 3 * DH, BLK), BF16),
+            pltpu.VMEM((2, OUTER, 3 * DH, BLK), F32),
             pltpu.VMEM((nk, BLK, AUG), BF16),
             pltpu.VMEM((nk, DH, BLK), BF16),
             pltpu.VMEM((nk, BLK, AUG), BF16),
@@ -981,16 +1176,16 @@
             dma((units, OUTER - 1)),
             dma((n - 1, units)),
             dma((n - 1, units)),
-            dma((units, OUTER - 1, 3)),
-            dma((units, OUTER - 1, 3)),
+            dma((units, 2, 3)),
+            dma((units, 2, 3)),
         ]
-        + Scatter(early, (True, True)).scratch(),
+        + early_scatter(early).scratch(),
         compiler_params=pltpu.CompilerParams(
             vmem_limit_bytes=VMEM_BYTES, collective_id=1, has_side_effects=True
         ),
         cost_estimate=pl.CostEstimate(flops=110 * 10**9, bytes_accessed=24 << 20, transcendentals=0),
         name="attention_backward",
-    )(lengths, far, tiles, own, pair, out, lse, dout, *weights)
+    )(lengths, far, tiles, own, pair, out, lse, dout, *weights, *projections)
 
 
 FF_STEP = 512
@@ -1128,18 +1323,18 @@
     result, grad_mixed, grad_attended_t, grad_norm_ffn, weights = middle(
         inputs, attended_t, cotangent, norm_ffn, w_out, w_gate, w_up, w_down
     )
-    early = Rows(places, [g.shape for g in weights])
-    grads, near, far_sum, parts = attention_backward(
-        n, early, lengths, far, tiles, own, pair, out, lse, grad_attended_t, weights
+    early = Rows(places, [g.shape for g in weights], LANES, 4)
+    projections = (w_query, w_key, w_value)
+    grads, near, far_sum, parts, other, leaving = attention_backward(
+        n, early, lengths, far, tiles, own, pair, out, lse, grad_attended_t, weights, projections
     )
-    shapes = [w_query.shape, w_key.shape, w_value.shape, (places.dp * SMALL, LANES)]
-    late = Rows(places, shapes)
+    late = Rows(places, [(width, HALF)] * 3 + [(places.dp * SMALL, LANE)], LANE, 2)
     loaded = (
-        parts, grads, normed_t, w_query, w_key, w_value, inputs, grad_mixed, near, far_sum, onehot
+        parts, grads, normed_t, *projections, inputs, grad_mixed, near, far_sum, onehot, other, leaving
     )
     grad_inputs, full_early, full_late = last_grads(early, late, loaded, norm_attn, grad_norm_ffn)
     part_out, part_gate, part_up, part_down, part_query, part_key, part_value, part_attn, part_ffn, part_table = unpack(
-        (early, late), (full_early, full_late), width
+        early, late, full_early, full_late, width
     )
     return (
         result,

time: 375 us -> 359 us (0.957)
  Pallas kernels: 361 us -> 345 us
    pallas_call x1, Pallas kernels: 114 us -> 106 us  [attention_backward(): pl.pallas_call(functools.partial(backward_kernel, n, early), in_specs=[sm...]
    pallas_call x1, Pallas kernels: 118 us -> 112 us  [attention_forward(): pl.pallas_call(functools.partial(forward_kernel, n), in_specs=[smem()] +...]
where the time goes in v5:
time: 359 us; the launch traced here: 353 us
  Pallas kernels  345 us (96%)
  local copies, waits for them, and re-layouts  7.14 us (2%)
    pallas_call x1, Pallas kernels, attention_forward(): pl.pallas_call(functools.partial(forward_kernel, n), in_specs=[smem()] +...  112 us
    pallas_call x1, Pallas kernels, attention_backward(): pl.pallas_call(functools.partial(backward_kernel, n, early), in_specs=[sm...  106 us
    pallas_call x1, Pallas kernels, last_grads(): pl.pallas_call(functools.partial(last_kernel, early, late), in_specs=[any...  83.1 us
    pallas_call x1, Pallas kernels, middle(): pl.pallas_call(middle_kernel, in_specs=[whole()] * 4 + [anywhere()] * 4,...  38.7 us

profile of v5, /device:TPU:0, one launch (start us, length us, event | category | flops | bytes accessed | tf_op | source)
XLA Modules:
  0.0 353.3 jit_solution(17026329681868502355)
XLA Ops:
  0.6 1.3 reshape.50.gain_ref.refs_13_
  1.9 1.3 reshape.52.gain_ref
  3.2 1.4 copy.26.table_ref
  4.6 112.3 %attention_forward.1 = (bf16[2,3,768,256]{3,2,1,0:T(8,128)(2,1)}, bf16[9,4,192,256]{3,2,1,0:T(8,128)(2,1)}, bf16[1,9,4,128,256]{4,3,2,1,0:T(8,128)(2,1)}, bf16[3...) custom-call(s32[3]{0:T(128)} %len_ref.3, ...), custom_call_target="tpu_custom_call" | custom-call | flops 44999999488 | bytes 25165824 | tf_op jit(solution)/shard_map/attention_forward/pallas_call | solution.py:812
  116.9 38.7 %middle.1 = (f32[768,768]{1,0:T(8,128)}, f32[768,768]{1,0:T(8,128)}, bf16[3,768,256]{2,1,0:T(8,128)(2,1)}, f32[1,768]{1,0:T(1,128)}, bf16[768,768]{1,0:T(8,128)(...) custom-call(f32[768,768]{1,0:T(8,128)} %bitcast.6, ...), custom_call_target="tpu_custom_call" | custom-call | flops 24999999488 | bytes 33554432 | tf_op jit(solution)/shard_map/middle/pallas_call | solution.py:1277
  155.6 105.9 %attention_backward.1 = (bf16[3,3,2,384,256]{4,3,2,1,0:T(8,128)(2,1)}, f32[3,4,256,256]{3,2,1,0:T(8,128)}, f32[3,8,256]{2,1,0:T(8,128)}, bf16[2624,256]{1,0:T(8,...) custom-call(s32[3]{0:T(128)} %len_ref.3, f32[3,2,1,256]{3,2,1,0:T(1,128)} %get-tuple-element.49.far_ref, ...), custom_call_target="tpu_custom_call" | custom-call | flops 109999996928 | bytes 25165824 | tf_op jit(solution)/shard_map/attention_backward/pallas_call | solution.py:1142
  261.5 83.1 %last_grads.1 = (f32[3,256,768]{2,1,0:T(8,128)}, bf16[5248,256]{1,0:T(8,128)(2,1)}, bf16[2,1792,128]{2,1,0:T(8,128)(2,1)}) custom-call(bf16[2624,256]{1,0:T(8,128)(2,1)} %get-tuple-element.60.refs_0_, bf16[3,3,2,384,256]{4,3,2,1,0:T(8,128)(2,1)} %get-tuple-element.61.refs_1_, bf16[2,3,768,256]{3,2,1,0:T(8,128)(2,1)} %get-tuple-element.62.refs_2_, ...), custom_call_target="tpu_custom_call" | custom-call | tf_op jit(solution)/shard_map/last_grads/pallas_call | solution.py:530
  344.6 5.0 %unpack.1 = (f32[192,768]{1,0:T(8,128)}, f32[192,2048]{1,0:T(8,128)}, f32[192,2048]{1,0:T(8,128)}, f32[512,768]{1,0:T(8,128)}, f32[192,768]{1,0:T(8,128)}, /*ind...) custom-call(bf16[5248,256]{1,0:T(8,128)(2,1)} %get-tuple-element.70.full_early, ...), custom_call_target="tpu_custom_call" | custom-call | tf_op jit(solution)/shard_map/unpack/pallas_call | solution.py:578
  349.6 3.2 copy.28

commit v6 on v5

--- a/solution.py
+++ b/solution.py
@@ -376,6 +376,58 @@
                 self.z_copy(line, i).wait_send()
 
 
+class Total:
+    def __init__(self, places, rows):
+        self.p = places
+        self.rows = rows
+        self.peers = [1, places.groups - 1, places.inner - 1, 1, 1]
+        self.hops = range(5)
+        self.count = 8
+
+    def scratch(self):
+        dma = pltpu.SemaphoreType.DMA
+        out = [pltpu.VMEM((len(self.hops) + 1, self.rows, LANE), F32)]
+        out += [pltpu.VMEM((k, self.rows, LANE), F32) for k in self.peers]
+        return out + [dma((len(self.hops), max(self.peers))) for _ in range(2)]
+
+    def bind(self, refs):
+        self.held, self.land, self.sems = refs[0], refs[1:6], refs[6:]
+        dp, seq = lax.axis_index("dp"), lax.axis_index("seq")
+        n, groups = self.p.inner, self.p.groups
+        core, group, z, x = lax.rem(dp, 2), lax.div(dp, 2), lax.div(seq, n), lax.rem(seq, n)
+        near, two, _ = around(z)
+        self.targets = [
+            [{"dp": group * 2 + 1 - core}],
+            [{"dp": lax.rem(group + t, groups) * 2 + core} for t in range(1, groups)],
+            [{"seq": z * n + lax.rem(x + s, n)} for s in range(1, n)],
+            [{"seq": near * n + x}],
+            [{"seq": two * n + x}],
+        ]
+
+    def copies(self, hop):
+        for i, target in enumerate(self.targets[hop]):
+            yield remote(self.held.at[hop], self.land[hop].at[i], (self.sems[0].at[hop, i], self.sems[1].at[hop, i]), **target)
+
+    def send(self, hop):
+        for c in self.copies(hop):
+            c.start()
+
+    def step(self, hop):
+        for c in self.copies(hop):
+            c.wait_recv()
+        total = self.held[hop]
+        for i in range(self.peers[hop]):
+            total = total + self.land[hop][i]
+        self.held[hop + 1] = total
+        if hop + 1 < len(self.hops):
+            self.send(hop + 1)
+
+    def end(self):
+        for hop in self.hops:
+            for c in self.copies(hop):
+                c.wait_send()
+
+
 def greet_all(places):
     dp, seq = lax.axis_index("dp"), lax.axis_index("seq")
     n = places.inner
@@ -397,12 +449,12 @@
 def last_kernel(early, late, *refs):
     count = 13
     sources, (gain_ref, ffn_ref), refs = refs[:count], refs[count : count + 2], refs[count + 2 :]
-    grad_in, full_early, full_late, refs = refs[0], refs[1], refs[2], refs[3:]
+    grad_in, full_early, full_late, small_out, refs = refs[0], refs[1], refs[2], refs[3], refs[4:]
     slots, load_sem, refs = refs[:count], refs[count], refs[count + 1 :]
     p = late.p
     scatter, spread_early, spread_late = Scatter(late, (True, False)), Spread(early), Spread(late, True)
-    (gq, gk, gv, small, arriving, n_sem), refs = refs[:6], refs[6:]
-    scatter.bind((gq, gk, gv, small), refs[: scatter.count])
+    (gq, gk, gv, arriving, n_sem), refs = refs[:5], refs[5:]
+    scatter.bind((gq, gk, gv), refs[: scatter.count])
     refs = refs[scatter.count :]
     z, x = scatter.z, scatter.x
     columns = half_columns(z)
@@ -426,41 +478,72 @@
     spread_late.bind(
         lambda line, c: scatter.held.at[scatter.group, late_rows(line, c)],
         lambda line, c: full_late.at[lax.div(c, 2), late_rows(line, c)],
-        refs[Spread.count :],
+        refs[Spread.count : 2 * Spread.count],
     )
+    total_small = Total(p, p.dp * SMALL)
+    total_small.bind(refs[2 * Spread.count :])
     two = spread_early.two
     n_copy = remote(leaving, arriving, (n_sem.at[0], n_sem.at[1]), seq=two * p.inner + x)
     greet_all(p)
     loads[0].wait()
     loads[-1].wait()
     n_copy.start()
-    for line in early.lines:
+    early_lines, late_lines = list(early.lines), list(late.lines)
+    for line in early_lines[:2]:
         spread_early.step_pair(line)
     for c in loads[1:-1]:
         c.wait()
     batch, height, width = x_ref.shape
-    for i, out in enumerate((gq, gk, gv)):
+
+    def weight(i, out):
         total = jnp.zeros((width, HALF), F32)
         for b in range(batch):
             for block in range(2):
                 total = total + lax.dot_general(normed_t[block, b], grads[i, b, block], NT, preferred_element_type=F32)
         out[...] = total.astype(BF16)
         scatter.step_core((i,))
-    gain = gain_ref[...]
-    gain_sum = jnp.zeros((1, width), F32)
-    for b in range(batch):
+
+    for i, out in enumerate((gq, gk, gv)):
+        weight(i, out)
+    spread_early.step_two(0)
+    spread_early.step_pair(2)
+    scatter.step_first(late.lines)
+    spread_early.step_two(1)
+    spread_early.step_pair(3)
+    gain = gain_ref[...].reshape(1, -1)
+    gain_sums = []
+
+    def positions(b, arrived):
         back = jnp.dot(wq_ref[...], grads[0, b, 0], preferred_element_type=F32)
         back = back + jnp.dot(wk_ref[...], grads[1, b, 0], preferred_element_type=F32)
         back = back + jnp.dot(wv_ref[...], grads[2, b, 0], preferred_element_type=F32)
-        if b == batch - 1:
-            n_copy.wait_recv()
-        back = (back + (arriving if b == batch - 1 else other.at[b])[...].astype(F32)).T
+        back = (back + arrived[...].astype(F32)).T
         values = x_ref[b]
         scale = lax.rsqrt(jnp.mean(values * values, axis=-1, keepdims=True) + epsilon)
-        gain_sum = gain_sum + jnp.sum(back * values * scale, axis=0, keepdims=True)
+        gain_sums.append(jnp.sum(back * values * scale, axis=0, keepdims=True))
         u = back * gain
         along = jnp.mean(u * values, axis=-1, keepdims=True)
         grad_in[b] = mixed_ref[b] + scale * (u - values * (scale * scale * along))
+
+    positions(0, other.at[0])
+    spread_early.step_back(0)
+    spread_early.step_two(2)
+    for line in late_lines:
+        scatter.step_second(line)
+    for b in range(1, batch - 1):
+        positions(b, other.at[b])
+    spread_early.step_back(1)
+    spread_early.step_two(3)
+    for line in late_lines:
+        scatter.step_third(line)
+        spread_late.step_pair(line)
+    n_copy.wait_recv()
+    positions(batch - 1, arriving)
+    gain_sum = sum(gain_sums)
+    spread_early.step_rest(0)
+    spread_early.step_back(2)
+    for line in late_lines:
+        spread_late.step_back(line)
     row = lax.broadcasted_iota(jnp.int32, (BLK, BLK), 0)
     col = lax.broadcasted_iota(jnp.int32, (BLK, BLK), 1)
     flip = (row + col == BLK - 1).astype(F32)
@@ -484,31 +567,33 @@
         for v in (gain_sum, ffn_ref[...]):
             for first, last in gain_rows(share):
                 v_row = v[:, i * share + first : i * share + last]
-                block.append(jnp.concatenate([v_row, jnp.zeros((1, LANE - (last - first)), F32)], axis=1) if last - first < LANE else v_row)
+                if last - first < LANE:
+                    v_row = jnp.concatenate([v_row, jnp.zeros((1, LANE - (last - first)), F32)], axis=1)
+                block.append(v_row)
         block.append(table[i * buckets : (i + 1) * buckets])
         block.append(jnp.zeros((SMALL - 2 * len(gain_rows(share)) - buckets, LANE), F32))
-        small[i * SMALL : (i + 1) * SMALL] = jnp.concatenate(block, axis=0).astype(BF16)
-    scatter.step_core((3,))
-    for line in early.lines:
-        spread_early.step_two(line)
-    scatter.step_first(late.lines)
-    for line in early.lines:
-        spread_early.step_back(line)
-    for line in late.lines:
-        scatter.step_second(line)
-    for line in early.lines:
-        spread_early.step_rest(line)
-    for line in late.lines:
-        scatter.step_third(line)
-        spread_late.step_pair(line)
-    for line in early.lines:
-        spread_early.step_last(line)
-    for line in late.lines:
-        spread_late.step_back(line)
-    for line in late.lines:
+        total_small.held[0, i * SMALL : (i + 1) * SMALL] = jnp.concatenate(block, axis=0)
+    total_small.send(0)
+    spread_early.step_rest(1)
+    spread_early.step_back(3)
+    spread_early.step_last(0)
+    total_small.step(0)
+    for line in late_lines:
         spread_late.step_rest(line)
-    for line in late.lines:
+    spread_early.step_rest(2)
+    spread_early.step_last(1)
+    total_small.step(1)
+    for line in late_lines:
         spread_late.step_last(line)
+    spread_early.step_rest(3)
+    total_small.step(2)
+    spread_early.step_last(2)
+    total_small.step(3)
+    spread_early.step_last(3)
+    total_small.step(4)
+    mine = pl.ds(pl.multiple_of(lax.axis_index("dp") * SMALL, SMALL), SMALL)
+    small_out[...] = total_small.held[len(total_small.hops), mine]
+    total_small.end()
     n_copy.wait_send()
     spread_early.end()
     spread_late.end()
@@ -530,38 +615,37 @@
     return pl.pallas_call(
         functools.partial(last_kernel, early, late),
         in_specs=[anywhere()] * len(loaded) + [whole()] * 2,
-        out_specs=[whole()] * 3,
+        out_specs=[whole()] * 4,
         out_shape=[
             jax.ShapeDtypeStruct(inputs.shape, F32),
             jax.ShapeDtypeStruct((early.total, early.lanes), BF16),
             jax.ShapeDtypeStruct((2, late.total, late.lanes), BF16),
+            jax.ShapeDtypeStruct((SMALL, LANE), F32),
         ],
         scratch_shapes=[pltpu.VMEM(shape, v.dtype) for shape, v in zip(shapes, loaded)]
         + [pltpu.SemaphoreType.DMA((len(loaded),))]
         + [pltpu.VMEM((width, HALF), BF16)] * 3
-        + [pltpu.VMEM((late.p.dp * SMALL, LANE), BF16)]
         + [pltpu.VMEM(loaded[-1].shape, BF16), pltpu.SemaphoreType.DMA((2,))]
         + Scatter(late, (True, False)).scratch()
         + Spread(early).scratch()
-        + Spread(late, True).scratch(),
+        + Spread(late, True).scratch()
+        + Total(late.p, late.p.dp * SMALL).scratch(),
         compiler_params=pltpu.CompilerParams(
             vmem_limit_bytes=VMEM_BYTES, collective_id=2, has_side_effects=True
         ),
         name="last_grads",
-    )(*loaded, gain.reshape(1, -1), ffn.reshape(1, -1))
-
-
-def unpack_kernel(early, late, full_early, full_late, *outs):
+    )(*loaded, gain, ffn)
+
+
+def unpack_kernel(early, late, full_early, full_late, small, *outs):
     for m, block, at, share in early.blocks:
         outs[m][:, block * LANES : (block + 1) * LANES] = full_early[at : at + share].astype(F32)
     outs = outs[len(early.shapes) :]
-    for m, block, at, share in late.blocks[:-1]:
+    for m, block, at, share in late.blocks:
         for half in range(2):
             first = half * HALF + block * LANE
             outs[m][:, first : first + LANE] = full_late[half, at : at + share].astype(F32)
-    *_, (_, _, first, _) = late.blocks
-    d_attn, d_ffn, d_table = outs[len(late.shapes) - 1 :]
-    small = full_late[0, first : first + SMALL].astype(F32) + full_late[1, first : first + SMALL].astype(F32)
+    d_attn, d_ffn, d_table = outs[len(late.shapes) :]
     at = 0
     for out in (d_attn, d_ffn):
         for begin, end in gain_rows(out.shape[1]):
@@ -571,18 +655,18 @@
     d_table[...] = small[at : at + buckets, :heads]
 
 
-def unpack(early, late, full_early, full_late, width):
+def unpack(early, late, full_early, full_late, small, width):
     dp = early.p.dp
     shapes = [(height // dp, columns) for height, columns in early.shapes]
     shapes += [(width // dp, width)] * 3 + [(1, width // dp)] * 2 + [(NB // dp, H)]
     return pl.pallas_call(
         functools.partial(unpack_kernel, early, late),
-        in_specs=[whole()] * 2,
+        in_specs=[whole()] * 3,
         out_specs=[whole()] * len(shapes),
         out_shape=[jax.ShapeDtypeStruct(s, F32) for s in shapes],
         compiler_params=params(),
         name="unpack",
-    )(full_early, full_late)
+    )(full_early, full_late, small)
 
 
 def greet(n, z, x):
@@ -654,7 +738,7 @@
     for b in range(batch):
         values = x_ref[b]
         scale = lax.rsqrt(jnp.mean(values * values, axis=-1, keepdims=True) + epsilon)
-        here[b] = (values * scale * gain_ref[...]).astype(BF16)
+        here[b] = (values * scale * gain_ref[...].reshape(1, -1)).astype(BF16)
         if b == 0:
             n_copy(0).start()
 
@@ -681,17 +765,19 @@
         if b == 0:
             start_near(0, 0)
 
-    head_lane = lax.broadcasted_iota(jnp.int32, (NB, H), 1)
+    table_lane = lax.broadcasted_iota(jnp.int32, (1, NB), 1)
     for h in range(HEADS):
-        chosen = jnp.where(head_lane == z * HEADS + h, table_ref[...], 0.0)
-        column = jnp.sum(chosen, axis=1, keepdims=True) * LOG2E
-        line = jnp.broadcast_to(jnp.sum(onehot_ref[...] * column, axis=0, keepdims=True), (BLK, SPAN))
+        chosen = table_ref[pl.ds(z * HEADS + h, 1), :] * LOG2E
+        padded = jnp.broadcast_to(chosen, (8, NB))
+        line = jnp.dot(padded, onehot_ref[...], preferred_element_type=F32, precision=highest)[0:1]
+        line = jnp.broadcast_to(line, (BLK, SPAN))
         tile_ref[h, 0] = jnp.zeros((BLK, BLK), F32)
         for off in (-1, 0, 1):
             shift = (off * BLK - (2 * BLK - 1)) % SPAN
             tile_ref[h, off + 2] = pltpu.roll(line, shift, 1, stride=1, stride_axis=0)[:, :BLK]
-        far_ref[h, 0] = jnp.broadcast_to(column[NB // 2 - 1 : NB // 2], (1, BLK))
-        far_ref[h, 1] = jnp.broadcast_to(column[NB - 1 :], (1, BLK))
+        for side, bucket in enumerate((NB // 2 - 1, NB - 1)):
+            value = jnp.sum(jnp.where(table_lane == bucket, chosen, 0.0), axis=1, keepdims=True)
+            far_ref[h, side] = jnp.broadcast_to(value, (1, BLK))
 
     def attend(u):
         b, h = lax.div(u, HEADS), lax.rem(u, HEADS)
@@ -844,7 +930,7 @@
         ),
         cost_estimate=pl.CostEstimate(flops=45 * 10**9, bytes_accessed=24 << 20, transcendentals=0),
         name="attention_forward",
-    )(lengths, table, onehot, inputs, gain.reshape(1, -1), wq, wk, wv)
+    )(lengths, table, onehot, inputs, gain, wq, wk, wv)
 
 
 def early_scatter(early):
@@ -1218,7 +1304,7 @@
     kept[...] = mixed
     result[...] = mixed
     scale = lax.rsqrt(jnp.mean(mixed * mixed, axis=-1, keepdims=True) + epsilon)
-    normed = (mixed * scale * gain_ref[...]).astype(BF16)
+    normed = (mixed * scale * gain_ref[...].reshape(1, -1)).astype(BF16)
     att[...] = normed
     for c in loads[1:]:
         c.wait()
@@ -1242,7 +1328,7 @@
     mixed = kept[...]
     scale = lax.rsqrt(jnp.mean(mixed * mixed, axis=-1, keepdims=True) + epsilon)
     d_gain[...] = jnp.sum(d_normed * mixed * scale, axis=0, keepdims=True)
-    u = d_normed * gain_ref[...]
+    u = d_normed * gain_ref[...].reshape(1, -1)
     along = jnp.mean(u * mixed, axis=-1, keepdims=True)
     d_mixed = cot_ref[...] + scale * (u - mixed * (scale * scale * along))
     grad_mixed[...] = d_mixed
@@ -1294,7 +1380,7 @@
         compiler_params=params(),
         cost_estimate=pl.CostEstimate(flops=25 * 10**9, bytes_accessed=32 << 20, transcendentals=0),
         name="middle",
-    )(inputs.reshape(flat), att, cotangent.reshape(flat), gain.reshape(1, -1), *weights)
+    )(inputs.reshape(flat), att, cotangent.reshape(flat), gain, *weights)
     return out[0].reshape(inputs.shape), out[1].reshape(inputs.shape), out[2], out[3], out[4:]
 
 
@@ -1318,7 +1404,7 @@
     n = places.inner
     onehot = jnp.asarray(ONEHOT)
     normed_t, own, pair, attended_t, out, lse, tiles, far = attention_forward(
-        n, lengths, bucket_bias, onehot, inputs, norm_attn, w_query, w_key, w_value
+        n, lengths, bucket_bias.T, onehot, inputs, norm_attn, w_query, w_key, w_value
     )
     result, grad_mixed, grad_attended_t, grad_norm_ffn, weights = middle(
         inputs, attended_t, cotangent, norm_ffn, w_out, w_gate, w_up, w_down
@@ -1328,13 +1414,13 @@
     grads, near, far_sum, parts, other, leaving = attention_backward(
         n, early, lengths, far, tiles, own, pair, out, lse, grad_attended_t, weights, projections
     )
-    late = Rows(places, [(width, HALF)] * 3 + [(places.dp * SMALL, LANE)], LANE, 2)
+    late = Rows(places, [(width, HALF)] * 3, LANE, 2)
     loaded = (
         parts, grads, normed_t, *projections, inputs, grad_mixed, near, far_sum, onehot, other, leaving
     )
-    grad_inputs, full_early, full_late = last_grads(early, late, loaded, norm_attn, grad_norm_ffn)
+    grad_inputs, full_early, full_late, small = last_grads(early, late, loaded, norm_attn, grad_norm_ffn)
     part_out, part_gate, part_up, part_down, part_query, part_key, part_value, part_attn, part_ffn, part_table = unpack(
-        early, late, full_early, full_late, width
+        early, late, full_early, full_late, small, width
     )
     return (
         result,

time: 359 us -> 355 us (0.989)
  local copies, waits for them, and re-layouts: 7.14 us -> 3.22 us
where the time goes in v6:
time: 355 us; the launch traced here: 350 us
  Pallas kernels  345 us (97%)
    pallas_call x1, Pallas kernels, attention_forward(): pl.pallas_call(functools.partial(forward_kernel, n), in_specs=[smem()] +...  110 us
    pallas_call x1, Pallas kernels, attention_backward(): pl.pallas_call(functools.partial(backward_kernel, n, early), in_specs=[sm...  107 us
    pallas_call x1, Pallas kernels, last_grads(): pl.pallas_call(functools.partial(last_kernel, early, late), in_specs=[any...  84.5 us
    pallas_call x1, Pallas kernels, middle(): pl.pallas_call(middle_kernel, in_specs=[whole()] * 4 + [anywhere()] * 4,...  38.7 us

profile of v6, /device:TPU:0, one launch (start us, length us, event | category | flops | bytes accessed | tf_op | source)
XLA Modules:
  0.0 349.6 jit_solution(8905209911403736571)
XLA Ops:
  0.6 110.2 %attention_forward.1 = (bf16[2,3,768,256]{3,2,1,0:T(8,128)(2,1)}, bf16[9,4,192,256]{3,2,1,0:T(8,128)(2,1)}, bf16[1,9,4,128,256]{4,3,2,1,0:T(8,128)(2,1)}, bf16[3...) custom-call(s32[3]{0:T(128)} %len_ref.3, ...), custom_call_target="tpu_custom_call" | custom-call | flops 44999999488 | bytes 25165824 | tf_op jit(solution)/shard_map/attention_forward/pallas_call | solution.py:898
  110.9 38.7 %middle.1 = (f32[768,768]{1,0:T(8,128)}, f32[768,768]{1,0:T(8,128)}, bf16[3,768,256]{2,1,0:T(8,128)(2,1)}, f32[1,768]{1,0:T(1,128)}, bf16[768,768]{1,0:T(8,128)(...) custom-call(f32[768,768]{1,0:T(8,128)} %bitcast.7, ...), custom_call_target="tpu_custom_call" | custom-call | flops 24999999488 | bytes 33554432 | tf_op jit(solution)/shard_map/middle/pallas_call | solution.py:1363
  149.6 106.8 %attention_backward.1 = (bf16[3,3,2,384,256]{4,3,2,1,0:T(8,128)(2,1)}, f32[3,4,256,256]{3,2,1,0:T(8,128)}, f32[3,8,256]{2,1,0:T(8,128)}, bf16[2624,256]{1,0:T(8,...) custom-call(s32[3]{0:T(128)} %len_ref.3, f32[3,2,1,256]{3,2,1,0:T(1,128)} %get-tuple-element.50.far_ref, ...), custom_call_target="tpu_custom_call" | custom-call | flops 109999996928 | bytes 25165824 | tf_op jit(solution)/shard_map/attention_backward/pallas_call | solution.py:1228
  256.4 84.5 %last_grads.1 = (f32[3,256,768]{2,1,0:T(8,128)}, bf16[5248,256]{1,0:T(8,128)(2,1)}, bf16[2,1792,128]{2,1,0:T(8,128)(2,1)}, f32[16,128]{1,0:T(8,128)}) custom-call(bf16[2624,256]{1,0:T(8,128)(2,1)} %get-tuple-element.61.refs_0_, bf16[3,3,2,384,256]{4,3,2,1,0:T(8,128)(2,1)} %get-tuple-element.62.refs_1_, bf16[2,3,768,256]{3,2,1,0:T(8,128)(2,1)} %get-tuple-element.63.refs_2_, ...), custom_call_target="tpu_custom_call" | custom-call | tf_op jit(solution)/shard_map/last_grads/pallas_call | solution.py:615
  340.9 5.1 %unpack.1 = (f32[192,768]{1,0:T(8,128)}, f32[192,2048]{1,0:T(8,128)}, f32[192,2048]{1,0:T(8,128)}, f32[512,768]{1,0:T(8,128)}, f32[192,768]{1,0:T(8,128)}, /*ind...) custom-call(bf16[5248,256]{1,0:T(8,128)(2,1)} %get-tuple-element.71.full_early, ...), custom_call_target="tpu_custom_call" | custom-call | tf_op jit(solution)/shard_map/unpack/pallas_call | solution.py:662
  346.0 3.2 copy.27

commit v7 on v6

--- a/solution.py
+++ b/solution.py
@@ -489,7 +489,7 @@
     loads[-1].wait()
     n_copy.start()
     early_lines, late_lines = list(early.lines), list(late.lines)
-    for line in early_lines[:2]:
+    for line in early_lines:
         spread_early.step_pair(line)
     for c in loads[1:-1]:
         c.wait()
@@ -506,10 +506,8 @@
     for i, out in enumerate((gq, gk, gv)):
         weight(i, out)
     spread_early.step_two(0)
-    spread_early.step_pair(2)
     scatter.step_first(late.lines)
     spread_early.step_two(1)
-    spread_early.step_pair(3)
     gain = gain_ref[...].reshape(1, -1)
     gain_sums = []
 
@@ -637,9 +635,15 @@
     )(*loaded, gain, ffn)
 
 
-def unpack_kernel(early, late, full_early, full_late, small, *outs):
+def unpack_kernel(early, late, full_early, full_late, small, grad_in, *outs):
+    *outs, grad_out, held, sems = outs
+    arrive = pltpu.make_async_copy(grad_in, held, sems.at[0])
+    leave = pltpu.make_async_copy(held, grad_out, sems.at[1])
+    arrive.start()
     for m, block, at, share in early.blocks:
         outs[m][:, block * LANES : (block + 1) * LANES] = full_early[at : at + share].astype(F32)
+    arrive.wait()
+    leave.start()
     outs = outs[len(early.shapes) :]
     for m, block, at, share in late.blocks:
         for half in range(2):
@@ -653,20 +657,23 @@
             at += 1
     buckets, heads = d_table.shape
     d_table[...] = small[at : at + buckets, :heads]
-
-
-def unpack(early, late, full_early, full_late, small, width):
+    leave.wait()
+
+
+def unpack(early, late, full_early, full_late, small, grad_in):
+    width = grad_in.shape[-1]
     dp = early.p.dp
     shapes = [(height // dp, columns) for height, columns in early.shapes]
     shapes += [(width // dp, width)] * 3 + [(1, width // dp)] * 2 + [(NB // dp, H)]
     return pl.pallas_call(
         functools.partial(unpack_kernel, early, late),
-        in_specs=[whole()] * 3,
-        out_specs=[whole()] * len(shapes),
-        out_shape=[jax.ShapeDtypeStruct(s, F32) for s in shapes],
+        in_specs=[whole()] * 3 + [anywhere()],
+        out_specs=[whole()] * len(shapes) + [anywhere()],
+        out_shape=[jax.ShapeDtypeStruct(s, F32) for s in shapes + [grad_in.shape]],
+        scratch_shapes=[pltpu.VMEM(grad_in.shape, F32), pltpu.SemaphoreType.DMA((2,))],
         compiler_params=params(),
         name="unpack",
-    )(full_early, full_late, small)
+    )(full_early, full_late, small, grad_in)
 
 
 def greet(n, z, x):
@@ -699,8 +706,8 @@
 
 def forward_kernel(
     n, len_ref, table_ref, onehot_ref, x_ref, gain_ref, wq_ref, wk_ref, wv_ref,
-    normed_ref, own, pair, att, o_ref, lse_ref, tile_ref, far_ref,
-    here, there, send, ka, qa, va,
+    normed_out, own_out, pair_out, att, o_ref, lse_ref, tile_out, far_ref,
+    normed_ref, own, pair, tile_ref, keep_sem, tile_sem, here, there, send, ka, qa, va,
     n_send, n_recv, z_send, z_recv, x_send, x_recv, o_send, o_recv,
 ):
     nk = OUTER * n
@@ -760,6 +767,13 @@
         for h in range(HEADS):
             z_copy(b * HEADS + h, i).start()
 
+    def keep(u):
+        yield pltpu.make_async_copy(own.at[u], own_out.at[u], keep_sem.at[u, 0])
+        for s in range(1, n):
+            yield pltpu.make_async_copy(pair.at[s - 1, u], pair_out.at[s - 1, u], keep_sem.at[u, s])
+
+    keep_normed = pltpu.make_async_copy(normed_ref, normed_out, tile_sem.at[0])
+    keep_tiles = pltpu.make_async_copy(tile_ref, tile_out, tile_sem.at[1])
     for b in range(batch):
         project(b, 0)
         if b == 0:
@@ -778,6 +792,7 @@
         for side, bucket in enumerate((NB // 2 - 1, NB - 1)):
             value = jnp.sum(jnp.where(table_lane == bucket, chosen, 0.0), axis=1, keepdims=True)
             far_ref[h, side] = jnp.broadcast_to(value, (1, BLK))
+    keep_tiles.start()
 
     def attend(u):
         b, h = lax.div(u, HEADS), lax.rem(u, HEADS)
@@ -827,6 +842,8 @@
             weight = total[DH : DH + 1]
             o_ref[u, j] = (total[:DH] / weight).astype(BF16)
             lse_ref[u, j] = tops[j] + jnp.log2(weight)
+        for c in keep(u):
+            c.start()
         rows = pl.ds(pl.multiple_of((z * HEADS + h) * DH, DH), DH)
         att[b, rows] = o_ref[u, z]
         @pl.when(u >= held_back)
@@ -874,8 +891,11 @@
         return carry
 
     lax.fori_loop(0, units + 1, turn, 0)
+    keep_normed.start()
 
     def finish(u, carry):
+        for c in keep(u):
+            c.wait()
         for d in range(1, OUTER):
             o_copy(u, d).wait_send()
             o_copy(u, d).wait_recv()
@@ -889,6 +909,8 @@
     lax.fori_loop(0, units, finish, 0)
     for b in range(batch):
         n_copy(b).wait_send()
+    keep_normed.wait()
+    keep_tiles.wait()
 
 
 def attention_forward(n, lengths, table, onehot, inputs, gain, wq, wk, wv):
@@ -898,7 +920,7 @@
     return pl.pallas_call(
         functools.partial(forward_kernel, n),
         in_specs=[smem()] + [whole()] * 7,
-        out_specs=[whole()] * 8,
+        out_specs=[anywhere()] * 3 + [whole()] * 3 + [anywhere(), whole()],
         out_shape=[
             jax.ShapeDtypeStruct((2, batch, width, height), BF16),
             jax.ShapeDtypeStruct((units, OUTER, 3 * DH, BLK), BF16),
@@ -910,6 +932,12 @@
             jax.ShapeDtypeStruct((HEADS, 2, 1, BLK), F32),
         ],
         scratch_shapes=[
+            pltpu.VMEM((2, batch, width, height), BF16),
+            pltpu.VMEM((units, OUTER, 3 * DH, BLK), BF16),
+            pltpu.VMEM((n - 1, units, OUTER, 2 * DH, BLK), BF16),
+            pltpu.VMEM((HEADS, TILES, BLK, BLK), F32),
+            dma((units, n)),
+            dma((2,)),
             pltpu.VMEM((batch, height, width), BF16),
             pltpu.VMEM((batch, height, width), BF16),
             pltpu.VMEM((units, 2, 3 * DH, BLK), BF16),
@@ -938,13 +966,14 @@
 
 
 def backward_kernel(
-    n, early, len_ref, far_ref, tile_ref, own, pair, o_ref, lse_ref, dout, *refs
+    n, early, len_ref, far_ref, lse_ref, tile_in, own, pair, o_in, dout, *refs
 ):
     scatter = early_scatter(early)
     count = len(early.shapes)
     weights, refs = refs[:count], refs[count:]
     projections, refs = refs[:3], refs[3:]
-    (grads, near, far_sum, parts, other, leaving, w_half, other_out, w_sem, n_send, n_recv, own_slot, pair_slot, load_sem,
+    (grads_out, near_out, far_sum, parts, other, leaving,
+    tile_ref, o_ref, grads, near, first_sem, own_sem, keep_sem, w_half, other_out, w_sem, n_send, n_recv, own_slot, pair_slot, load_sem,
     do_land, x_out, x_land, z_out, kept,
     ka, kt, va, qa, da, dk_all, dv_all,
     d_send, d_recv, x_send, x_recv, z_send, z_recv) = refs[: -scatter.count]
@@ -959,6 +988,19 @@
     low = lax.rem(z, 2) * HW
     greet_all(early.p)
     scatter.step_core()
+    firsts = [
+        pltpu.make_async_copy(src, dst, first_sem.at[i]) for i, (src, dst) in enumerate(((tile_in, tile_ref), (o_in, o_ref)))
+    ]
+    for c in firsts:
+        c.start()
+
+    def own_part(u):
+        b, h = lax.div(u, HEADS), lax.rem(u, HEADS)
+        return pltpu.make_async_copy(dout.at[b, head_rows(z, h)], do_land.at[u, z], own_sem.at[u])
+
+    def keep_grads(b):
+        return [pltpu.make_async_copy(grads.at[m, b], grads_out.at[m, b], keep_sem.at[m, b]) for m in range(3)]
+
     columns = half_columns(z)
     w_loads = [pltpu.make_async_copy(w.at[:, columns], w_half.at[m], w_sem.at[m]) for m, w in enumerate(projections)]
     for c in w_loads:
@@ -1009,7 +1051,7 @@
     start_d(1)
 
     def begin(u, carry):
-        do_land[u, z] = dout[lax.div(u, HEADS), head_rows(z, lax.rem(u, HEADS))]
+        own_part(u).start()
         return carry
 
     lax.fori_loop(0, units, begin, 0)
@@ -1048,6 +1090,7 @@
                 ka[kb] = key_rows(keys, kb, length)
                 kt[kb] = keys
                 va[kb] = jnp.concatenate([vals, ones3], axis=0).T
+        own_part(u).wait()
         for d in range(1, OUTER):
             d_copy(u, d).wait_recv()
         for j in range(OUTER):
@@ -1143,6 +1186,8 @@
             for i in range(2):
                 for m in range(3):
                     z_copy(b * HEADS + h, i, m).wait_recv()
+        for c in keep_grads(b):
+            c.start()
         total = jnp.dot(w_half[0], grads[0, b, 1], preferred_element_type=F32)
         total = total + jnp.dot(w_half[1], grads[1, b, 1], preferred_element_type=F32)
         total = total + jnp.dot(w_half[2], grads[2, b, 1], preferred_element_type=F32)
@@ -1182,9 +1227,11 @@
 
         return carry
 
-    for c in w_loads:
+    for c in w_loads + firsts:
         c.wait()
     lax.fori_loop(0, units + 2, turn, 0)
+    near_copy = pltpu.make_async_copy(near, near_out, first_sem.at[0])
+    near_copy.start()
 
     def finish(u, carry):
         for d in range(1, OUTER):
@@ -1211,6 +1258,10 @@
         scatter.step_third(line)
         parts[early.part_start[line] : early.part_start[line] + early.size[line]] = scatter.part(line)[...]
     scatter.end()
+    for b in range(batch):
+        for c in keep_grads(b):
+            c.wait()
+    near_copy.wait()
 
 
 def staging(n, units):
@@ -1227,8 +1278,8 @@
     x_slots, z_slots = staging(n, units)
     return pl.pallas_call(
         functools.partial(backward_kernel, n, early),
-        in_specs=[smem()] + [whole()] * 2 + [anywhere()] * 2 + [whole()] * 3 + [anywhere()] * (len(weights) + 3),
-        out_specs=[whole()] * 6,
+        in_specs=[smem()] + [whole()] * 2 + [anywhere()] * (8 + len(weights)),
+        out_specs=[anywhere()] * 2 + [whole()] * 4,
         out_shape=[
             jax.ShapeDtypeStruct((3, batch, 2, HALF, height), BF16),
             jax.ShapeDtypeStruct((HEADS, TILES, BLK, BLK), F32),
@@ -1238,6 +1289,13 @@
             jax.ShapeDtypeStruct((width, height), BF16),
         ],
         scratch_shapes=[
+            pltpu.VMEM(tiles.shape, F32),
+            pltpu.VMEM(out.shape, BF16),
+            pltpu.VMEM((3, batch, 2, HALF, height), BF16),
+            pltpu.VMEM((HEADS, TILES, BLK, BLK), F32),
+            dma((2,)),
+            dma((units,)),
+            dma((3, batch)),
             pltpu.VMEM((3, width, HALF), BF16),
             pltpu.VMEM((batch - 1, width, height), BF16),
             dma((3,)),
@@ -1271,42 +1329,43 @@
         ),
         cost_estimate=pl.CostEstimate(flops=110 * 10**9, bytes_accessed=24 << 20, transcendentals=0),
         name="attention_backward",
-    )(lengths, far, tiles, own, pair, out, lse, dout, *weights, *projections)
+    )(lengths, far, lse, tiles, own, pair, out, dout, *weights, *projections)
 
 
 FF_STEP = 512
 
 
 def middle_kernel(
-    x_ref, att_ref, cot_ref, gain_ref, w_out, w_gate, w_up, w_down,
-    result, grad_mixed, dout, d_gain, d_out, d_gate, d_up, d_down,
+    x_in, att_in, cot_in, gain_ref, w_out, w_gate, w_up, w_down,
+    result_out, mixed_out, dout_out, d_gain, d_out, d_gate, d_up, d_down,
+    x_ref, att_ref, cot_ref, result, grad_mixed, dout,
     wo, wg, wu, wd, att, low, hidden, g_gate, g_up, s_out, s_gate, s_up, s_down, kept, in_sem, out_sem,
 ):
     tokens, width = x_ref.shape
     batch = att_ref.shape[0]
     ff = w_gate.shape[1]
-    loads = [
-        pltpu.make_async_copy(src, dst, in_sem.at[i])
-        for i, (src, dst) in enumerate(((w_out, wo), (w_gate, wg), (w_up, wu), (w_down, wd)))
-    ]
-    stores = [
-        pltpu.make_async_copy(src, dst, out_sem.at[i])
-        for i, (src, dst) in enumerate(((s_out, d_out), (s_gate, d_gate), (s_up, d_up), (s_down, d_down)))
-    ]
+    pairs = ((w_out, wo), (w_gate, wg), (w_up, wu), (w_down, wd), (att_in, att_ref), (x_in, x_ref), (cot_in, cot_ref))
+    loads = [pltpu.make_async_copy(src, dst, in_sem.at[i]) for i, (src, dst) in enumerate(pairs)]
+    pairs = ((s_out, d_out), (s_gate, d_gate), (s_up, d_up), (s_down, d_down))
+    pairs += ((result, result_out), (grad_mixed, mixed_out), (dout, dout_out))
+    stores = [pltpu.make_async_copy(src, dst, out_sem.at[i]) for i, (src, dst) in enumerate(pairs)]
+    loads = loads[4:5] + loads[:1] + loads[5:] + loads[1:4]
     for c in loads:
         c.start()
     height = tokens // batch
+    loads[0].wait()
     for b in range(batch):
         att[b * height : (b + 1) * height] = att_ref[b].T
+    for c in loads[1:4]:
+        c.wait()
     low[...] = cot_ref[...].astype(BF16)
-    loads[0].wait()
     mixed = x_ref[...] + jnp.dot(att[...], wo[...], preferred_element_type=F32)
     kept[...] = mixed
     result[...] = mixed
     scale = lax.rsqrt(jnp.mean(mixed * mixed, axis=-1, keepdims=True) + epsilon)
     normed = (mixed * scale * gain_ref[...].reshape(1, -1)).astype(BF16)
     att[...] = normed
-    for c in loads[1:]:
+    for c in loads[4:]:
         c.wait()
     root = 0.7978845608028654
     for at in range(0, ff, FF_STEP):
@@ -1323,6 +1382,7 @@
         g_gate[:, part] = (g_hidden * upward * slope).astype(BF16)
         g_up[:, part] = (g_hidden * act).astype(BF16)
     result[...] += jnp.dot(hidden[...], wd[...], preferred_element_type=F32)
+    stores[4].start()
     d_normed = lax.dot_general(g_gate[...], wg[...], NT, preferred_element_type=F32)
     d_normed = d_normed + lax.dot_general(g_up[...], wu[...], NT, preferred_element_type=F32)
     mixed = kept[...]
@@ -1332,10 +1392,12 @@
     along = jnp.mean(u * mixed, axis=-1, keepdims=True)
     d_mixed = cot_ref[...] + scale * (u - mixed * (scale * scale * along))
     grad_mixed[...] = d_mixed
+    stores[5].start()
     d_low = d_mixed.astype(BF16)
     turned = lax.dot_general(wo[...], d_low, NT, preferred_element_type=F32).astype(BF16)
     for b in range(batch):
         dout[b] = turned[:, b * height : (b + 1) * height]
+    stores[6].start()
     total = jnp.zeros((width, width), F32)
     for b in range(batch):
         total = total + jnp.dot(att_ref[b], d_low[b * height : (b + 1) * height], preferred_element_type=F32)
@@ -1362,8 +1424,8 @@
     flat = (tokens, width)
     out = pl.pallas_call(
         middle_kernel,
-        in_specs=[whole()] * 4 + [anywhere()] * 4,
-        out_specs=[whole()] * 4 + [anywhere()] * 4,
+        in_specs=[anywhere()] * 3 + [whole()] + [anywhere()] * 4,
+        out_specs=[anywhere()] * 3 + [whole()] + [anywhere()] * 4,
         out_shape=[
             jax.ShapeDtypeStruct(flat, F32),
             jax.ShapeDtypeStruct(flat, F32),
@@ -1371,12 +1433,20 @@
             jax.ShapeDtypeStruct((1, width), F32),
         ]
         + [jax.ShapeDtypeStruct(w.shape, BF16) for w in weights],
-        scratch_shapes=[pltpu.VMEM(w.shape, BF16) for w in weights]
+        scratch_shapes=[
+            pltpu.VMEM(flat, F32),
+            pltpu.VMEM(att.shape, BF16),
+            pltpu.VMEM(flat, F32),
+            pltpu.VMEM(flat, F32),
+            pltpu.VMEM(flat, F32),
+            pltpu.VMEM(att.shape, BF16),
+        ]
+        + [pltpu.VMEM(w.shape, BF16) for w in weights]
         + [pltpu.VMEM(flat, BF16)] * 2
         + [pltpu.VMEM((tokens, ff), BF16)] * 3
         + [pltpu.VMEM(w.shape, BF16) for w in weights]
         + [pltpu.VMEM(flat, F32)]
-        + [pltpu.SemaphoreType.DMA((4,))] * 2,
+        + [pltpu.SemaphoreType.DMA((7,))] * 2,
         compiler_params=params(),
         cost_estimate=pl.CostEstimate(flops=25 * 10**9, bytes_accessed=32 << 20, transcendentals=0),
         name="middle",
@@ -1419,9 +1489,8 @@
         parts, grads, normed_t, *projections, inputs, grad_mixed, near, far_sum, onehot, other, leaving
     )
     grad_inputs, full_early, full_late, small = last_grads(early, late, loaded, norm_attn, grad_norm_ffn)
-    part_out, part_gate, part_up, part_down, part_query, part_key, part_value, part_attn, part_ffn, part_table = unpack(
-        early, late, full_early, full_late, small, width
-    )
+    (part_out, part_gate, part_up, part_down, part_query, part_key, part_value, part_attn, part_ffn, part_table,
+     grad_inputs) = unpack(early, late, full_early, full_late, small, grad_inputs)
     return (
         result,
         grad_inputs,

time: 355 us -> 345 us (0.972)
  Pallas kernels: 345 us -> 339 us
    pallas_call x1, Pallas kernels: 110 us -> 106 us  [attention_forward(): pl.pallas_call(functools.partial(forward_kernel, n), in_specs=[smem()] +...]
    pallas_call x1, Pallas kernels: 107 us -> 103 us  [attention_backward(): pl.pallas_call(functools.partial(backward_kernel, n, early), in_specs=[sm...]
where the time goes in v7:
time: 345 us; the launch traced here: 340 us
  Pallas kernels  339 us (98%)
    pallas_call x1, Pallas kernels, attention_forward(): pl.pallas_call(functools.partial(forward_kernel, n), in_specs=[smem()] +...  106 us
    pallas_call x1, Pallas kernels, attention_backward(): pl.pallas_call(functools.partial(backward_kernel, n, early), in_specs=[sm...  103 us
    pallas_call x1, Pallas kernels, last_grads(): pl.pallas_call(functools.partial(last_kernel, early, late), in_specs=[any...  85 us
    pallas_call x1, Pallas kernels, middle(): pl.pallas_call(middle_kernel, in_specs=[anywhere()] * 3 + [whole()] + [an...  36.4 us
    pallas_call x1, Pallas kernels, unpack(): pl.pallas_call(functools.partial(unpack_kernel, early, late), in_specs=[w...  8.04 us

profile of v7, /device:TPU:0, one launch (start us, length us, event | category | flops | bytes accessed | tf_op | source)
XLA Modules:
  0.0 339.7 jit_solution(13840587389924528704)
XLA Ops:
  0.6 106.1 %attention_forward.1 = (bf16[2,3,768,256]{3,2,1,0:T(8,128)(2,1)}, bf16[9,4,192,256]{3,2,1,0:T(8,128)(2,1)}, bf16[1,9,4,128,256]{4,3,2,1,0:T(8,128)(2,1)}, bf16[3...) custom-call(s32[3]{0:T(128)} %len_ref.3, ...), custom_call_target="tpu_custom_call" | custom-call | flops 44999999488 | bytes 25165824 | tf_op jit(solution)/shard_map/attention_forward/pallas_call | solution.py:920
  106.8 36.4 %middle.1 = (f32[768,768]{1,0:T(8,128)}, f32[768,768]{1,0:T(8,128)}, bf16[3,768,256]{2,1,0:T(8,128)(2,1)}, f32[1,768]{1,0:T(1,128)}, bf16[768,768]{1,0:T(8,128)(...) custom-call(f32[768,768]{1,0:T(8,128)} %bitcast.7, ...), custom_call_target="tpu_custom_call" | custom-call | flops 24999999488 | bytes 33554432 | tf_op jit(solution)/shard_map/middle/pallas_call | solution.py:1425
  143.2 103.0 %attention_backward.1 = (bf16[3,3,2,384,256]{4,3,2,1,0:T(8,128)(2,1)}, f32[3,4,256,256]{3,2,1,0:T(8,128)}, f32[3,8,256]{2,1,0:T(8,128)}, bf16[2624,256]{1,0:T(8,...) custom-call(s32[3]{0:T(128)} %len_ref.3, f32[3,2,1,256]{3,2,1,0:T(1,128)} %get-tuple-element.51.far_ref, ...), custom_call_target="tpu_custom_call" | custom-call | flops 109999996928 | bytes 25165824 | tf_op jit(solution)/shard_map/attention_backward/pallas_call | solution.py:1279
  246.2 85.0 %last_grads.1 = (f32[3,256,768]{2,1,0:T(8,128)}, bf16[5248,256]{1,0:T(8,128)(2,1)}, bf16[2,1792,128]{2,1,0:T(8,128)(2,1)}, f32[16,128]{1,0:T(8,128)}) custom-call(bf16[2624,256]{1,0:T(8,128)(2,1)} %get-tuple-element.62.refs_0_, bf16[3,3,2,384,256]{4,3,2,1,0:T(8,128)(2,1)} %get-tuple-element.63.refs_1_, bf16[2,3,768,256]{3,2,1,0:T(8,128)(2,1)} %get-tuple-element.64.refs_2_, ...), custom_call_target="tpu_custom_call" | custom-call | tf_op jit(solution)/shard_map/last_grads/pallas_call | solution.py:613
  331.2 8.0 %unpack.1 = (f32[192,768]{1,0:T(8,128)}, f32[192,2048]{1,0:T(8,128)}, f32[192,2048]{1,0:T(8,128)}, f32[512,768]{1,0:T(8,128)}, f32[192,768]{1,0:T(8,128)}, /*ind...) custom-call(bf16[5248,256]{1,0:T(8,128)(2,1)} %get-tuple-element.71., ...), custom_call_target="tpu_custom_call" | custom-call | tf_op jit(solution)/shard_map/unpack/pallas_call | solution.py:668

commit v8 on v7

--- a/solution.py
+++ b/solution.py
@@ -449,11 +449,11 @@
 def last_kernel(early, late, *refs):
     count = 13
     sources, (gain_ref, ffn_ref), refs = refs[:count], refs[count : count + 2], refs[count + 2 :]
-    grad_in, full_early, full_late, small_out, refs = refs[0], refs[1], refs[2], refs[3], refs[4:]
+    grad_out, full_early, full_late, small_out, refs = refs[0], refs[1], refs[2], refs[3], refs[4:]
     slots, load_sem, refs = refs[:count], refs[count], refs[count + 1 :]
     p = late.p
     scatter, spread_early, spread_late = Scatter(late, (True, False)), Spread(early), Spread(late, True)
-    (gq, gk, gv, arriving, n_sem), refs = refs[:5], refs[5:]
+    (gq, gk, gv, arriving, n_sem, grad_in, out_sem), refs = refs[:7], refs[7:]
     scatter.bind((gq, gk, gv), refs[: scatter.count])
     refs = refs[scatter.count :]
     z, x = scatter.z, scatter.x
@@ -511,6 +511,8 @@
     gain = gain_ref[...].reshape(1, -1)
     gain_sums = []
 
+    leaves = [pltpu.make_async_copy(grad_in.at[b], grad_out.at[b], out_sem.at[b]) for b in range(batch)]
+
     def positions(b, arrived):
         back = jnp.dot(wq_ref[...], grads[0, b, 0], preferred_element_type=F32)
         back = back + jnp.dot(wk_ref[...], grads[1, b, 0], preferred_element_type=F32)
@@ -522,6 +524,7 @@
         u = back * gain
         along = jnp.mean(u * values, axis=-1, keepdims=True)
         grad_in[b] = mixed_ref[b] + scale * (u - values * (scale * scale * along))
+        leaves[b].start()
 
     positions(0, other.at[0])
     spread_early.step_back(0)
@@ -593,6 +596,8 @@
     small_out[...] = total_small.held[len(total_small.hops), mine]
     total_small.end()
     n_copy.wait_send()
+    for c in leaves:
+        c.wait()
     spread_early.end()
     spread_late.end()
     scatter.end()
@@ -613,7 +618,7 @@
     return pl.pallas_call(
         functools.partial(last_kernel, early, late),
         in_specs=[anywhere()] * len(loaded) + [whole()] * 2,
-        out_specs=[whole()] * 4,
+        out_specs=[anywhere()] + [whole()] * 3,
         out_shape=[
             jax.ShapeDtypeStruct(inputs.shape, F32),
             jax.ShapeDtypeStruct((early.total, early.lanes), BF16),
@@ -624,6 +629,7 @@
         + [pltpu.SemaphoreType.DMA((len(loaded),))]
         + [pltpu.VMEM((width, HALF), BF16)] * 3
         + [pltpu.VMEM(loaded[-1].shape, BF16), pltpu.SemaphoreType.DMA((2,))]
+        + [pltpu.VMEM(inputs.shape, F32), pltpu.SemaphoreType.DMA((inputs.shape[0],))]
         + Scatter(late, (True, False)).scratch()
         + Spread(early).scratch()
         + Spread(late, True).scratch()
@@ -635,21 +641,35 @@
     )(*loaded, gain, ffn)
 
 
-def unpack_kernel(early, late, full_early, full_late, small, grad_in, *outs):
-    *outs, grad_out, held, sems = outs
-    arrive = pltpu.make_async_copy(grad_in, held, sems.at[0])
-    leave = pltpu.make_async_copy(held, grad_out, sems.at[1])
-    arrive.start()
-    for m, block, at, share in early.blocks:
-        outs[m][:, block * LANES : (block + 1) * LANES] = full_early[at : at + share].astype(F32)
-    arrive.wait()
-    leave.start()
-    outs = outs[len(early.shapes) :]
-    for m, block, at, share in late.blocks:
-        for half in range(2):
-            first = half * HALF + block * LANE
-            outs[m][:, first : first + LANE] = full_late[half, at : at + share].astype(F32)
-    d_attn, d_ffn, d_table = outs[len(late.shapes) :]
+def unpack_kernel(early, late, full_early, full_late, small, grad_in, *refs):
+    count = len(early.shapes) + len(late.shapes)
+    targets, (d_attn, d_ffn, d_table, grad_out), refs = refs[:count], refs[count : count + 4], refs[count + 4 :]
+    outs, (held, taken_early, taken_late, sems) = refs[:count], refs[count:]
+    arrive = [
+        pltpu.make_async_copy(src, dst, sems.at[i])
+        for i, (src, dst) in enumerate(((full_early, taken_early), (full_late, taken_late), (grad_in, held)))
+    ]
+    leave = [pltpu.make_async_copy(held, grad_out, sems.at[3])]
+    leave += [pltpu.make_async_copy(src, dst, sems.at[4 + i]) for i, (src, dst) in enumerate(zip(outs, targets))]
+    for c in arrive:
+        c.start()
+    arrive[0].wait()
+    for m in range(len(early.shapes)):
+        for i, block, at, share in early.blocks:
+            if i == m:
+                outs[m][:, block * LANES : (block + 1) * LANES] = taken_early[at : at + share].astype(F32)
+        leave[1 + m].start()
+    arrive[1].wait()
+    for m in range(len(late.shapes)):
+        for i, block, at, share in late.blocks:
+            for half in range(2):
+                first = half * HALF + block * LANE
+                if i == m:
+                    out = outs[len(early.shapes) + m]
+                    out[:, first : first + LANE] = taken_late[half, at : at + share].astype(F32)
+        leave[1 + len(early.shapes) + m].start()
+    arrive[2].wait()
+    leave[0].start()
     at = 0
     for out in (d_attn, d_ffn):
         for begin, end in gain_rows(out.shape[1]):
@@ -657,20 +677,27 @@
             at += 1
     buckets, heads = d_table.shape
     d_table[...] = small[at : at + buckets, :heads]
-    leave.wait()
+    for c in leave:
+        c.wait()
 
 
 def unpack(early, late, full_early, full_late, small, grad_in):
     width = grad_in.shape[-1]
     dp = early.p.dp
-    shapes = [(height // dp, columns) for height, columns in early.shapes]
-    shapes += [(width // dp, width)] * 3 + [(1, width // dp)] * 2 + [(NB // dp, H)]
+    shapes = [(height // dp, columns) for height, columns in early.shapes] + [(width // dp, width)] * 3
+    few = [(1, width // dp)] * 2 + [(NB // dp, H)]
     return pl.pallas_call(
         functools.partial(unpack_kernel, early, late),
-        in_specs=[whole()] * 3 + [anywhere()],
-        out_specs=[whole()] * len(shapes) + [anywhere()],
-        out_shape=[jax.ShapeDtypeStruct(s, F32) for s in shapes + [grad_in.shape]],
-        scratch_shapes=[pltpu.VMEM(grad_in.shape, F32), pltpu.SemaphoreType.DMA((2,))],
+        in_specs=[anywhere()] * 2 + [whole(), anywhere()],
+        out_specs=[anywhere()] * len(shapes) + [whole()] * len(few) + [anywhere()],
+        out_shape=[jax.ShapeDtypeStruct(s, F32) for s in shapes + few + [grad_in.shape]],
+        scratch_shapes=[pltpu.VMEM(s, F32) for s in shapes]
+        + [
+            pltpu.VMEM(grad_in.shape, F32),
+            pltpu.VMEM(full_early.shape, BF16),
+            pltpu.VMEM(full_late.shape, BF16),
+            pltpu.SemaphoreType.DMA((4 + len(shapes),)),
+        ],
         compiler_params=params(),
         name="unpack",
     )(full_early, full_late, small, grad_in)
@@ -846,13 +873,6 @@
             c.start()
         rows = pl.ds(pl.multiple_of((z * HEADS + h) * DH, DH), DH)
         att[b, rows] = o_ref[u, z]
-        @pl.when(u >= held_back)
-        def _():
-            start_o(u)
-
-    held_back = units - HEADS - 1
-
-    def start_o(u):
         for d in (2, 1, 3):
             o_copy(u, d).start()
 
@@ -861,10 +881,6 @@
         def _():
             b = lax.div(u, HEADS)
             n_copy(b).wait_recv()
-
-            @pl.when(b == batch - 1)
-            def _():
-                lax.fori_loop(0, held_back, lambda u, c: (start_o(u), c)[1], 0)
 
             @pl.when(b + 1 < batch)
             def _():

time: 345 us -> 342 us (level)
  Pallas kernels: 339 us -> 335 us
where the time goes in v8:
time: 342 us; the launch traced here: 336 us
  Pallas kernels  335 us (98%)
    pallas_call x1, Pallas kernels, attention_forward(): pl.pallas_call(functools.partial(forward_kernel, n), in_specs=[smem()] +...  106 us
    pallas_call x1, Pallas kernels, attention_backward(): pl.pallas_call(functools.partial(backward_kernel, n, early), in_specs=[sm...  103 us
    pallas_call x1, Pallas kernels, last_grads(): pl.pallas_call(functools.partial(last_kernel, early, late), in_specs=[any...  83.1 us
    pallas_call x1, Pallas kernels, middle(): pl.pallas_call(middle_kernel, in_specs=[anywhere()] * 3 + [whole()] + [an...  36.4 us
    pallas_call x1, Pallas kernels, unpack(): pl.pallas_call(functools.partial(unpack_kernel, early, late), in_specs=[a...  6.89 us

profile of v8, /device:TPU:0, one launch (start us, length us, event | category | flops | bytes accessed | tf_op | source)
XLA Modules:
  0.0 336.2 jit_solution(11085037170461661000)
XLA Ops:
  0.6 106.2 %attention_forward.1 = (bf16[2,3,768,256]{3,2,1,0:T(8,128)(2,1)}, bf16[9,4,192,256]{3,2,1,0:T(8,128)(2,1)}, bf16[1,9,4,128,256]{4,3,2,1,0:T(8,128)(2,1)}, bf16[3...) custom-call(s32[3]{0:T(128)} %len_ref.3, ...), custom_call_target="tpu_custom_call" | custom-call | flops 44999999488 | bytes 25165824 | tf_op jit(solution)/shard_map/attention_forward/pallas_call | solution.py:936
  106.8 36.4 %middle.1 = (f32[768,768]{1,0:T(8,128)}, f32[768,768]{1,0:T(8,128)}, bf16[3,768,256]{2,1,0:T(8,128)(2,1)}, f32[1,768]{1,0:T(1,128)}, bf16[768,768]{1,0:T(8,128)(...) custom-call(f32[768,768]{1,0:T(8,128)} %bitcast.7, ...), custom_call_target="tpu_custom_call" | custom-call | flops 24999999488 | bytes 33554432 | tf_op jit(solution)/shard_map/middle/pallas_call | solution.py:1441
  143.2 102.5 %attention_backward.1 = (bf16[3,3,2,384,256]{4,3,2,1,0:T(8,128)(2,1)}, f32[3,4,256,256]{3,2,1,0:T(8,128)}, f32[3,8,256]{2,1,0:T(8,128)}, bf16[2624,256]{1,0:T(8,...) custom-call(s32[3]{0:T(128)} %len_ref.3, f32[3,2,1,256]{3,2,1,0:T(1,128)} %get-tuple-element.51.far_ref, ...), custom_call_target="tpu_custom_call" | custom-call | flops 109999996928 | bytes 25165824 | tf_op jit(solution)/shard_map/attention_backward/pallas_call | solution.py:1295
  245.7 83.1 %last_grads.1 = (f32[3,256,768]{2,1,0:T(8,128)}, bf16[5248,256]{1,0:T(8,128)(2,1)}, bf16[2,1792,128]{2,1,0:T(8,128)(2,1)}, f32[16,128]{1,0:T(8,128)}) custom-call(bf16[2624,256]{1,0:T(8,128)(2,1)} %get-tuple-element.62.refs_0_, bf16[3,3,2,384,256]{4,3,2,1,0:T(8,128)(2,1)} %get-tuple-element.63.refs_1_, bf16[2,3,768,256]{3,2,1,0:T(8,128)(2,1)} %get-tuple-element.64.refs_2_, ...), custom_call_target="tpu_custom_call" | custom-call | tf_op jit(solution)/shard_map/last_grads/pallas_call | solution.py:618
  328.8 6.9 %unpack.1 = (f32[192,768]{1,0:T(8,128)}, f32[192,2048]{1,0:T(8,128)}, f32[192,2048]{1,0:T(8,128)}, f32[512,768]{1,0:T(8,128)}, f32[192,768]{1,0:T(8,128)}, /*ind...) custom-call(bf16[5248,256]{1,0:T(8,128)(2,1)} %get-tuple-element.71., ...), custom_call_target="tpu_custom_call" | custom-call | tf_op jit(solution)/shard_map/unpack/pallas_call | solution.py:689

commit v9 on v8

--- a/solution.py
+++ b/solution.py
@@ -17,11 +17,11 @@
 HALF = 2 * HW
 BLK = 256
 AUG = DH + 16
+QAUG = 2 * DH + 16
 SPAN = 4 * BLK
 LANES = 256
 LANE = 128
 LOG2E = 1.4426950408889634
-LN2 = 0.6931471805599453
 F32 = jnp.float32
 BF16 = jnp.bfloat16
 NT = (((1,), (1,)), ((), ()))
@@ -728,7 +728,13 @@
     one = jnp.ones((1, BLK), F32)
     lane = lax.broadcasted_iota(jnp.int32, (1, BLK), 1)
     mask = jnp.where(kb * BLK + lane < length, 0.0, -1e30)
-    return jnp.concatenate([keys, tail(BLK, (one, one, one, mask)).astype(BF16)], axis=0).T
+    return jnp.concatenate([keys, keys, tail(BLK, (one, one, one, mask)).astype(BF16)], axis=0).T
+
+
+def query_parts(queries):
+    scaled = queries.astype(F32) * LOG2E
+    high = scaled.astype(BF16)
+    return jnp.concatenate([high, (scaled - high.astype(F32)).astype(BF16)], axis=0)
 
 
 def forward_kernel(
@@ -779,8 +785,8 @@
     def project(b, i):
         normed = (here, there)[i][b]
         normed_ref[i, b] = normed.T
-        for m, (w_ref, factor) in enumerate(((wq_ref, LOG2E), (wk_ref, 1.0), (wv_ref, 1.0))):
-            turned = (jnp.dot(normed, w_ref[:, columns], preferred_element_type=F32) * factor).T.astype(BF16)
+        for m, w_ref in enumerate((wq_ref, wk_ref, wv_ref)):
+            turned = jnp.dot(normed, w_ref[:, columns], preferred_element_type=F32).T.astype(BF16)
             for h in range(HEADS):
                 first, second = turned[h * DH : (h + 1) * DH], turned[HW + h * DH : HW + (h + 1) * DH]
                 rows = slice(m * DH, (m + 1) * DH)
@@ -851,9 +857,10 @@
             return jnp.dot(ka[kb], qa[case, j], preferred_element_type=F32) + tile_ref[h, tile]
 
         for j in range(OUTER):
+            both = query_parts(own[u, j, :DH])
             for v, c in enumerate((left, 0.0 * one, right)):
-                qa[v, j, :DH] = own[u, j, :DH]
-                qa[v, j, DH:] = tail(BLK, split3(c) + (one,)).astype(BF16)
+                qa[v, j, : 2 * DH] = both
+                qa[v, j, 2 * DH :] = tail(BLK, split3(c) + (one,)).astype(BF16)
         tops = []
         for j in range(OUTER):
             top = jnp.full((8, BLK), -1e30, F32)
@@ -862,7 +869,7 @@
             top = jnp.max(top, axis=0, keepdims=True)
             tops.append(top)
             for v, c in enumerate((left, 0.0, right)):
-                qa[v, j, DH:] = tail(BLK, split3(c - top) + (one,)).astype(BF16)
+                qa[v, j, 2 * DH :] = tail(BLK, split3(c - top) + (one,)).astype(BF16)
         for j in range(OUTER):
             weights = [jnp.exp2(scores(kb, j)).astype(BF16) for kb in range(nk)]
             total = jnp.dot(va[...], jnp.concatenate(weights, axis=0), preferred_element_type=F32)
@@ -957,8 +964,8 @@
             pltpu.VMEM((batch, height, width), BF16),
             pltpu.VMEM((batch, height, width), BF16),
             pltpu.VMEM((units, 2, 3 * DH, BLK), BF16),
-            pltpu.VMEM((nk, BLK, AUG), BF16),
-            pltpu.VMEM((3, OUTER, AUG, BLK), BF16),
+            pltpu.VMEM((nk, BLK, QAUG), BF16),
+            pltpu.VMEM((3, OUTER, QAUG, BLK), BF16),
             pltpu.VMEM((AUG, nk * BLK), BF16),
             dma((batch,)),
             dma((batch,)),
@@ -1111,9 +1118,10 @@
             d_copy(u, d).wait_recv()
         for j in range(OUTER):
             lse = lse_ref[u, j]
+            both = query_parts(own_slot[slot, j, :DH])
             for v, c in enumerate((left, 0.0, right)):
-                qa[v, j, :DH] = own_slot[slot, j, :DH]
-                qa[v, j, DH:] = tail(BLK, split3(c - lse) + (one,)).astype(BF16)
+                qa[v, j, : 2 * DH] = both
+                qa[v, j, 2 * DH :] = tail(BLK, split3(c - lse) + (one,)).astype(BF16)
             arrived = do_land[u, j]
             delta = jnp.sum(arrived.astype(F32) * o_ref[u, j].astype(F32), axis=0, keepdims=True)
             da[j, :DH] = arrived
@@ -1147,8 +1155,8 @@
                 dv, dk = jnp.zeros((DH, BLK), F32), jnp.zeros((DH, BLK), F32)
                 for j in range(OUTER):
                     dv = dv + lax.dot_general(da[j, :DH], ps[kb, j], NT, preferred_element_type=F32)
-                    dk = dk + lax.dot_general(qa[0, j, :DH], dss[kb, j], NT, preferred_element_type=F32)
-                dk_all[kb] = dk * LN2
+                    dk = dk + lax.dot_general(own_slot[slot, j, :DH], dss[kb, j], NT, preferred_element_type=F32)
+                dk_all[kb] = dk
                 dv_all[kb] = dv
         @pl.when(u >= x_slots)
         def _():
@@ -1325,10 +1333,10 @@
             pltpu.VMEM((n - 1, X_LAND, OUTER, 2 * DH, BLK), BF16),
             pltpu.VMEM((z_slots, 2, 3 * DH, BLK), BF16),
             pltpu.VMEM((2, OUTER, 3 * DH, BLK), F32),
-            pltpu.VMEM((nk, BLK, AUG), BF16),
+            pltpu.VMEM((nk, BLK, QAUG), BF16),
             pltpu.VMEM((nk, DH, BLK), BF16),
             pltpu.VMEM((nk, BLK, AUG), BF16),
-            pltpu.VMEM((3, OUTER, AUG, BLK), BF16),
+            pltpu.VMEM((3, OUTER, QAUG, BLK), BF16),
             pltpu.VMEM((OUTER, AUG, BLK), BF16),
             pltpu.VMEM((nk, DH, BLK), F32),
             pltpu.VMEM((nk, DH, BLK), F32),

time: 342 us -> 342 us (level)
  no operation moved by 1% of the time
where the time goes in v9:
time: 342 us; the launch traced here: 336 us
  Pallas kernels  335 us (98%)
    pallas_call x1, Pallas kernels, attention_forward(): pl.pallas_call(functools.partial(forward_kernel, n), in_specs=[smem()] +...  107 us
    pallas_call x1, Pallas kernels, attention_backward(): pl.pallas_call(functools.partial(backward_kernel, n, early), in_specs=[sm...  102 us
    pallas_call x1, Pallas kernels, last_grads(): pl.pallas_call(functools.partial(last_kernel, early, late), in_specs=[any...  82.6 us
    pallas_call x1, Pallas kernels, middle(): pl.pallas_call(middle_kernel, in_specs=[anywhere()] * 3 + [whole()] + [an...  36.4 us
    pallas_call x1, Pallas kernels, unpack(): pl.pallas_call(functools.partial(unpack_kernel, early, late), in_specs=[a...  6.89 us

profile of v9, /device:TPU:0, one launch (start us, length us, event | category | flops | bytes accessed | tf_op | source)
XLA Modules:
  0.0 335.8 jit_solution(230086751594402450)
XLA Ops:
  0.6 106.6 %attention_forward.1 = (bf16[2,3,768,256]{3,2,1,0:T(8,128)(2,1)}, bf16[9,4,192,256]{3,2,1,0:T(8,128)(2,1)}, bf16[1,9,4,128,256]{4,3,2,1,0:T(8,128)(2,1)}, bf16[3...) custom-call(s32[3]{0:T(128)} %len_ref.3, ...), custom_call_target="tpu_custom_call" | custom-call | flops 44999999488 | bytes 25165824 | tf_op jit(solution)/shard_map/attention_forward/pallas_call | solution.py:943
  107.3 36.4 %middle.1 = (f32[768,768]{1,0:T(8,128)}, f32[768,768]{1,0:T(8,128)}, bf16[3,768,256]{2,1,0:T(8,128)(2,1)}, f32[1,768]{1,0:T(1,128)}, bf16[768,768]{1,0:T(8,128)(...) custom-call(f32[768,768]{1,0:T(8,128)} %bitcast.7, ...), custom_call_target="tpu_custom_call" | custom-call | flops 24999999488 | bytes 33554432 | tf_op jit(solution)/shard_map/middle/pallas_call | solution.py:1449
  143.6 102.1 %attention_backward.1 = (bf16[3,3,2,384,256]{4,3,2,1,0:T(8,128)(2,1)}, f32[3,4,256,256]{3,2,1,0:T(8,128)}, f32[3,8,256]{2,1,0:T(8,128)}, bf16[2624,256]{1,0:T(8,...) custom-call(s32[3]{0:T(128)} %len_ref.3, f32[3,2,1,256]{3,2,1,0:T(1,128)} %get-tuple-element.51.far_ref, ...), custom_call_target="tpu_custom_call" | custom-call | flops 109999996928 | bytes 25165824 | tf_op jit(solution)/shard_map/attention_backward/pallas_call | solution.py:1303
  245.8 82.6 %last_grads.1 = (f32[3,256,768]{2,1,0:T(8,128)}, bf16[5248,256]{1,0:T(8,128)(2,1)}, bf16[2,1792,128]{2,1,0:T(8,128)(2,1)}, f32[16,128]{1,0:T(8,128)}) custom-call(bf16[2624,256]{1,0:T(8,128)(2,1)} %get-tuple-element.62.refs_0_, bf16[3,3,2,384,256]{4,3,2,1,0:T(8,128)(2,1)} %get-tuple-element.63.refs_1_, bf16[2,3,768,256]{3,2,1,0:T(8,128)(2,1)} %get-tuple-element.64.refs_2_, ...), custom_call_target="tpu_custom_call" | custom-call | tf_op jit(solution)/shard_map/last_grads/pallas_call | solution.py:618
  328.4 6.9 %unpack.1 = (f32[192,768]{1,0:T(8,128)}, f32[192,2048]{1,0:T(8,128)}, f32[192,2048]{1,0:T(8,128)}, f32[512,768]{1,0:T(8,128)}, f32[192,768]{1,0:T(8,128)}, /*ind...) custom-call(bf16[5248,256]{1,0:T(8,128)(2,1)} %get-tuple-element.71., ...), custom_call_target="tpu_custom_call" | custom-call | tf_op jit(solution)/shard_map/unpack/pallas_call | solution.py:689

commit v10 on v9

--- a/solution.py
+++ b/solution.py
@@ -985,7 +985,7 @@
 
 
 def early_scatter(early):
-    return Scatter(early, (True,) * len(early.lines))
+    return Scatter(early, (True,) * (len(early.lines) - 1) + (False,))
 
 
 def backward_kernel(
@@ -1239,14 +1239,14 @@
 
         @pl.when(u == 0)
         def _():
-            scatter.step_first((0,))
+            scatter.step_first((0, early.lines[-1]))
 
         for line in early.lines:
 
-            @pl.when(u == 2 * line + 2)
+            @pl.when(u == (2 * line + 2 if line < early.lines[-1] else 7))
             def _():
                 scatter.step_second(line)
-                if line + 1 < len(early.lines):
+                if line + 1 < early.lines[-1]:
                     scatter.start_first(line + 1)
 
         return carry

time: 342 us -> 356 us (1.041)
  Pallas kernels: 335 us -> 348 us
    pallas_call x1, Pallas kernels: 102 us -> 116 us  [attention_backward(): pl.pallas_call(functools.partial(backward_kernel, n, early), in_specs=[sm...]
where the time goes in v10:
time: 356 us; the launch traced here: 349 us
  Pallas kernels  348 us (98%)
    pallas_call x1, Pallas kernels, attention_backward(): pl.pallas_call(functools.partial(backward_kernel, n, early), in_specs=[sm...  116 us
    pallas_call x1, Pallas kernels, attention_forward(): pl.pallas_call(functools.partial(forward_kernel, n), in_specs=[smem()] +...  107 us
    pallas_call x1, Pallas kernels, last_grads(): pl.pallas_call(functools.partial(last_kernel, early, late), in_specs=[any...  82.6 us
    pallas_call x1, Pallas kernels, middle(): pl.pallas_call(middle_kernel, in_specs=[anywhere()] * 3 + [whole()] + [an...  36.4 us

profile of v10, /device:TPU:0, one launch (start us, length us, event | category | flops | bytes accessed | tf_op | source)
XLA Modules:
  0.0 349.5 jit_solution(14164317345412839580)
XLA Ops:
  0.6 106.6 %attention_forward.1 = (bf16[2,3,768,256]{3,2,1,0:T(8,128)(2,1)}, bf16[9,4,192,256]{3,2,1,0:T(8,128)(2,1)}, bf16[1,9,4,128,256]{4,3,2,1,0:T(8,128)(2,1)}, bf16[3...) custom-call(s32[3]{0:T(128)} %len_ref.3, ...), custom_call_target="tpu_custom_call" | custom-call | flops 44999999488 | bytes 25165824 | tf_op jit(solution)/shard_map/attention_forward/pallas_call | solution.py:943
  107.3 36.4 %middle.1 = (f32[768,768]{1,0:T(8,128)}, f32[768,768]{1,0:T(8,128)}, bf16[3,768,256]{2,1,0:T(8,128)(2,1)}, f32[1,768]{1,0:T(1,128)}, bf16[768,768]{1,0:T(8,128)(...) custom-call(f32[768,768]{1,0:T(8,128)} %bitcast.7, ...), custom_call_target="tpu_custom_call" | custom-call | flops 24999999488 | bytes 33554432 | tf_op jit(solution)/shard_map/middle/pallas_call | solution.py:1449
  143.6 115.8 %attention_backward.1 = (bf16[3,3,2,384,256]{4,3,2,1,0:T(8,128)(2,1)}, f32[3,4,256,256]{3,2,1,0:T(8,128)}, f32[3,8,256]{2,1,0:T(8,128)}, bf16[2624,256]{1,0:T(8,...) custom-call(s32[3]{0:T(128)} %len_ref.3, f32[3,2,1,256]{3,2,1,0:T(1,128)} %get-tuple-element.51.far_ref, ...), custom_call_target="tpu_custom_call" | custom-call | flops 109999996928 | bytes 25165824 | tf_op jit(solution)/shard_map/attention_backward/pallas_call | solution.py:1303
  259.5 82.6 %last_grads.1 = (f32[3,256,768]{2,1,0:T(8,128)}, bf16[5248,256]{1,0:T(8,128)(2,1)}, bf16[2,1792,128]{2,1,0:T(8,128)(2,1)}, f32[16,128]{1,0:T(8,128)}) custom-call(bf16[2624,256]{1,0:T(8,128)(2,1)} %get-tuple-element.62.refs_0_, bf16[3,3,2,384,256]{4,3,2,1,0:T(8,128)(2,1)} %get-tuple-element.63.refs_1_, bf16[2,3,768,256]{3,2,1,0:T(8,128)(2,1)} %get-tuple-element.64.refs_2_, ...), custom_call_target="tpu_custom_call" | custom-call | tf_op jit(solution)/shard_map/last_grads/pallas_call | solution.py:618
  342.1 6.9 %unpack.1 = (f32[192,768]{1,0:T(8,128)}, f32[192,2048]{1,0:T(8,128)}, f32[192,2048]{1,0:T(8,128)}, f32[512,768]{1,0:T(8,128)}, f32[192,768]{1,0:T(8,128)}, /*ind...) custom-call(bf16[5248,256]{1,0:T(8,128)(2,1)} %get-tuple-element.71., ...), custom_call_target="tpu_custom_call" | custom-call | tf_op jit(solution)/shard_map/unpack/pallas_call | solution.py:689
